TPU v7x, 256 devices: a whole 4x4x8 slice. The times are simulated.
256 devices in a mesh: dp: 32 (over z, x_lo, core), seg: 8 (over x_hi, y).
Axes of the slice: x: 4 (x_hi: 2, x_lo: 2; x = x_hi * 2 + x_lo), y: 4, z: 8, core: 2. Of those that a mesh axis runs over, the one named last changes fastest.
Arguments:
- tokens: bfloat16 [32, 1024, 768], P('dp', 'seg'), may hold values from -6 to 6
- coords: int32 [32, 1024, 2], P('dp', 'seg'), may hold values from 0 to 255
- lengths: int32 [32], P('dp'), may hold values from 256 to 1024, as said below
- w_qkv: bfloat16 [768, 2304], replicated, may hold values from -16 to 16
- w_out: bfloat16 [768, 768], replicated, may hold values from -1.5 to 1.5
- cotangent: bfloat16 [32, 1024, 768], P('dp', 'seg'), may hold values from -6 to 6
Outputs:
- layer_out: bfloat16 [32, 1024, 768], P('dp', 'seg')
- token_grad: bfloat16 [32, 1024, 768], P('dp', 'seg')
- grad_w_qkv: float32 [768, 2304], P('seg', 'dp')
- grad_w_out: float32 [768, 768], P('seg', 'dp')
Inputs may be any that keep to these rules, and one draw needn't show every extreme that they name: `lengths`: each slide's length lies in the range; in every draw one slide has exactly 1024 tiles and another exactly 256.
All inputs are finite; a program needn't handle non-finite values.
Results may differ from a plain program's by a relative error of at most 0.034.
Values may be sent and summed in bfloat16 or wider, within the bound.
No kernel may reach another device: no remote copies, remote signals or barrier semaphores. Data moves between devices by JAX's collectives and lax.ppermute only.
A program may use at most 64 MiB of HBM per device.

v0:
```python
import jax
import jax.numpy as jnp
from jax import lax
from jax.sharding import PartitionSpec as P

HEADS = 16
RATE = 4


EPSILON = 1e-05
NEG_FILL = -1e30


def position_code(coords, width):
    quarter = width // 4
    freqs = jnp.exp(-jnp.log(10000.0) * jnp.arange(quarter, dtype=jnp.float32) / quarter)
    across = coords[:, 0:1].astype(jnp.float32) * freqs[None, :]
    upward = coords[:, 1:2].astype(jnp.float32) * freqs[None, :]
    return jnp.concatenate(
        [jnp.sin(across), jnp.cos(across), jnp.sin(upward), jnp.cos(upward)], axis=1
    )


def layer_norm(embedded):
    centred = embedded - jnp.mean(embedded, axis=-1, keepdims=True)
    spread = jnp.mean(centred * centred, axis=-1, keepdims=True)
    return centred * lax.rsqrt(spread + EPSILON)


def project_in(tokens, coords, w_qkv):
    embedded = tokens.astype(jnp.float32) + position_code(coords, tokens.shape[-1])
    normed = layer_norm(embedded).astype(jnp.bfloat16)
    packed = jnp.dot(normed, w_qkv, preferred_element_type=jnp.float32).astype(jnp.bfloat16)
    return (embedded, normed, packed)


def project_in_back(embedded, normed, w_qkv, packed_grad):
    grad_weight = lax.dot_general(
        normed, packed_grad, (((0,), (0,)), ((), ())), preferred_element_type=jnp.float32
    )
    normed_grad = lax.dot_general(
        packed_grad, w_qkv, (((1,), (1,)), ((), ())), preferred_element_type=jnp.float32
    )
    _, norm_pull = jax.vjp(layer_norm, embedded)
    token_grad = norm_pull(normed_grad)[0].astype(jnp.bfloat16)
    return (token_grad, grad_weight)


def split_heads(packed, head_count):
    row_count = packed.shape[0]
    width = packed.shape[1] // 3
    shaped = packed.reshape(row_count, 3, head_count, width // head_count)
    return (shaped[:, 0], shaped[:, 1], shaped[:, 2])


def sample_mask(head_count, dilation):
    return (
        jnp.arange(dilation, dtype=jnp.int32)[:, None]
        == (jnp.arange(head_count, dtype=jnp.int32) % dilation)[None, :]
    )


def pick_samples(rows_in, dilation):
    grouped = rows_in.reshape((rows_in.shape[0] // dilation, dilation) + rows_in.shape[1:])
    chosen = sample_mask(rows_in.shape[1], dilation).astype(rows_in.dtype)
    chosen = chosen.reshape(chosen.shape + (1,) * (rows_in.ndim - 2))
    return jnp.sum(grouped * chosen[None], axis=1)


def place_samples(samples, dilation):
    chosen = sample_mask(samples.shape[1], dilation).astype(samples.dtype)
    chosen = chosen.reshape(chosen.shape + (1,) * (samples.ndim - 2))
    spread = samples[:, None] * chosen[None]
    return spread.reshape((samples.shape[0] * dilation,) + samples.shape[1:])


def masked_softmax(scores, allowed):
    scores = jnp.where(allowed, scores, NEG_FILL)
    row_max = lax.stop_gradient(jnp.max(scores, axis=-1, keepdims=True))
    shifted = jnp.exp(scores - row_max)
    row_sum = jnp.sum(shifted, axis=-1, keepdims=True)
    weights = lax.optimization_barrier((shifted / row_sum).astype(jnp.bfloat16)).astype(jnp.float32)
    return (weights, (row_max + jnp.log(row_sum))[..., 0])


def dense_branch(queries, key_rows, value_rows, positions, length):
    score_scale = queries.shape[-1] ** (-0.5)
    scores = (
        jnp.einsum("bqhe,bkhe->bhqk", queries.astype(jnp.float32), key_rows.astype(jnp.float32))
        * score_scale
    )
    allowed = jnp.logical_or(
        positions[:, None, None, :] < length,
        positions[:, None, :, None] == positions[:, None, None, :],
    )
    weights, log_total = masked_softmax(scores, allowed)
    output = jnp.einsum("bhqk,bkhe->bqhe", weights, value_rows.astype(jnp.float32))
    return (output, jnp.transpose(log_total, (0, 2, 1)))


def sparse_branch(queries, key_rows, value_rows, query_index, key_index, dilation, length):
    score_scale = queries.shape[-1] ** (-0.5)
    offsets = jnp.arange(queries.shape[1], dtype=jnp.int32) % dilation
    scores = jnp.einsum("qhe,khe->hqk", queries.astype(jnp.float32), key_rows) * score_scale
    key_place = key_index[None, :] * dilation + offsets[:, None]
    allowed = jnp.logical_or(
        key_place[:, None, :] < length, query_index[None, :, None] == key_index[None, None, :]
    )
    weights, log_total = masked_softmax(scores, allowed)
    output = jnp.einsum("hqk,khe->qhe", weights, value_rows)
    return (output, jnp.transpose(log_total))


def combine_branches(dense_out, dense_lse, sparse_out, sparse_lse, dilation):
    sampled = jnp.tile(sample_mask(dense_lse.shape[1], dilation), (sparse_lse.shape[0], 1))
    spread_out = place_samples(sparse_out, dilation)
    spread_lse = place_samples(sparse_lse, dilation)
    larger = lax.stop_gradient(jnp.where(sampled, jnp.maximum(dense_lse, spread_lse), dense_lse))
    dense_weight = jnp.exp(dense_lse - larger)
    sparse_weight = jnp.where(sampled, jnp.exp(jnp.where(sampled, spread_lse - larger, 0.0)), 0.0)
    blended = (dense_weight[..., None] * dense_out + sparse_weight[..., None] * spread_out) / (
        dense_weight + sparse_weight
    )[..., None]
    return blended.reshape(dense_out.shape[0], -1).astype(jnp.bfloat16)


def assemble_grads(dense_grads, sparse_grads, dilation):
    query_grad = dense_grads[0] + place_samples(sparse_grads[0], dilation)
    key_grad = dense_grads[1] + place_samples(sparse_grads[1], dilation)
    value_grad = dense_grads[2] + place_samples(sparse_grads[2], dilation)
    row_count = query_grad.shape[0]
    return jnp.concatenate(
        [
            query_grad.reshape(row_count, -1),
            key_grad.reshape(row_count, -1),
            value_grad.reshape(row_count, -1),
        ],
        axis=1,
    )


def project_out(blended, w_out, live):
    return jnp.where(live, jnp.dot(blended, w_out, preferred_element_type=jnp.float32), 0.0).astype(
        jnp.bfloat16
    )


def per_device(tokens, coords, lengths, w_qkv, w_out, cotangent):
    row_count = tokens.shape[1]
    seg_index = lax.axis_index("seg")
    length = lengths[0]
    positions = seg_index * row_count + jnp.arange(row_count, dtype=jnp.int32)
    embedded, normed, packed = project_in(tokens[0], coords[0], w_qkv)
    q_rows, k_rows, v_rows = split_heads(packed, HEADS)

    def dense_part(q_in, k_in, v_in):
        block_out, block_lse = dense_branch(
            q_in[None], k_in[None], v_in[None], positions[None], length
        )
        return (block_out[0], block_lse[0])

    sample_count = row_count // RATE
    query_index = seg_index * sample_count + jnp.arange(sample_count, dtype=jnp.int32)
    key_index = jnp.arange(sample_count * lax.axis_size("seg"), dtype=jnp.int32)

    def sparse_part(q_in, k_in, v_in):
        return sparse_branch(q_in, k_in, v_in, query_index, key_index, RATE, length)

    def combine_part(first_out, first_lse, second_out, second_lse):
        return combine_branches(first_out, first_lse, second_out, second_lse, RATE)

    own_keys = pick_samples(k_rows, RATE)
    own_values = pick_samples(v_rows, RATE)
    sampled_queries = pick_samples(q_rows, RATE)
    gathered_keys, gathered_values = (
        lax.all_gather(own_keys, "seg", axis=0, tiled=True),
        lax.all_gather(own_values, "seg", axis=0, tiled=True),
    )
    (sparse_out, sparse_lse), sparse_pull = jax.vjp(
        sparse_part,
        sampled_queries,
        gathered_keys.astype(jnp.float32),
        gathered_values.astype(jnp.float32),
    )
    (dense_out, dense_lse), dense_pull = jax.vjp(dense_part, q_rows, k_rows, v_rows)
    blended, combine_pull = jax.vjp(combine_part, dense_out, dense_lse, sparse_out, sparse_lse)
    live = (positions < length)[:, None]
    layer_out = project_out(blended, w_out, live)
    out_grad = jnp.where(live, cotangent[0], jnp.zeros_like(cotangent[0]))
    grad_out = lax.dot_general(
        blended, out_grad, (((0,), (0,)), ((), ())), preferred_element_type=jnp.float32
    )
    blended_grad = lax.dot_general(
        out_grad, w_out, (((1,), (1,)), ((), ())), preferred_element_type=jnp.float32
    ).astype(jnp.bfloat16)
    grad_dense_out, grad_dense_lse, grad_sparse_out, grad_sparse_lse = combine_pull(blended_grad)
    query_sparse, key_terms, value_terms = sparse_pull((grad_sparse_out, grad_sparse_lse))
    dense_grads = dense_pull((grad_dense_out, grad_dense_lse))
    key_sparse, value_sparse = (
        lax.psum_scatter(
            key_terms.astype(jnp.bfloat16), "seg", scatter_dimension=0, tiled=True
        ).astype(jnp.float32),
        lax.psum_scatter(
            value_terms.astype(jnp.bfloat16), "seg", scatter_dimension=0, tiled=True
        ).astype(jnp.float32),
    )
    sparse_grads = (
        query_sparse,
        key_sparse.astype(jnp.bfloat16),
        value_sparse.astype(jnp.bfloat16),
    )
    packed_grad = assemble_grads(dense_grads, sparse_grads, RATE)
    token_grad, grad_in = project_in_back(embedded, normed, w_qkv, packed_grad)
    partial_in, partial_out = (
        lax.psum_scatter(
            grad_in.astype(jnp.bfloat16), "seg", scatter_dimension=0, tiled=True
        ).astype(jnp.float32),
        lax.psum_scatter(
            grad_out.astype(jnp.bfloat16), "seg", scatter_dimension=0, tiled=True
        ).astype(jnp.float32),
    )
    final_in, final_out = (
        lax.psum_scatter(
            partial_in.astype(jnp.bfloat16), "dp", scatter_dimension=1, tiled=True
        ).astype(jnp.float32),
        lax.psum_scatter(
            partial_out.astype(jnp.bfloat16), "dp", scatter_dimension=1, tiled=True
        ).astype(jnp.float32),
    )
    return (layer_out[None], token_grad[None], final_in, final_out)


def solution(mesh):
    placed = (P("dp", "seg", None), P("dp", "seg", None), P("dp"), P(), P(), P("dp", "seg", None))
    return jax.shard_map(
        per_device,
        mesh=mesh,
        in_specs=placed,
        out_specs=(P("dp", "seg", None), P("dp", "seg", None), P("seg", "dp"), P("seg", "dp")),
        check_vma=False,
    )
```

profile of v0, /device:TPU:6, one launch (start us, length us, event | category | flops | bytes accessed | tf_op | source)
XLA Modules:
  0.0 687.7 jit_solution(10199884737596046465)
XLA Ops:
  12.6 1.5 convolution_convert_fusion.1
  14.2 2.1 copy.159
  17.0 1.9 fusion.91
  20.4 2.1 copy.173
  22.6 2.1 copy.161
  24.7 2.1 copy.160
  26.8 2.7 multiply_reduce_fusion.1
  29.5 38.4 %all_gather.6 = bf16[256,16,48]{2,0,1:T(8,128)(2,1)} all-gather(bf16[32,16,48]{2,0,1:T(8,128)(2,1)S(1)} %copy.162), channel_id=1, replica_groups=mesh['dp'=32,'seg'=8] {'seg'}, dimensions={0}, use_global_device_ids=true | all-gather | bytes 442368 | tf_op jit(solution)/shard_map/all_gather | solution.py:176
  68.1 1.8 fusion.93
  73.4 38.3 %all_gather.7 = bf16[256,16,48]{2,0,1:T(8,128)(2,1)} all-gather(bf16[32,16,48]{2,0,1:T(8,128)(2,1)S(1)} %copy.174), channel_id=1, replica_groups=mesh['dp'=32,'seg'=8] {'seg'}, dimensions={0}, use_global_device_ids=true | all-gather | bytes 442368 | tf_op jit(solution)/shard_map/all_gather | solution.py:177
  113.1 2.5 reshape.698
  115.6 1.4 fusion.16
  117.6 1.4 copy.187
  120.0 1.8 multiply_reduce_fusion
  125.2 2.9 copy.202
  128.3 2.3 convolution_bitcast_fusion
  130.6 1.9 copy.180
  132.5 2.3 fusion.25
  138.1 1.5 copy.165
  140.9 1.5 copy.166
  144.6 2.4 copy.183
  147.7 3.1 multiply_reduce_fusion.5
  152.0 1.4 copy.189
  153.4 2.2 multiply_reduce_fusion.8
  158.3 2.5 fusion.3
  160.8 2.9 copy.197
  163.7 2.6 convolution_convert_fusion.2
  166.4 2.3 fusion.2
  170.1 1.5 copy.184
  171.6 1.8 fusion.15
  174.2 2.1 convolution_convert_fusion.8
  176.3 1.7 copy.194
  178.0 2.0 fusion.8
  180.9 2.2 mul.523
  184.4 1.4 copy.192
  187.2 1.7 copy.193
  189.0 2.3 convolution_convert_fusion.10
  191.3 1.7 copy.204
  193.0 2.7 convolution_convert_fusion.7
  195.7 1.7 copy.199
  197.5 9.7 %reduce-scatter.9.cloned.1.call-done = bf16[32,16,48]{2,1,0:T(8,128)(2,1)} async-done(((bf16[256,16,48]{2,1,0:T(8,128)(2,1)}), bf16[32,16,48]{2,1,0:T(8,128)(2,1)}) %reduce-scatter.9.cloned.1.call-update) | async-done | bytes 49168 | tf_op jit(solution)/shard_map/reduce_scatter | solution.py:203
  207.1 1.8 mul.532
  208.9 2.2 mul.533
  211.1 76.3 %reduce-scatter.7.cloned.1.call-done = bf16[32,16,48]{2,1,0:T(8,128)(2,1)} async-done(((bf16[256,16,48]{2,1,0:T(8,128)(2,1)}), bf16[32,16,48]{2,1,0:T(8,128)(2,1)}) %reduce-scatter.7.cloned.1.call-update) | async-done | bytes 49168 | tf_op jit(solution)/shard_map/reduce_scatter | solution.py:200
  287.4 1.8 mul.529
  289.2 2.2 mul.530
  291.4 1.5 multiply_add_fusion.2
  293.7 3.0 convolution_convert_fusion
  296.8 2.4 mul.484
  300.0 1.9 copy.179
  301.9 1.5 mul.480
  303.4 1.9 copy.178
  306.1 1.9 copy.177
  308.8 1.9 copy.169
  310.7 1.9 copy.170
  314.5 3.2 fusion.7
  317.8 2.0 multiply_reduce_fusion.4
  319.9 48.4 %reduce-scatter.13.cloned.1.call-done = bf16[96,768]{1,0:T(8,128)(2,1)} async-done(((bf16[768,768]{1,0:T(8,128)(2,1)}), bf16[96,768]{1,0:T(8,128)(2,1)}) %reduce-scatter.13.cloned.1.call-update) | async-done | bytes 147472 | tf_op jit(solution)/shard_map/reduce_scatter | solution.py:218
  368.3 88.9 %reduce-scatter.11.cloned.1.call-done = bf16[96,2304]{1,0:T(8,128)(2,1)} async-done(((bf16[768,2304]{1,0:T(8,128)(2,1)}), bf16[96,2304]{1,0:T(8,128)(2,1)}) %reduce-scatter.11.cloned.1.call-update) | async-done | bytes 442384 | tf_op jit(solution)/shard_map/reduce_scatter | solution.py:215
  459.3 215.9 %all-reduce.5.cloned.1.call-done = (bf16[96,2304]{1,0:T(8,128)(2,1)}, bf16[96,768]{1,0:T(8,128)(2,1)}) async-done(((bf16[96,2304]{1,0:T(8,128)(2,1)}, bf16[96,768]{1,0:T(8,128)(2,1)}), (bf16[96,2304]{1,0:T(8,128)(2,1)}, bf16[96,768]{1,0:T(8,128)(2,1)})) %all-reduce.5.cloned.1.call-update) | async-done | bytes 589840
  675.2 1.5 dynamic-slice_convert_fusion.1
  676.7 1.5 copy.205
  678.2 1.5 dynamic-slice_convert_fusion
  679.7 1.5 copy.206
  (175 shorter events, 40.2 us)
Async XLA Ops:
  7.2 5.5 copy-start
  7.2 199.9 %reduce-scatter.9.cloned.1.call-start = ((), (), s32[]{:S(2)}) async-start(), calls=%async_computation.5 | async-start | bytes 1179648 | tf_op jit(solution)/shard_map/reduce_scatter | solution.py:203
  8.4 18.4 %copy-start.41 = (bf16[4,16]{1,0:T(4,128)(2,1)}, bf16[4,16]{1,0:T(4,128)(2,1)S(1)}, u32[]{:S(2)}) copy-start(bf16[4,16]{1,0:T(4,128)(2,1)S(1)} %get-tuple-element.64) | copy-start | bytes 388
  11.3 0.8 copy-start.1
  11.3 0.8 copy-start.38
  11.5 0.5 copy-start.53
  12.1 0.5 copy-start.42
  16.3 2.8 copy-start.9
  17.0 3.4 copy-start.49
  19.1 1.4 copy-start.36
  29.5 38.5 %copy-start.52 = (s32[256]{0:T(256)S(1)}, s32[256]{0:T(256)}, u32[]{:S(2)}) copy-start(s32[256]{0:T(256)} %iota_multiply_fusion) | copy-start | bytes 3076
  68.0 3.6 copy-start.25
  68.1 3.5 copy-start.35
  69.9 0.8 copy-start.6
  69.9 1.1 copy-start.20
  71.0 0.6 copy-start.22
  72.3 39.4 %copy-start.8 = (bf16[768,768]{1,0:T(8,128)(2,1)S(1)}, bf16[768,768]{1,0:T(8,128)(2,1)}, u32[]{:S(2)}) copy-start(bf16[768,768]{1,0:T(8,128)(2,1)} %param.10) | copy-start | bytes 3538948
  72.3 39.4 %copy-start.12 = (bf16[1,128,768]{2,1,0:T(8,128)(2,1)S(1)}, bf16[1,128,768]{2,1,0:T(8,128)(2,1)}, u32[]{:S(2)}) copy-start(bf16[1,128,768]{2,1,0:T(8,128)(2,1)} %param.11) | copy-start | bytes 589828
  72.3 39.4 %copy-start.50 = (pred[128]{0:T(512)(128)(4,1)S(1)}, pred[128]{0:T(512)(128)(4,1)}, u32[]{:S(2)}) copy-start(pred[128]{0:T(512)(128)(4,1)} %copy-done.49) | copy-start | bytes 388
  119.0 2.9 copy-start.4
  120.0 2.4 copy-start.7
  120.0 2.4 copy-start.21
  120.0 2.4 copy-start.23
  120.0 2.4 copy-start.26
  122.3 1.0 copy-start.11
  123.4 0.7 copy-start.10
  128.1 159.3 %reduce-scatter.7.cloned.1.call-start = ((), (), s32[]{:S(2)}) async-start(), calls=%async_computation.4 | async-start | bytes 1179648 | tf_op jit(solution)/shard_map/reduce_scatter | solution.py:200
  132.5 2.3 copy-start.45
  147.7 3.1 copy-start.27
  147.7 3.1 copy-start.29
  147.7 3.1 copy-start.30
  150.8 0.6 copy-start.32
  157.7 0.6 copy-start.46
  163.7 204.6 %reduce-scatter.13.cloned.1.call-start = ((), (), s32[]{:S(2)}) async-start(), calls=%async_computation.7 | async-start | bytes 1327104 | tf_op jit(solution)/shard_map/reduce_scatter | solution.py:218
  166.4 290.8 %reduce-scatter.11.cloned.1.call-start = ((), (), s32[]{:S(2)}) async-start(), calls=%async_computation.6 | async-start | bytes 3981312 | tf_op jit(solution)/shard_map/reduce_scatter | solution.py:215
  171.6 1.8 copy-start.33
  171.6 1.8 copy-start.34
  171.6 1.8 copy-start.47
  171.6 2.6 copy-start.5
  171.6 2.6 copy-start.19
  171.6 2.6 copy-start.37
  174.2 2.1 copy-start.48
  289.1 4.6 copy-start.39
  289.2 4.6 copy-start.43
  291.4 2.3 copy-start.2
  292.9 0.7 copy-start.13
  292.9 0.7 copy-start.15
  292.9 0.8 copy-start.17
  296.7 2.5 copy-start.31
  296.7 378.5 %all-reduce.5.cloned.1.call-start = ((), (), s32[]{:S(2)}) async-start(), calls=%async_computation.8 | async-start | bytes 1179648
  299.2 6.1 copy-start.24
  301.9 6.1 copy-start.28
  308.0 4.6 copy-start.55
  308.0 6.5 copy-start.51
  314.5 3.3 copy-start.3
  314.5 3.3 copy-start.14
  314.5 3.3 copy-start.16
  314.5 3.2 copy-start.18
  314.5 3.2 copy-start.40
  317.8 2.1 copy-start.54
  317.8 139.4 %copy-start.44 = (f32[128]{0:T(128)S(1)}, f32[128]{0:T(128)}, u32[]{:S(2)}) copy-start(f32[128]{0:T(128)} %copy-done.42) | copy-start | bytes 1540
Sparse Core Ops, SparseCore 0:
  128.2 78.8 reduce-scatter.8
  211.5 75.8 reduce-scatter.6
  291.3 76.9 reduce-scatter.12
  372.3 84.7 reduce-scatter.10
  459.7 215.4 all-reduce.4
where the time goes:
time: 691 us; the launch traced here: 688 us
  waiting for transfers between devices  439 us (64%)
  local copies, waits for them, and re-layouts  87.9 us (13%)
  blocking collectives  76.8 us (11%)
  matrix products  37.6 us (5%)
  other arithmetic  29.4 us (4%)
  between operations  16.4 us (2%)
    unnamed x6, waiting for transfers between devices  216 us
    reduce_scatter x1, waiting for transfers between devices, per_device(): lax.psum_scatter(grad_in.astype(jnp.bfloat16), 'seg', scatter_dimension=0...  88.9 us
    reduce_scatter x1, waiting for transfers between devices, per_device(): lax.psum_scatter(key_terms.astype(jnp.bfloat16), 'seg', scatter_dimension...  76.3 us
    reduce_scatter x1, waiting for transfers between devices, per_device(): lax.psum_scatter(grad_out.astype(jnp.bfloat16), 'seg', scatter_dimension=...  48.4 us
    all_gather x1, blocking collectives, per_device(): lax.all_gather(own_keys, 'seg', axis=0, tiled=True)  38.4 us
    all_gather x1, blocking collectives, per_device(): lax.all_gather(own_values, 'seg', axis=0, tiled=True)  38.3 us
    mul x16, local copies, waits for them, and re-layouts, place_samples(): spread = samples[:, None] * chosen[None]  26.8 us
  transfers between devices with their start and end apart: 5, of which 5 were waited for; matrix products, arithmetic and copies ran while one was open for 15% of the time, Pallas kernels for 0%

commit v1 on v0

v1 whole, which is shorter than its diff:
```python
import functools

import jax
import jax.numpy as jnp
from jax import lax
from jax.experimental import pallas as pl
from jax.experimental.pallas import tpu as pltpu
from jax.sharding import Mesh
from jax.sharding import PartitionSpec as P

HEADS = 16
RATE = 4
HEAD = 48
GROUP = 8
WIDE = GROUP * HEAD
ROWS = 128
SLAB = ROWS // RATE
D = 768
N_SEG = 8
BLOCK = 96
EPSILON = 1e-05
NEG_FILL = -1e30
SCALE = HEAD ** (-0.5)
BF = jnp.bfloat16
F32 = jnp.float32
VMEM = pl.BlockSpec(memory_space=pltpu.VMEM)
SMEM = pl.BlockSpec(memory_space=pltpu.SMEM)
LIMIT = 40 * 1024 * 1024


def iota(shape, dim):
    return lax.broadcasted_iota(jnp.int32, shape, dim)


def mm(a, b):
    return lax.dot_general(a, b, (((1,), (0,)), ((), ())), preferred_element_type=F32)


def mm_nt(a, b):
    return lax.dot_general(a, b, (((1,), (1,)), ((), ())), preferred_element_type=F32)


def mm_tn(a, b):
    return lax.dot_general(a, b, (((0,), (0,)), ((), ())), preferred_element_type=F32)


def regroup():
    row, col = iota((ROWS, ROWS), 0), iota((ROWS, ROWS), 1)
    return (col == RATE * (row % SLAB) + row // SLAB).astype(BF)


def place_of(row):
    return RATE * (row % SLAB) + row // SLAB


def sin_cos_code(c0, c1):
    quarter = D // 4
    col = iota((1, D), 1)
    block = col // quarter
    freqs = jnp.exp((-jnp.log(F32(10000.0))) * (col - block * quarter).astype(F32) / quarter)
    angle = jnp.where(block < 2, c0, c1) * freqs
    turns = jnp.floor(angle * F32(0.6366197723675814) + F32(0.5))
    rest = angle - turns * F32(1.5703125)
    rest = rest - turns * F32(4.837512969970703e-4)
    rest = rest - turns * F32(7.549789948768648e-8)
    sq = rest * rest
    sine = rest + rest * sq * (
        F32(-1.6666654611e-1) + sq * (F32(8.3321608736e-3) + sq * F32(-1.9515295891e-4))
    )
    cosine = (
        F32(1.0)
        - F32(0.5) * sq
        + sq * sq * (F32(4.166664568298827e-2) + sq * (F32(-1.388731625493765e-3) + sq * F32(2.443315711809948e-5)))
    )
    quadrant = turns.astype(jnp.int32) + (block & 1)
    value = jnp.where((quadrant & 1) == 1, cosine, sine)
    return jnp.where((quadrant & 2) == 2, -value, value)


def head_mask(rows_per_head):
    shape = (GROUP * rows_per_head, WIDE)
    return iota(shape, 0) // rows_per_head == iota(shape, 1) // HEAD


def split3(x):
    hi = x.astype(BF)
    rest = x - hi.astype(F32)
    mid = rest.astype(BF)
    lo = (rest - mid.astype(F32)).astype(BF)
    return hi, mid, lo


def put_scalars(base, columns):
    lane = iota(base.shape, 1)
    for n, column in enumerate(columns):
        base = jnp.where(lane == BLOCK + n, column.astype(F32), base)
    return base


def stack_slabs(array, group):
    part = array[:, group * WIDE : (group + 1) * WIDE]
    return jnp.concatenate(
        [part[SLAB * (h % RATE) : SLAB * (h % RATE) + SLAB] for h in range(GROUP)], axis=0
    )


def unstack_slabs(stack):
    return jnp.concatenate(
        [
            stack[SLAB * o : SLAB * o + SLAB] + stack[SLAB * (o + RATE) : SLAB * (o + RATE) + SLAB]
            for o in range(RATE)
        ],
        axis=0,
    )


def seg_index():
    return lax.axis_index("xh") * 4 + lax.axis_index("y")


def first_kernel(
    length_ref, tok_ref, coord_ref, cot_ref, w_qkv_ref, w_out_ref,
    message_ref, packed_ref, g_ref, xhat_ref, rstd_ref, normed_ref, grad_ref, blocks_ref,
):
    length = length_ref[0]
    base = seg_index() * ROWS
    order = regroup()
    tokens = mm(order, tok_ref[0])
    coords = mm(order, coord_ref[0].astype(F32).astype(BF))
    embedded = tokens + sin_cos_code(coords[:, 0:1], coords[:, 1:2])
    centred = embedded - jnp.mean(embedded, axis=-1, keepdims=True)
    rstd = lax.rsqrt(jnp.mean(centred * centred, axis=-1, keepdims=True) + EPSILON)
    xhat = centred * rstd
    normed = xhat.astype(BF)
    xhat_ref[...] = xhat
    rstd_ref[...] = jnp.broadcast_to(rstd, rstd_ref.shape)
    normed_ref[...] = normed
    packed = mm(normed, w_qkv_ref[...]).astype(BF)
    packed_ref[...] = packed
    live = (base + place_of(iota((ROWS, 1), 0))) < length
    out_grad = jnp.where(live, mm(order, cot_ref[0]), 0.0).astype(BF)
    grad_ref[...] = out_grad
    g = mm_nt(out_grad, w_out_ref[...]).astype(BF)
    g_ref[...] = g

    mask = head_mask(SLAB)
    key_col = place_of(iota((1, ROWS), 1))
    row = iota((GROUP * SLAB, 1), 0)
    query_col = RATE * (row % SLAB) + (row // SLAB) % RATE
    allowed = jnp.logical_or(base + key_col < length, key_col == query_col)
    scalars = []
    for group in range(2):
        q = jnp.where(mask, stack_slabs(packed[:, :D], group).astype(F32), 0.0).astype(BF)
        gs = stack_slabs(g, group).astype(F32)
        k = packed[:, D + group * WIDE : D + (group + 1) * WIDE]
        v = packed[:, 2 * D + group * WIDE : 2 * D + (group + 1) * WIDE]
        s = jnp.where(allowed, mm_nt(q, k) * SCALE, NEG_FILL)
        top = jnp.max(s, axis=-1, keepdims=True)
        e = jnp.exp(s - top)
        total = jnp.sum(e, axis=-1, keepdims=True)
        lse = top + jnp.log(total)
        out = mm((e / total).astype(BF), v)
        g_dot = jnp.sum(jnp.where(mask, gs * out, 0.0), axis=-1, keepdims=True)
        scalars.append((lse, g_dot))

    lane = iota((SLAB, BLOCK), 1)
    pad = jnp.zeros((SLAB, 128 - BLOCK), F32)
    for j in range(N_SEG):
        r0 = SLAB * ((2 * j) % RATE)
        columns = [[], []]
        for h in (2 * j, 2 * j + 1):
            at = (h % GROUP) * SLAB
            for which in range(2):
                columns[which] += list(split3(scalars[h // GROUP][which][at : at + SLAB]))
        for a in range(4):
            if a < 3:
                part = packed[r0 : r0 + 2 * SLAB, a * D + BLOCK * j : a * D + BLOCK * (j + 1)]
            else:
                part = g[r0 : r0 + 2 * SLAB, BLOCK * j : BLOCK * (j + 1)]
            part = part.astype(F32)
            part = jnp.where(lane < HEAD, part[:SLAB], part[SLAB:])
            part = jnp.concatenate([part, pad], axis=1)
            if a < 2:
                part = put_scalars(part, columns[a])
            message_ref[j, a] = part.astype(BF)

    core = lax.axis_index("core")
    zero = jnp.zeros((ROWS, 72), F32)
    wide = out_grad.astype(F32)
    for b in range(16):
        z_hi, xl, z_lo = b // 8, (b // 4) % 2, b % 4
        for c in range(2):
            dp = (z_hi * 4 + z_lo) * 4 + xl * 2 + c
            rel = (core + c) % 2
            block = jnp.concatenate([zero, wide[:, 24 * dp : 24 * dp + 24]], axis=1)
            blocks_ref[rel, :, BLOCK * b : BLOCK * (b + 1)] = block.astype(BF)


def dense_kernel(
    length_ref, packed_ref, g_ref, out_ref, back_ref, weight_ref, dweight_ref, sampled_out_ref
):
    length = length_ref[0]
    base = seg_index() * ROWS
    mask = head_mask(ROWS)
    small = head_mask(SLAB)
    row = iota((GROUP * ROWS, 1), 0)
    key_col = place_of(iota((1, ROWS), 1))
    query_col = place_of(row % ROWS)
    allowed = jnp.logical_or(base + key_col < length, key_col == query_col)
    free = (row % ROWS) // SLAB != (row // ROWS) % RATE

    def spread(part):
        return jnp.where(mask, jnp.concatenate([part.astype(F32)] * GROUP, axis=0), 0.0)

    def fold(stack):
        stack = jnp.where(mask, stack, 0.0)
        return sum(stack[ROWS * h : ROWS * (h + 1)] for h in range(GROUP))

    for group in range(2):
        lanes = slice(group * WIDE, (group + 1) * WIDE)
        q = spread(packed_ref[:, group * WIDE : (group + 1) * WIDE]).astype(BF)
        k = packed_ref[:, D + group * WIDE : D + (group + 1) * WIDE]
        v = packed_ref[:, 2 * D + group * WIDE : 2 * D + (group + 1) * WIDE]
        gm = spread(g_ref[:, lanes])
        gb = gm.astype(BF)
        s = jnp.where(allowed, mm_nt(q, k) * SCALE, NEG_FILL)
        e = jnp.exp(s - jnp.max(s, axis=-1, keepdims=True))
        p = e / jnp.sum(e, axis=-1, keepdims=True)
        out = mm(p.astype(BF), v)
        delta = jnp.sum(gm * out, axis=-1, keepdims=True)
        dp = mm_nt(gb, v)
        out_ref[:, lanes] = fold(out)
        free_p = jnp.where(free, p, 0.0)
        ds = (free_p * (dp - delta) * SCALE).astype(BF)
        back_ref[0, :, lanes] = fold(mm(ds, k))
        back_ref[1, :, lanes] = mm_tn(ds, q)
        back_ref[2, :, lanes] = mm_tn(free_p.astype(BF), gb)
        for h in range(GROUP):
            at = ROWS * h + SLAB * (h % RATE)
            to = slice(SLAB * h, SLAB * (h + 1))
            weight_ref[group, to] = p[at : at + SLAB]
            dweight_ref[group, to] = dp[at : at + SLAB]
            sampled_out_ref[group, to] = jnp.where(small[to], out[at : at + SLAB], 0.0)


def dilated_kernel(length_ref, message_ref, reply_ref):
    length = length_ref[0]
    j = seg_index()
    n = N_SEG * SLAB
    stack = []
    for a in range(4):
        stack.append(jnp.concatenate([message_ref[i, a] for i in range(N_SEG)], axis=0))
    q, k, v, g = stack
    lane = iota((n, 128), 1)
    scalar_lane = q.astype(F32), k.astype(F32)
    key = iota((1, n), 1)
    query = iota((n, 1), 0)
    outs = [jnp.zeros((n, 128), F32) for _ in range(4)]
    columns = [[], []]
    for half in range(2):
        mine = jnp.logical_and(lane >= HEAD * half, lane < HEAD * (half + 1))
        offset = (2 * j + half) % RATE

        def scalar(which):
            at = BLOCK + 3 * half
            x = scalar_lane[which]
            return x[:, at : at + 1] + x[:, at + 1 : at + 2] + x[:, at + 2 : at + 3]

        dense_lse, dense_dot = scalar(0), scalar(1)
        qm = jnp.where(mine, q.astype(F32), 0.0).astype(BF)
        gf = jnp.where(mine, g.astype(F32), 0.0)
        gm = gf.astype(BF)
        allowed = jnp.logical_or(RATE * key + offset < length, key == query)
        s = jnp.where(allowed, mm_nt(qm, k) * SCALE, NEG_FILL)
        top = jnp.max(s, axis=-1, keepdims=True)
        e = jnp.exp(s - top)
        total = jnp.sum(e, axis=-1, keepdims=True)
        lse = top + jnp.log(total)
        p = e / total
        out = mm(p.astype(BF), v)
        larger = jnp.maximum(lse, dense_lse)
        dense_part = jnp.exp(dense_lse - larger)
        own_part = jnp.exp(lse - larger)
        both = dense_part + own_part
        dense_part = dense_part / both
        own_part = own_part / both
        delta = dense_part * dense_dot + own_part * jnp.sum(gf * out, axis=-1, keepdims=True)
        p = p * own_part
        ds = (p * (mm_nt(gm, v) - delta) * SCALE).astype(BF)
        outs[0] = outs[0] + jnp.where(mine, mm(ds, k), 0.0)
        outs[1] = outs[1] + mm_tn(ds, qm)
        outs[2] = outs[2] + mm_tn(p.astype(BF), gm)
        outs[3] = outs[3] + jnp.where(mine, out * own_part, 0.0)
        columns[0] += list(split3(dense_part))
        columns[1] += list(split3(delta))
    outs[0] = put_scalars(outs[0], columns[0])
    outs[1] = put_scalars(outs[1], columns[1])
    for a in range(4):
        result = outs[a].astype(BF)
        for i in range(N_SEG):
            reply_ref[i, a] = result[SLAB * i : SLAB * (i + 1)]


def join_kernel(
    reply_ref, packed_ref, g_ref, out_ref, back_ref, weight_ref, dweight_ref, sampled_out_ref,
    blended_ref, packed_grad_ref, blocks_ref,
):
    small = head_mask(SLAB)
    shape = (ROWS, D)
    sampled = (iota(shape, 1) // HEAD) % RATE == iota(shape, 0) // SLAB

    def placed(a):
        row = jnp.concatenate(
            [reply_ref[j, a].astype(F32)[:, :BLOCK] for j in range(N_SEG)], axis=1
        )
        return jnp.where(sampled, jnp.concatenate([row] * RATE, axis=0), 0.0)

    def scalars(a, group):
        columns = []
        for h in range(GROUP * group, GROUP * (group + 1)):
            x = reply_ref[h // 2, a].astype(F32)
            at = BLOCK + 3 * (h % 2)
            columns.append(x[:, at : at + 1] + x[:, at + 1 : at + 2] + x[:, at + 2 : at + 3])
        return jnp.concatenate(columns, axis=0)

    parts = [[], [], [], []]
    for group in range(2):
        lanes = slice(group * WIDE, (group + 1) * WIDE)
        share, delta = scalars(0, group), scalars(1, group)
        q = jnp.where(small, stack_slabs(packed_ref[:, :D], group).astype(F32), 0.0).astype(BF)
        gm = jnp.where(small, stack_slabs(g_ref[...], group).astype(F32), 0.0).astype(BF)
        k = packed_ref[:, D + group * WIDE : D + (group + 1) * WIDE]
        p = weight_ref[group] * share
        ds = (p * (dweight_ref[group] - delta) * SCALE).astype(BF)
        parts[0].append(back_ref[0, :, lanes] + unstack_slabs(jnp.where(small, mm(ds, k), 0.0)))
        parts[1].append(back_ref[1, :, lanes] + mm_tn(ds, q))
        parts[2].append(back_ref[2, :, lanes] + mm_tn(p.astype(BF), gm))
        parts[3].append(unstack_slabs(sampled_out_ref[group] * share))
    whole = [jnp.concatenate(part, axis=1) for part in parts]
    blended_ref[...] = jnp.where(sampled, whole[3] + placed(3), out_ref[...]).astype(BF)
    grads = []
    for a in range(3):
        grad = (whole[a] + placed(a)).astype(BF)
        packed_grad_ref[:, a * D : (a + 1) * D] = grad
        grads.append(grad.astype(F32))
    grads = jnp.concatenate(grads, axis=1)
    core = lax.axis_index("core")
    zero = jnp.zeros((ROWS, 24), F32)
    for b in range(16):
        z_hi, xl, z_lo = b // 8, (b // 4) % 2, b % 4
        for c in range(2):
            dp = (z_hi * 4 + z_lo) * 4 + xl * 2 + c
            rel = (core + c) % 2
            block = jnp.concatenate([grads[:, 72 * dp : 72 * dp + 72], zero], axis=1)
            blocks_ref[rel, :, BLOCK * b : BLOCK * (b + 1)] = block.astype(BF)


def finish_kernel(
    length_ref, blended_ref, packed_grad_ref, xhat_ref, rstd_ref, w_qkv_ref, w_out_ref,
    layer_ref, token_grad_ref,
):
    length = length_ref[0]
    base = seg_index() * ROWS
    order = regroup()
    live = (base + place_of(iota((ROWS, 1), 0))) < length
    layer = jnp.where(live, mm(blended_ref[...], w_out_ref[...]), 0.0).astype(BF)
    layer_ref[0] = mm_tn(order, layer).astype(BF)
    dn = mm_nt(packed_grad_ref[...], w_qkv_ref[...])
    xhat = xhat_ref[...]
    mean = jnp.mean(dn, axis=-1, keepdims=True)
    slope = jnp.mean(dn * xhat, axis=-1, keepdims=True)
    dx = ((dn - mean - xhat * slope) * rstd_ref[:, 0:1]).astype(BF)
    token_grad_ref[0] = mm_tn(order, dx).astype(BF)


def weight_kernel(
    n0_ref, n1_ref, b0_ref, b1_ref, p0_ref, p1_ref, g0_ref, g1_ref, along_y_ref, along_x_ref
):
    xh, xl, y = lax.axis_index("xh"), lax.axis_index("xl"), lax.axis_index("y")
    left = jnp.concatenate([n0_ref[...], n1_ref[...], b0_ref[...], b1_ref[...]], axis=0)
    for part in range(4):
        z_hi, to_xl = part // 2, part % 2
        lanes = slice(part * WIDE, (part + 1) * WIDE)
        right = jnp.concatenate(
            [p0_ref[:, lanes], p1_ref[:, lanes], g0_ref[:, lanes], g1_ref[:, lanes]], axis=0
        )
        total = mm_tn(left, right).astype(BF)
        xl_rel = (to_xl + xl) % 2
        for s in range(N_SEG):
            xh_rel = (s // 4 + xh) % 2
            y_rel = (s % 4 - y + 4) % 4
            chunk = total[BLOCK * s : BLOCK * (s + 1)]
            if z_hi == 0:
                along_y_ref[y_rel, xh_rel, xl_rel] = chunk
            else:
                along_x_ref[xh_rel, xl_rel, y_rel] = chunk


def call(kernel, outs, specs, *args):
    return pl.pallas_call(
        kernel,
        out_shape=[jax.ShapeDtypeStruct(shape, dtype) for shape, dtype in outs],
        in_specs=specs,
        out_specs=[VMEM] * len(outs),
        compiler_params=pltpu.CompilerParams(vmem_limit_bytes=LIMIT),
    )(*args)


def to_core(x):
    return lax.ppermute(x, "core", [(0, 1), (1, 0)])


def along_y(x, k):
    return lax.ppermute(x, "y", [(i, (i + k) % 4) for i in range(4)])


def along_x(x, xh_rel, xl_rel):
    pairs = [(i, i ^ (2 * xl_rel + xh_rel)) for i in range(4)]
    return lax.ppermute(x, ("xl", "xh"), pairs)


def along_z(x, k):
    return lax.ppermute(x, "z", [(i, (i + k) % 8) for i in range(8)])


def add_up(parts):
    return sum(part.astype(F32) for part in parts)


def per_device(tokens, coords, lengths, w_qkv, w_out, cotangent):
    message, packed, g, xhat, rstd, normed, out_grad, grad_blocks = call(
        first_kernel,
        [
            ((N_SEG, 4, SLAB, 128), BF),
            ((ROWS, 3 * D), BF),
            ((ROWS, D), BF),
            ((ROWS, D), F32),
            ((ROWS, 128), F32),
            ((ROWS, D), BF),
            ((ROWS, D), BF),
            ((2, ROWS, 16 * BLOCK), BF),
        ],
        [SMEM] + [VMEM] * 5,
        lengths, tokens, coords, cotangent, w_qkv, w_out,
    )
    message = lax.all_to_all(message, ("xh", "y"), 0, 0, tiled=True)
    other_normed = to_core(normed)
    other_grad = to_core(grad_blocks[1])
    out, back, weight, dweight, sampled_out = call(
        dense_kernel,
        [
            ((ROWS, D), F32),
            ((3, ROWS, D), F32),
            ((2, GROUP * SLAB, ROWS), F32),
            ((2, GROUP * SLAB, ROWS), F32),
            ((2, GROUP * SLAB, WIDE), F32),
        ],
        [SMEM] + [VMEM] * 2,
        lengths, packed, g,
    )
    (reply,) = call(
        dilated_kernel, [((N_SEG, 4, SLAB, 128), BF)], [SMEM, VMEM], lengths, message
    )
    reply = lax.all_to_all(reply, ("xh", "y"), 0, 0, tiled=True)
    blended, packed_grad, blocks = call(
        join_kernel,
        [((ROWS, D), BF), ((ROWS, 3 * D), BF), ((2, ROWS, 16 * BLOCK), BF)],
        [VMEM] * 8,
        reply, packed, g, out, back, weight, dweight, sampled_out,
    )
    other_blended = to_core(blended)
    other_blocks = to_core(blocks[1])
    first, second = call(
        weight_kernel,
        [((4, 2, 2, BLOCK, WIDE), BF), ((2, 2, 4, BLOCK, WIDE), BF)],
        [VMEM] * 8,
        normed, other_normed, blended, other_blended,
        blocks[0], other_blocks, grad_blocks[0], other_grad,
    )
    layer_out, token_grad = call(
        finish_kernel,
        [((1, ROWS, D), BF), ((1, ROWS, D), BF)],
        [SMEM] + [VMEM] * 6,
        lengths, blended, packed_grad, xhat, rstd, w_qkv, w_out,
    )
    near = [(0, 1), (1, 0), (1, 1)]
    first = add_up([first[0]] + [along_y(first[k], k) for k in (1, 3, 2)]).astype(BF)
    second = add_up([second[0, 0]] + [along_x(second[a, b], a, b) for a, b in near]).astype(BF)
    first = add_up([first[0, 0]] + [along_x(first[a, b], a, b) for a, b in near]).astype(BF)
    second = add_up([second[0]] + [along_y(second[k], k) for k in (1, 3, 2)]).astype(BF)
    both = jnp.concatenate([first, second], axis=1)
    both = both.reshape(BLOCK, 8, BLOCK).transpose(1, 0, 2)
    z = lax.axis_index("z")
    both = jnp.roll(both, -z, axis=0)
    total = add_up([both[0]] + [along_z(both[k], k) for k in range(1, 8)])
    return layer_out, token_grad, total[:, :72], total[:, 72:]


def solution(mesh):
    devices = mesh.devices.reshape(8, 2, 2, 2, 4)
    fine = Mesh(devices, ("z", "xl", "core", "xh", "y"))
    dp, seg = ("z", "xl", "core"), ("xh", "y")
    placed = (P(dp, seg, None), P(dp, seg, None), P(dp), P(), P(), P(dp, seg, None))
    return jax.shard_map(
        per_device,
        mesh=fine,
        in_specs=placed,
        out_specs=(P(dp, seg, None), P(dp, seg, None), P(seg, dp), P(seg, dp)),
        check_vma=False,
    )
```

time: 691 us -> 124 us (0.18)
  waiting for transfers between devices: 439 us -> 12.2 us
  local copies, waits for them, and re-layouts: 87.9 us -> 21.9 us
  blocking collectives: 76.8 us -> 13 us
  starting transfers between devices: 0.39 us -> 50.7 us
  matrix products: 37.6 us -> 0 us
  other arithmetic: 29.4 us -> 4.38 us
  Pallas kernels: 0 us -> 17.9 us
  between operations: 16.4 us -> 1.51 us
    reduce_scatter x4 -> x0, waiting for transfers between devices: 223 us -> none  [the longest x1 88.9 us: per_device(): lax.psum_scatter(grad_in.astype(jnp.bfloat16), 'seg', scatter_dimension=0...]
    unnamed x6 -> x0, waiting for transfers between devices: 216 us -> none
    all_gather x2 -> x0, blocking collectives: 76.8 us -> none  [the longest x1 38.4 us: per_device(): lax.all_gather(own_keys, 'seg', axis=0, tiled=True)]
    ppermute x0 -> x23, starting transfers between devices: none -> 44.4 us  [the longest x7 18.5 us: along_z(): return lax.ppermute(x, 'z', [(i, (i + k) % 8) for i in range(8)])]
    mul x24 -> x0, local copies, waits for them, and re-layouts: 38.7 us -> none  [the longest x16 26.8 us: place_samples(): spread = samples[:, None] * chosen[None]]
    dot_general x18 -> x0, matrix products: 37.6 us -> none  [the longest x3 7.7 us: dense_branch(): jnp.einsum('bhqk,bkhe->bqhe', weights, value_rows.astype(jnp.float32))]
    pallas_call x0 -> x6, Pallas kernels: none -> 17.9 us  [call(): pl.pallas_call(kernel, out_shape=[jax.ShapeDtypeStruct(shape, dtype) for...]
    reduce_sum x10 -> x0, other arithmetic: 13.7 us -> none  [the longest x2 4 us: place_samples(): spread = samples[:, None] * chosen[None]]
  transfers between devices with their start and end apart: 5 -> 24, of which waited for: 5 -> 6; matrix products, arithmetic and copies ran while one was open for 15% -> 3% of each run, Pallas kernels for 0% -> 7%
where the time goes in v1:
time: 124 us; the launch traced here: 122 us
  starting transfers between devices  50.7 us (41%)
  local copies, waits for them, and re-layouts  21.9 us (18%)
  Pallas kernels  17.9 us (14%)
  blocking collectives  13 us (10%)
  waiting for transfers between devices  12.2 us (10%)
  other arithmetic  4.38 us (4%)
  between operations  1.51 us (1%)
    ppermute x7, starting transfers between devices, along_z(): return lax.ppermute(x, 'z', [(i, (i + k) % 8) for i in range(8)])  18.5 us
    pallas_call x6, Pallas kernels, call(): pl.pallas_call(kernel, out_shape=[jax.ShapeDtypeStruct(shape, dtype) for...  17.9 us
    unnamed x47, local copies, waits for them, and re-layouts  17.9 us
    ppermute x6, starting transfers between devices, along_x(): return lax.ppermute(x, ('xl', 'xh'), pairs)  15.2 us
    all_to_all x1, blocking collectives, per_device(): message = lax.all_to_all(message, ('xh', 'y'), 0, 0, tiled=True)  13 us
    ppermute x6, starting transfers between devices, along_y(): return lax.ppermute(x, 'y', [(i, (i + k) % 4) for i in range(4)])  9.65 us
    ppermute x6, waiting for transfers between devices, along_y(): return lax.ppermute(x, 'y', [(i, (i + k) % 4) for i in range(4)])  7.87 us
    all_to_all x1, starting transfers between devices, per_device(): reply = lax.all_to_all(reply, ('xh', 'y'), 0, 0, tiled=True)  6.24 us
  transfers between devices with their start and end apart: 24, of which 6 were waited for; matrix products, arithmetic and copies ran while one was open for 3% of the time, Pallas kernels for 7%

profile of v1, /device:TPU:6, one launch (start us, length us, event | category | flops | bytes accessed | tf_op | source)
XLA Modules:
  0.0 121.7 jit_solution(221497797336202273)
XLA Ops:
  1.3 0.8 copy.10.coord_ref
  2.1 2.0 %copy-done = bf16[768,2304]{1,0:T(8,128)(2,1)S(1)} copy-done((bf16[768,2304]{1,0:T(8,128)(2,1)S(1)}, bf16[768,2304]{1,0:T(8,128)(2,1)}, u32[]{:S(2)}) %copy-start) | copy-done | bytes 3538968
  4.1 1.3 %copy-done.2 = bf16[768,768]{1,0:T(8,128)(2,1)S(1)} copy-done((bf16[768,768]{1,0:T(8,128)(2,1)S(1)}, bf16[768,768]{1,0:T(8,128)(2,1)}, u32[]{:S(2)}) %copy-start.2) | copy-done | bytes 1179672
  5.3 0.9 copy-done.19
  6.3 0.9 copy-done.20
  7.2 3.9 %shard_map.93 = (bf16[8,4,32,128]{3,2,1,0:T(8,128)(2,1)S(1)}, bf16[128,2304]{1,0:T(8,128)(2,1)S(1)}, bf16[128,768]{1,0:T(8,128)(2,1)S(1)}, f32[128,768]{1,0:T(8,...) custom-call(s32[1]{0:T(128)S(6)} %copy.13.length_ref, ...), custom_call_target="tpu_custom_call" | custom-call | tf_op jit(solution)/shard_map/pallas_call | solution.py:400
  11.1 0.7 copy-done.17
  11.8 0.6 copy-done.21
  12.4 13.0 %all_to_all.10.message_ref = bf16[8,4,32,128]{3,2,1,0:T(8,128)(2,1)S(1)} all-to-all(bf16[8,4,32,128]{3,2,1,0:T(8,128)(2,1)S(1)} %get-tuple-element.23), channel_id=1, replica_groups=mesh['z'=8,'xl'=2,'core'=2,'xh'=2,'y'=4] {'xh','y'}, dimensions={0} | all-to-all | bytes 524288 | tf_op jit(solution)/shard_map/all_to_all | solution.py:446
  25.4 2.3 %shard_map.94 = bf16[8,4,32,128]{3,2,1,0:T(8,128)(2,1)} custom-call(s32[1]{0:T(128)S(6)} %copy.13.length_ref, bf16[8,4,32,128]{3,2,1,0:T(8,128)(2,1)S(1)} %all_to_all.10.message_ref), custom_call_target="tpu_custom_call" | custom-call | tf_op jit(solution)/shard_map/pallas_call | solution.py:400
  27.7 6.2 %all-to-all-start.1 = ((bf16[8,4,32,128]{3,2,1,0:T(8,128)(2,1)}), bf16[8,4,32,128]{3,2,1,0:T(8,128)(2,1)S(1)}, u32[]{:S(2)}, u32[]{:S(2)}) async-start(bf16[8,4,32,128]{3,2,1,0:T(8,128)(2,1)} %shard_map.94), calls=%async_computation.1 | async-start | bytes 524288 | tf_op jit(solution)/shard_map/all_to_all | solution.py:464
  34.0 0.8 slice_bitcast_fusion
  34.8 3.4 %shard_map.95 = (f32[128,768]{1,0:T(8,128)S(1)}, f32[3,128,768]{2,1,0:T(8,128)S(1)}, f32[2,256,128]{2,1,0:T(8,128)S(1)}, f32[2,256,128]{2,1,0:T(8,128)S(1)}, f32[2,256,384]{2,1,0:T(8,128)S(1)}) custom-call(s32[1]{0:T(128)S(6)} %copy.13.length_ref, bf16[128,2304]{1,0:T(8,128)(2,1)S(1)} %get-tuple-element.24.packed_ref, ...), custom_call_target="tpu_custom_call" | custom-call | tf_op jit(solution)/shard_map/pallas_call | solution.py:400
  38.2 0.7 copy-done.11
  39.0 0.7 copy-done.13
  39.7 0.7 copy-done.15
  40.4 1.0 copy-done.12
  41.4 0.9 copy-done.14
  42.3 0.9 copy-done.16
  43.3 3.0 %shard_map.96 = (bf16[128,768]{1,0:T(8,128)(2,1)S(1)}, bf16[128,2304]{1,0:T(8,128)(2,1)S(1)}, bf16[2,128,1536]{2,1,0:T(8,128)(2,1)S(1)}) custom-call(bf16[8,4,32,128]{3,2,1,0:T(8,128)(2,1)S(1)} %all-to-all-done.1.reply_ref, bf16[128,2304]{1,0:T(8,128)(2,1)S(1)} %get-tuple-element.24.packed_ref, bf16[128,768]{1,0:T(8,128)(2,1)S(1)} %get-tuple-element.25.g_ref, ...), custom_call_target="tpu_custom_call" | custom-call | tf_op jit(solution)/shard_map/pallas_call | solution.py:400
  46.3 0.6 collective-permute-start.2
  46.9 0.5 copy-done.18
  47.4 0.5 collective-permute-start
  48.0 1.1 collective-permute-done.n1_ref
  49.0 0.4 collective-permute-done.1.b1_ref
  49.4 2.8 %shard_map.98 = (bf16[4,2,2,96,384]{4,3,2,1,0:T(8,128)(2,1)S(1)}, bf16[2,2,4,96,384]{4,3,2,1,0:T(8,128)(2,1)S(1)}) custom-call(bf16[128,768]{1,0:T(8,128)(2,1)S(1)} %copy-done.18, bf16[128,768]{1,0:T(8,128)(2,1)S(1)} %collective-permute-done.n1_ref, bf16[128,768]{1,0:T(8,128)(2,1)S(1)} %get-tuple-element.31.blended_ref.b0_ref, ...), custom_call_target="tpu_custom_call" | custom-call | tf_op jit(solution)/shard_map/pallas_call | solution.py:400
  52.2 0.1 slice_bitcast_fusion.9
  52.3 1.5 %collective-permute-start.4 = (bf16[2,2,96,384]{3,2,1,0:T(8,128)(2,1)S(1)}, bf16[2,2,96,384]{3,2,1,0:T(8,128)(2,1)}, u32[]{:S(2)}, u32[]{:S(2)}) collective-permute-start(bf16[2,2,96,384]{3,2,1,0:T(8,128)(2,1)S(1)} %get-tuple-element.42), channel_id=1, source_target_pairs={{0,1},{1,2},{2,3},{3,0},{4,5},{5,6},{6,7},{7,4},{8,9},{9,10},{10,1... | collective-permute-start | bytes 884744 | tf_op jit(solution)/shard_map/ppermute | solution.py:414
  53.9 1.8 %collective-permute-start.5 = (bf16[2,2,96,384]{3,2,1,0:T(8,128)(2,1)S(1)}, bf16[2,2,96,384]{3,2,1,0:T(8,128)(2,1)}, u32[]{:S(2)}, u32[]{:S(2)}) collective-permute-start(bf16[2,2,96,384]{3,2,1,0:T(8,128)(2,1)S(1)} %get-tuple-element.44), channel_id=1, source_target_pairs={{0,3},{1,0},{2,1},{3,2},{4,7},{5,4},{6,5},{7,6},{8,11},{9,8},{10,9... | collective-permute-start | bytes 884744 | tf_op jit(solution)/shard_map/ppermute | solution.py:414
  55.7 1.8 %collective-permute-start.6 = (bf16[2,2,96,384]{3,2,1,0:T(8,128)(2,1)S(1)}, bf16[2,2,96,384]{3,2,1,0:T(8,128)(2,1)}, u32[]{:S(2)}, u32[]{:S(2)}) collective-permute-start(bf16[2,2,96,384]{3,2,1,0:T(8,128)(2,1)S(1)} %get-tuple-element.43), channel_id=1, source_target_pairs={{0,2},{1,3},{2,0},{3,1},{4,6},{5,7},{6,4},{7,5},{8,10},{9,11},{10,... | collective-permute-start | bytes 884744 | tf_op jit(solution)/shard_map/ppermute | solution.py:414
  57.4 0.1 slice_bitcast_fusion.6
  57.5 0.9 collective-permute-start.10
  58.5 1.1 collective-permute-start.11
  59.6 3.3 %collective-permute-done.4 = bf16[2,2,96,384]{3,2,1,0:T(8,128)(2,1)} collective-permute-done((bf16[2,2,96,384]{3,2,1,0:T(8,128)(2,1)S(1)}, bf16[2,2,96,384]{3,2,1,0:T(8,128)(2,1)}, u32[]{:S(2)}, u32[]{:S(2)}) %collective-permute-start.4) | collective-permute-done | bytes 294944 | tf_op jit(solution)/shard_map/ppermute | solution.py:414
  62.9 8.4 %collective-permute-start.12 = (bf16[4,96,384]{2,1,0:T(8,128)(2,1)S(1)}, bf16[4,96,384]{2,1,0:T(8,128)(2,1)S(1)}, u32[]{:S(2)}, u32[]{:S(2)}) collective-permute-start(bf16[4,96,384]{2,1,0:T(8,128)(2,1)S(1)} %get-tuple-element.46), channel_id=1, source_target_pairs={{0,20},{4,16},{16,4},{20,0},{1,21},{5,17},{17,5},{21,1},{2,22},{6,... | collective-permute-start | bytes 884744 | tf_op jit(solution)/shard_map/ppermute | solution.py:419
  71.3 1.3 %fusion.5 = bf16[2,2,96,384]{3,2,1,0:T(8,128)(2,1)S(1)} fusion(bf16[2,2,96,384]{3,2,1,0:T(8,128)(2,1)} %collective-permute-done.6, bf16[2,2,96,384]{3,2,1,0:T(8,128)(2,1)} %collective-permute-done.5, bf16[2,2,96,384]{3,2,1,0:T(8,128)(2,1)} %collective-permute-done.4, bf16[4,2,2,96,384]{4,3,2,1,0:T(8,128)(2,1)S(1)} %get-tuple-element.40), kind=kLoop, calls=%fused_computation.7 | loop fusion | flops 1179648 | bytes 1474560 | tf_op jit(solution)/shard_map/convert_element_type | solution.py:487
  72.6 0.1 collective-permute-start.7
  72.7 1.5 %collective-permute-start.8 = (bf16[96,384]{1,0:T(8,128)(2,1)S(1)}, bf16[96,384]{1,0:T(8,128)(2,1)S(1)}, u32[]{:S(2)}, u32[]{:S(2)}) collective-permute-start(bf16[96,384]{1,0:T(8,128)(2,1)S(1)} %get-tuple-element.54), channel_id=1, source_target_pairs={{0,4},{4,0},{16,20},{20,16},{1,5},{5,1},{17,21},{21,17},{2,6},{6,2... | collective-permute-start | bytes 221192 | tf_op jit(solution)/shard_map/ppermute | solution.py:419
  74.2 3.2 %collective-permute-start.9 = (bf16[96,384]{1,0:T(8,128)(2,1)S(1)}, bf16[96,384]{1,0:T(8,128)(2,1)S(1)}, u32[]{:S(2)}, u32[]{:S(2)}) collective-permute-start(bf16[96,384]{1,0:T(8,128)(2,1)S(1)} %get-tuple-element.53), channel_id=1, source_target_pairs={{0,20},{4,16},{16,4},{20,0},{1,21},{5,17},{17,5},{21,1},{2,22},{6,... | collective-permute-start | bytes 221192 | tf_op jit(solution)/shard_map/ppermute | solution.py:419
  77.4 2.9 %collective-permute-done.12 = bf16[4,96,384]{2,1,0:T(8,128)(2,1)S(1)} collective-permute-done((bf16[4,96,384]{2,1,0:T(8,128)(2,1)S(1)}, bf16[4,96,384]{2,1,0:T(8,128)(2,1)S(1)}, u32[]{:S(2)}, u32[]{:S(2)}) %collective-permute-start.12) | collective-permute-done | bytes 294944 | tf_op jit(solution)/shard_map/ppermute | solution.py:419
  80.3 1.3 %fusion.2 = bf16[4,96,384]{2,1,0:T(8,128)(2,1)S(1)} fusion(bf16[4,96,384]{2,1,0:T(8,128)(2,1)S(1)} %collective-permute-done.12, bf16[4,96,384]{2,1,0:T(8,128)(2,1)S(1)} %collective-permute-done.11, bf16[4,96,384]{2,1,0:T(8,128)(2,1)S(1)} %collective-permute-done.10, bf16[2,2,4,96,384]{4,3,2,1,0:T(8,128)(2,1)} %copy-done.4), kind=kLoop, calls=%fused_computation.3 | loop fusion | flops 1179648 | bytes 1474560 | tf_op jit(solution)/shard_map/convert_element_type | solution.py:488
  81.6 0.7 collective-permute-start.13
  82.4 2.6 %collective-permute-start.14 = (bf16[96,384]{1,0:T(8,128)(2,1)S(1)}, bf16[96,384]{1,0:T(8,128)(2,1)S(1)}, u32[]{:S(2)}, u32[]{:S(2)}) collective-permute-start(bf16[96,384]{1,0:T(8,128)(2,1)S(1)} %get-tuple-element.57), channel_id=1, source_target_pairs={{0,3},{1,0},{2,1},{3,2},{4,7},{5,4},{6,5},{7,6},{8,11},{9,8},{10,9... | collective-permute-start | bytes 221192 | tf_op jit(solution)/shard_map/ppermute | solution.py:414
  84.9 1.3 %collective-permute-start.15 = (bf16[96,384]{1,0:T(8,128)(2,1)S(1)}, bf16[96,384]{1,0:T(8,128)(2,1)S(1)}, u32[]{:S(2)}, u32[]{:S(2)}) collective-permute-start(bf16[96,384]{1,0:T(8,128)(2,1)S(1)} %get-tuple-element.56), channel_id=1, source_target_pairs={{0,2},{1,3},{2,0},{3,1},{4,6},{5,7},{6,4},{7,5},{8,10},{9,11},{10,... | collective-permute-start | bytes 221192 | tf_op jit(solution)/shard_map/ppermute | solution.py:414
  86.2 1.2 collective-permute-done.13
  87.5 3.3 %collective-permute-done.15 = bf16[96,384]{1,0:T(8,128)(2,1)S(1)} collective-permute-done((bf16[96,384]{1,0:T(8,128)(2,1)S(1)}, bf16[96,384]{1,0:T(8,128)(2,1)S(1)}, u32[]{:S(2)}, u32[]{:S(2)}) %collective-permute-start.15) | collective-permute-done | bytes 73760 | tf_op jit(solution)/shard_map/ppermute | solution.py:414
  90.8 0.7 pad_maximum_fusion
  91.5 1.7 %copy.12 = bf16[96,768]{0,1:T(8,128)(2,1)} copy(bf16[96,768]{1,0:T(8,128)(2,1)} %pad_maximum_fusion) | data formatting | bytes 294912 | tf_op jit(solution)/shard_map/reshape | solution.py:492
  93.2 1.0 fusion.6
  94.3 2.0 %collective-permute-start.16 = (bf16[96,96]{0,1:T(8,128)(2,1)S(1)}, bf16[96,96]{0,1:T(8,128)(2,1)S(1)}, u32[]{:S(2)}, u32[]{:S(2)}) collective-permute-start(bf16[96,96]{0,1:T(8,128)(2,1)S(1)} %get-tuple-element.58), channel_id=1, source_target_pairs={{0,32},{32,64},{64,96},{96,128},{128,160},{160,192},{192,224},{224... | collective-permute-start | bytes 55304 | tf_op jit(solution)/shard_map/ppermute | solution.py:423
  96.3 3.3 %collective-permute-start.17 = (bf16[96,96]{0,1:T(8,128)(2,1)S(1)}, bf16[96,96]{0,1:T(8,128)(2,1)S(1)}, u32[]{:S(2)}, u32[]{:S(2)}) collective-permute-start(bf16[96,96]{0,1:T(8,128)(2,1)S(1)} %get-tuple-element.63), channel_id=1, source_target_pairs={{0,64},{32,96},{64,128},{96,160},{128,192},{160,224},{192,0},{224,... | collective-permute-start | bytes 55304 | tf_op jit(solution)/shard_map/ppermute | solution.py:423
  99.6 4.0 %collective-permute-start.18 = (bf16[96,96]{0,1:T(8,128)(2,1)S(1)}, bf16[96,96]{0,1:T(8,128)(2,1)S(1)}, u32[]{:S(2)}, u32[]{:S(2)}) collective-permute-start(bf16[96,96]{0,1:T(8,128)(2,1)S(1)} %get-tuple-element.62), channel_id=1, source_target_pairs={{0,96},{32,128},{64,160},{96,192},{128,224},{160,0},{192,32},{224,... | collective-permute-start | bytes 55304 | tf_op jit(solution)/shard_map/ppermute | solution.py:423
  103.6 0.5 collective-permute-start.19
  104.1 5.0 %collective-permute-start.20 = (bf16[96,96]{0,1:T(8,128)(2,1)S(1)}, bf16[96,96]{0,1:T(8,128)(2,1)S(1)}, u32[]{:S(2)}, u32[]{:S(2)}) collective-permute-start(bf16[96,96]{0,1:T(8,128)(2,1)S(1)} %get-tuple-element.60), channel_id=1, source_target_pairs={{0,160},{32,192},{64,224},{96,0},{128,32},{160,64},{192,96},{224,1... | collective-permute-start | bytes 55304 | tf_op jit(solution)/shard_map/ppermute | solution.py:423
  109.1 2.7 %collective-permute-start.21 = (bf16[96,96]{0,1:T(8,128)(2,1)S(1)}, bf16[96,96]{0,1:T(8,128)(2,1)S(1)}, u32[]{:S(2)}, u32[]{:S(2)}) collective-permute-start(bf16[96,96]{0,1:T(8,128)(2,1)S(1)} %get-tuple-element.59), channel_id=1, source_target_pairs={{0,192},{32,224},{64,0},{96,32},{128,64},{160,96},{192,128},{224,1... | collective-permute-start | bytes 55304 | tf_op jit(solution)/shard_map/ppermute | solution.py:423
  111.8 1.0 collective-permute-start.22
  112.8 1.3 %copy-done.3 = bf16[768,768]{1,0:T(8,128)(2,1)S(1)} copy-done((bf16[768,768]{1,0:T(8,128)(2,1)S(1)}, bf16[768,768]{1,0:T(8,128)(2,1)}, u32[]{:S(2)}) %copy-start.3) | copy-done | bytes 1179672
  114.1 0.9 copy-done.6
  115.0 1.1 copy-done.8
  116.0 1.0 copy-done.10
  117.0 0.8 copy-done.22
  117.9 2.5 %shard_map.97 = (bf16[1,128,768]{2,1,0:T(8,128)(2,1)}, bf16[1,128,768]{2,1,0:T(8,128)(2,1)}) custom-call(s32[1]{0:T(128)S(6)} %copy.13.length_ref, bf16[128,768]{1,0:T(8,128)(2,1)S(1)} %copy-done.6, bf16[128,2304]{1,0:T(8,128)(2,1)S(1)} %copy-done.8, f32[128,768]{1,0:T(8,128)S(1)} %copy-done.10, f32[128,128]{1,0:T(8,128)S(1)} %copy-done.22, ...), custom_call_target="tpu_custom_call" | custom-call | tf_op jit(solution)/shard_map/pallas_call | solution.py:400
  120.4 0.6 slice.136
  121.0 0.6 slice.137
  (55 shorter events, 0.3 us)
Async XLA Ops:
  2.1 2.0 %copy-start = (bf16[768,2304]{1,0:T(8,128)(2,1)S(1)}, bf16[768,2304]{1,0:T(8,128)(2,1)}, u32[]{:S(2)}) copy-start(bf16[768,2304]{1,0:T(8,128)(2,1)} %w_qkv_ref.3) | copy-start | bytes 10616836
  4.1 1.3 %copy-start.2 = (bf16[768,768]{1,0:T(8,128)(2,1)S(1)}, bf16[768,768]{1,0:T(8,128)(2,1)}, u32[]{:S(2)}) copy-start(bf16[768,768]{1,0:T(8,128)(2,1)} %w_out_ref.3) | copy-start | bytes 3538948
  5.3 0.9 copy-start.19
  6.3 0.9 copy-start.20
  11.1 0.7 copy-start.17
  11.8 0.6 copy-start.21
  12.4 21.6 %copy-start.9 = (f32[128,768]{1,0:T(8,128)}, f32[128,768]{1,0:T(8,128)S(1)}, u32[]{:S(2)}) copy-start(f32[128,768]{1,0:T(8,128)S(1)} %get-tuple-element.33.xhat_ref) | copy-start | bytes 1179652
  27.7 12.7 %all-to-all-start.1 = ((bf16[8,4,32,128]{3,2,1,0:T(8,128)(2,1)}), bf16[8,4,32,128]{3,2,1,0:T(8,128)(2,1)S(1)}, u32[]{:S(2)}, u32[]{:S(2)}) async-start(bf16[8,4,32,128]{3,2,1,0:T(8,128)(2,1)} %shard_map.94), calls=%async_computation.1 | async-start | bytes 524288 | tf_op jit(solution)/shard_map/all_to_all | solution.py:464
  34.8 14.2 %collective-permute-start.3 = (bf16[128,1536]{1,0:T(8,128)(2,1)}, bf16[128,1536]{1,0:T(8,128)(2,1)}, u32[]{:S(2)}, u32[]{:S(2)}) collective-permute-start(bf16[128,1536]{1,0:T(8,128)(2,1)} %get-tuple-element.48), channel_id=1, source_target_pairs={{0,8},{8,0},{1,9},{9,1},{2,10},{10,2},{3,11},{11,3},{4,12},{12,4},... | collective-permute-start | bytes 1179656 | tf_op jit(solution)/shard_map/ppermute | solution.py:410
  38.2 0.7 copy-start.11
  39.0 0.7 copy-start.13
  39.7 0.7 copy-start.15
  40.4 1.0 copy-start.12
  41.4 0.9 copy-start.14
  42.3 0.9 copy-start.16
  46.3 3.1 %copy-start.7 = (bf16[128,2304]{1,0:T(8,128)(2,1)}, bf16[128,2304]{1,0:T(8,128)(2,1)S(1)}, u32[]{:S(2)}) copy-start(bf16[128,2304]{1,0:T(8,128)(2,1)S(1)} %get-tuple-element.32.packed_grad_ref) | copy-start | bytes 1769476
  46.3 6.0 %copy-start.5 = (bf16[128,768]{1,0:T(8,128)(2,1)}, bf16[128,768]{1,0:T(8,128)(2,1)S(1)}, u32[]{:S(2)}) copy-start(bf16[128,768]{1,0:T(8,128)(2,1)S(1)} %get-tuple-element.31.blended_ref.b0_ref) | copy-start | bytes 589828
  46.3 1.2 copy-start.18
  46.3 3.0 %collective-permute-start.2 = (bf16[128,1536]{1,0:T(8,128)(2,1)S(1)}, bf16[128,1536]{1,0:T(8,128)(2,1)S(1)}, u32[]{:S(2)}, u32[]{:S(2)}) collective-permute-start(bf16[128,1536]{1,0:T(8,128)(2,1)S(1)} %get-tuple-element.50), channel_id=1, source_target_pairs={{0,8},{8,0},{1,9},{9,1},{2,10},{10,2},{3,11},{11,3},{4,12},{12,4},... | collective-permute-start | bytes 1179656 | tf_op jit(solution)/shard_map/ppermute | solution.py:410
  47.4 1.6 %collective-permute-start = (bf16[128,768]{1,0:T(8,128)(2,1)S(1)}, bf16[128,768]{1,0:T(8,128)(2,1)S(1)}, u32[]{:S(2)}, u32[]{:S(2)}) collective-permute-start(bf16[128,768]{1,0:T(8,128)(2,1)S(1)} %copy-done.18), channel_id=1, source_target_pairs={{0,8},{8,0},{1,9},{9,1},{2,10},{10,2},{3,11},{11,3},{4,12},{12,4},... | collective-permute-start | bytes 589832 | tf_op jit(solution)/shard_map/ppermute | solution.py:410
  47.9 1.4 %collective-permute-start.1 = (bf16[128,768]{1,0:T(8,128)(2,1)S(1)}, bf16[128,768]{1,0:T(8,128)(2,1)S(1)}, u32[]{:S(2)}, u32[]{:S(2)}) collective-permute-start(bf16[128,768]{1,0:T(8,128)(2,1)S(1)} %get-tuple-element.31.blended_ref.b0_ref), channel_id=1, source_target_pairs={{0,8},{8,0},{1,9},{9,1},{2,10},{10,2},{3,11},{11,3},{4,12},{12,4},... | collective-permute-start | bytes 589832 | tf_op jit(solution)/shard_map/ppermute | solution.py:410
  52.2 5.3 %copy-start.4 = (bf16[2,2,4,96,384]{4,3,2,1,0:T(8,128)(2,1)}, bf16[2,2,4,96,384]{4,3,2,1,0:T(8,128)(2,1)S(1)}, u32[]{:S(2)}) copy-start(bf16[2,2,4,96,384]{4,3,2,1,0:T(8,128)(2,1)S(1)} %get-tuple-element.41) | copy-start | bytes 3538948
  52.3 10.6 %collective-permute-start.4 = (bf16[2,2,96,384]{3,2,1,0:T(8,128)(2,1)S(1)}, bf16[2,2,96,384]{3,2,1,0:T(8,128)(2,1)}, u32[]{:S(2)}, u32[]{:S(2)}) collective-permute-start(bf16[2,2,96,384]{3,2,1,0:T(8,128)(2,1)S(1)} %get-tuple-element.42), channel_id=1, source_target_pairs={{0,1},{1,2},{2,3},{3,0},{4,5},{5,6},{6,7},{7,4},{8,9},{9,10},{10,1... | collective-permute-start | bytes 884744 | tf_op jit(solution)/shard_map/ppermute | solution.py:414
  53.9 17.4 %collective-permute-start.5 = (bf16[2,2,96,384]{3,2,1,0:T(8,128)(2,1)S(1)}, bf16[2,2,96,384]{3,2,1,0:T(8,128)(2,1)}, u32[]{:S(2)}, u32[]{:S(2)}) collective-permute-start(bf16[2,2,96,384]{3,2,1,0:T(8,128)(2,1)S(1)} %get-tuple-element.44), channel_id=1, source_target_pairs={{0,3},{1,0},{2,1},{3,2},{4,7},{5,4},{6,5},{7,6},{8,11},{9,8},{10,9... | collective-permute-start | bytes 884744 | tf_op jit(solution)/shard_map/ppermute | solution.py:414
  55.7 15.6 %collective-permute-start.6 = (bf16[2,2,96,384]{3,2,1,0:T(8,128)(2,1)S(1)}, bf16[2,2,96,384]{3,2,1,0:T(8,128)(2,1)}, u32[]{:S(2)}, u32[]{:S(2)}) collective-permute-start(bf16[2,2,96,384]{3,2,1,0:T(8,128)(2,1)S(1)} %get-tuple-element.43), channel_id=1, source_target_pairs={{0,2},{1,3},{2,0},{3,1},{4,6},{5,7},{6,4},{7,5},{8,10},{9,11},{10,... | collective-permute-start | bytes 884744 | tf_op jit(solution)/shard_map/ppermute | solution.py:414
  57.5 16.6 %collective-permute-start.10 = (bf16[4,96,384]{2,1,0:T(8,128)(2,1)S(1)}, bf16[4,96,384]{2,1,0:T(8,128)(2,1)S(1)}, u32[]{:S(2)}, u32[]{:S(2)}) collective-permute-start(bf16[4,96,384]{2,1,0:T(8,128)(2,1)S(1)} %get-tuple-element.45), channel_id=1, source_target_pairs={{0,16},{4,20},{16,0},{20,4},{1,17},{5,21},{17,1},{21,5},{2,18},{6,... | collective-permute-start | bytes 884744 | tf_op jit(solution)/shard_map/ppermute | solution.py:419
  58.5 19.0 %collective-permute-start.11 = (bf16[4,96,384]{2,1,0:T(8,128)(2,1)S(1)}, bf16[4,96,384]{2,1,0:T(8,128)(2,1)S(1)}, u32[]{:S(2)}, u32[]{:S(2)}) collective-permute-start(bf16[4,96,384]{2,1,0:T(8,128)(2,1)S(1)} %get-tuple-element.47), channel_id=1, source_target_pairs={{0,4},{4,0},{16,20},{20,16},{1,5},{5,1},{17,21},{21,17},{2,6},{6,2... | collective-permute-start | bytes 884744 | tf_op jit(solution)/shard_map/ppermute | solution.py:419
  62.9 17.4 %collective-permute-start.12 = (bf16[4,96,384]{2,1,0:T(8,128)(2,1)S(1)}, bf16[4,96,384]{2,1,0:T(8,128)(2,1)S(1)}, u32[]{:S(2)}, u32[]{:S(2)}) collective-permute-start(bf16[4,96,384]{2,1,0:T(8,128)(2,1)S(1)} %get-tuple-element.46), channel_id=1, source_target_pairs={{0,20},{4,16},{16,4},{20,0},{1,21},{5,17},{17,5},{21,1},{2,22},{6,... | collective-permute-start | bytes 884744 | tf_op jit(solution)/shard_map/ppermute | solution.py:419
  72.6 12.3 %collective-permute-start.7 = (bf16[96,384]{1,0:T(8,128)(2,1)S(1)}, bf16[96,384]{1,0:T(8,128)(2,1)S(1)}, u32[]{:S(2)}, u32[]{:S(2)}) collective-permute-start(bf16[96,384]{1,0:T(8,128)(2,1)S(1)} %get-tuple-element.52), channel_id=1, source_target_pairs={{0,16},{4,20},{16,0},{20,4},{1,17},{5,21},{17,1},{21,5},{2,18},{6,... | collective-permute-start | bytes 221192 | tf_op jit(solution)/shard_map/ppermute | solution.py:419
  72.7 13.5 %collective-permute-start.8 = (bf16[96,384]{1,0:T(8,128)(2,1)S(1)}, bf16[96,384]{1,0:T(8,128)(2,1)S(1)}, u32[]{:S(2)}, u32[]{:S(2)}) collective-permute-start(bf16[96,384]{1,0:T(8,128)(2,1)S(1)} %get-tuple-element.54), channel_id=1, source_target_pairs={{0,4},{4,0},{16,20},{20,16},{1,5},{5,1},{17,21},{21,17},{2,6},{6,2... | collective-permute-start | bytes 221192 | tf_op jit(solution)/shard_map/ppermute | solution.py:419
  74.2 12.0 %collective-permute-start.9 = (bf16[96,384]{1,0:T(8,128)(2,1)S(1)}, bf16[96,384]{1,0:T(8,128)(2,1)S(1)}, u32[]{:S(2)}, u32[]{:S(2)}) collective-permute-start(bf16[96,384]{1,0:T(8,128)(2,1)S(1)} %get-tuple-element.53), channel_id=1, source_target_pairs={{0,20},{4,16},{16,4},{20,0},{1,21},{5,17},{17,5},{21,1},{2,22},{6,... | collective-permute-start | bytes 221192 | tf_op jit(solution)/shard_map/ppermute | solution.py:419
  80.3 32.5 %copy-start.1 = (bf16[768,2304]{1,0:T(8,128)(2,1)S(1)}, bf16[768,2304]{1,0:T(8,128)(2,1)}, u32[]{:S(2)}) copy-start(bf16[768,2304]{1,0:T(8,128)(2,1)} %w_qkv_ref.3) | copy-start | bytes 10616836
  81.6 5.8 %collective-permute-start.13 = (bf16[96,384]{1,0:T(8,128)(2,1)S(1)}, bf16[96,384]{1,0:T(8,128)(2,1)S(1)}, u32[]{:S(2)}, u32[]{:S(2)}) collective-permute-start(bf16[96,384]{1,0:T(8,128)(2,1)S(1)} %get-tuple-element.55), channel_id=1, source_target_pairs={{0,1},{1,2},{2,3},{3,0},{4,5},{5,6},{6,7},{7,4},{8,9},{9,10},{10,1... | collective-permute-start | bytes 221192 | tf_op jit(solution)/shard_map/ppermute | solution.py:414
  82.4 5.1 %collective-permute-start.14 = (bf16[96,384]{1,0:T(8,128)(2,1)S(1)}, bf16[96,384]{1,0:T(8,128)(2,1)S(1)}, u32[]{:S(2)}, u32[]{:S(2)}) collective-permute-start(bf16[96,384]{1,0:T(8,128)(2,1)S(1)} %get-tuple-element.57), channel_id=1, source_target_pairs={{0,3},{1,0},{2,1},{3,2},{4,7},{5,4},{6,5},{7,6},{8,11},{9,8},{10,9... | collective-permute-start | bytes 221192 | tf_op jit(solution)/shard_map/ppermute | solution.py:414
  84.9 5.9 %collective-permute-start.15 = (bf16[96,384]{1,0:T(8,128)(2,1)S(1)}, bf16[96,384]{1,0:T(8,128)(2,1)S(1)}, u32[]{:S(2)}, u32[]{:S(2)}) collective-permute-start(bf16[96,384]{1,0:T(8,128)(2,1)S(1)} %get-tuple-element.56), channel_id=1, source_target_pairs={{0,2},{1,3},{2,0},{3,1},{4,6},{5,7},{6,4},{7,5},{8,10},{9,11},{10,... | collective-permute-start | bytes 221192 | tf_op jit(solution)/shard_map/ppermute | solution.py:414
  94.3 14.8 %collective-permute-start.16 = (bf16[96,96]{0,1:T(8,128)(2,1)S(1)}, bf16[96,96]{0,1:T(8,128)(2,1)S(1)}, u32[]{:S(2)}, u32[]{:S(2)}) collective-permute-start(bf16[96,96]{0,1:T(8,128)(2,1)S(1)} %get-tuple-element.58), channel_id=1, source_target_pairs={{0,32},{32,64},{64,96},{96,128},{128,160},{160,192},{192,224},{224... | collective-permute-start | bytes 55304 | tf_op jit(solution)/shard_map/ppermute | solution.py:423
  96.3 15.5 %collective-permute-start.17 = (bf16[96,96]{0,1:T(8,128)(2,1)S(1)}, bf16[96,96]{0,1:T(8,128)(2,1)S(1)}, u32[]{:S(2)}, u32[]{:S(2)}) collective-permute-start(bf16[96,96]{0,1:T(8,128)(2,1)S(1)} %get-tuple-element.63), channel_id=1, source_target_pairs={{0,64},{32,96},{64,128},{96,160},{128,192},{160,224},{192,0},{224,... | collective-permute-start | bytes 55304 | tf_op jit(solution)/shard_map/ppermute | solution.py:423
  99.6 20.8 %collective-permute-start.18 = (bf16[96,96]{0,1:T(8,128)(2,1)S(1)}, bf16[96,96]{0,1:T(8,128)(2,1)S(1)}, u32[]{:S(2)}, u32[]{:S(2)}) collective-permute-start(bf16[96,96]{0,1:T(8,128)(2,1)S(1)} %get-tuple-element.62), channel_id=1, source_target_pairs={{0,96},{32,128},{64,160},{96,192},{128,224},{160,0},{192,32},{224,... | collective-permute-start | bytes 55304 | tf_op jit(solution)/shard_map/ppermute | solution.py:423
  103.6 16.8 %collective-permute-start.19 = (bf16[96,96]{0,1:T(8,128)(2,1)S(1)}, bf16[96,96]{0,1:T(8,128)(2,1)S(1)}, u32[]{:S(2)}, u32[]{:S(2)}) collective-permute-start(bf16[96,96]{0,1:T(8,128)(2,1)S(1)} %get-tuple-element.61), channel_id=1, source_target_pairs={{0,128},{32,160},{64,192},{96,224},{128,0},{160,32},{192,64},{224,... | collective-permute-start | bytes 55304 | tf_op jit(solution)/shard_map/ppermute | solution.py:423
  104.1 16.2 %collective-permute-start.20 = (bf16[96,96]{0,1:T(8,128)(2,1)S(1)}, bf16[96,96]{0,1:T(8,128)(2,1)S(1)}, u32[]{:S(2)}, u32[]{:S(2)}) collective-permute-start(bf16[96,96]{0,1:T(8,128)(2,1)S(1)} %get-tuple-element.60), channel_id=1, source_target_pairs={{0,160},{32,192},{64,224},{96,0},{128,32},{160,64},{192,96},{224,1... | collective-permute-start | bytes 55304 | tf_op jit(solution)/shard_map/ppermute | solution.py:423
  109.1 11.3 %collective-permute-start.21 = (bf16[96,96]{0,1:T(8,128)(2,1)S(1)}, bf16[96,96]{0,1:T(8,128)(2,1)S(1)}, u32[]{:S(2)}, u32[]{:S(2)}) collective-permute-start(bf16[96,96]{0,1:T(8,128)(2,1)S(1)} %get-tuple-element.59), channel_id=1, source_target_pairs={{0,192},{32,224},{64,0},{96,32},{128,64},{160,96},{192,128},{224,1... | collective-permute-start | bytes 55304 | tf_op jit(solution)/shard_map/ppermute | solution.py:423
  111.8 8.6 %collective-permute-start.22 = (bf16[96,96]{0,1:T(8,128)(2,1)S(1)}, bf16[96,96]{0,1:T(8,128)(2,1)S(1)}, u32[]{:S(2)}, u32[]{:S(2)}) collective-permute-start(bf16[96,96]{0,1:T(8,128)(2,1)S(1)} %get-tuple-element.64), channel_id=1, source_target_pairs={{0,224},{32,0},{64,32},{96,64},{128,96},{160,128},{192,160},{224,1... | collective-permute-start | bytes 55304 | tf_op jit(solution)/shard_map/ppermute | solution.py:423
  112.8 1.3 %copy-start.3 = (bf16[768,768]{1,0:T(8,128)(2,1)S(1)}, bf16[768,768]{1,0:T(8,128)(2,1)}, u32[]{:S(2)}) copy-start(bf16[768,768]{1,0:T(8,128)(2,1)} %w_out_ref.3) | copy-start | bytes 3538948
  114.0 0.9 copy-start.6
  115.0 1.1 copy-start.8
  116.0 1.0 copy-start.10
  117.0 0.8 copy-start.22

commit v2 on v1

--- a/solution.py
+++ b/solution.py
@@ -1,5 +1,3 @@
-import functools
-
 import jax
 import jax.numpy as jnp
 from jax import lax
@@ -25,7 +23,8 @@
 F32 = jnp.float32
 VMEM = pl.BlockSpec(memory_space=pltpu.VMEM)
 SMEM = pl.BlockSpec(memory_space=pltpu.SMEM)
-LIMIT = 40 * 1024 * 1024
+ANY = pl.BlockSpec(memory_space=pl.ANY)
+LIMIT = 20 * 1024 * 1024
 
 
 def iota(shape, dim):
@@ -119,15 +118,16 @@
 
 
 def first_kernel(
-    length_ref, tok_ref, coord_ref, cot_ref, w_qkv_ref, w_out_ref,
-    message_ref, packed_ref, g_ref, xhat_ref, rstd_ref, normed_ref, grad_ref, blocks_ref,
+    length_ref, coord_ref, tok_ref, w_qkv_ref, cot_ref, w_out_ref,
+    message_ref, packed_ref, g_ref, xhat_ref, rstd_ref, normed_ref, blocks_ref,
 ):
     length = length_ref[0]
     base = seg_index() * ROWS
     order = regroup()
+    coords = mm_nt(order, coord_ref[0].astype(F32).astype(BF))
+    code = sin_cos_code(coords[:, 0:1], coords[:, 1:2])
     tokens = mm(order, tok_ref[0])
-    coords = mm(order, coord_ref[0].astype(F32).astype(BF))
-    embedded = tokens + sin_cos_code(coords[:, 0:1], coords[:, 1:2])
+    embedded = tokens + code
     centred = embedded - jnp.mean(embedded, axis=-1, keepdims=True)
     rstd = lax.rsqrt(jnp.mean(centred * centred, axis=-1, keepdims=True) + EPSILON)
     xhat = centred * rstd
@@ -139,7 +139,6 @@
     packed_ref[...] = packed
     live = (base + place_of(iota((ROWS, 1), 0))) < length
     out_grad = jnp.where(live, mm(order, cot_ref[0]), 0.0).astype(BF)
-    grad_ref[...] = out_grad
     g = mm_nt(out_grad, w_out_ref[...]).astype(BF)
     g_ref[...] = g
 
@@ -188,21 +187,20 @@
     zero = jnp.zeros((ROWS, 72), F32)
     wide = out_grad.astype(F32)
     for b in range(16):
-        z_hi, xl, z_lo = b // 8, (b // 4) % 2, b % 4
+        xl, z = b // 8, b % 8
         for c in range(2):
-            dp = (z_hi * 4 + z_lo) * 4 + xl * 2 + c
+            dp = z * 4 + xl * 2 + c
             rel = (core + c) % 2
             block = jnp.concatenate([zero, wide[:, 24 * dp : 24 * dp + 24]], axis=1)
             blocks_ref[rel, :, BLOCK * b : BLOCK * (b + 1)] = block.astype(BF)
 
 
 def dense_kernel(
-    length_ref, packed_ref, g_ref, out_ref, back_ref, weight_ref, dweight_ref, sampled_out_ref
+    length_ref, packed_ref, g_ref, out_ref, back_ref, weight_ref, dweight_ref
 ):
     length = length_ref[0]
     base = seg_index() * ROWS
     mask = head_mask(ROWS)
-    small = head_mask(SLAB)
     row = iota((GROUP * ROWS, 1), 0)
     key_col = place_of(iota((1, ROWS), 1))
     query_col = place_of(row % ROWS)
@@ -240,7 +238,6 @@
             to = slice(SLAB * h, SLAB * (h + 1))
             weight_ref[group, to] = p[at : at + SLAB]
             dweight_ref[group, to] = dp[at : at + SLAB]
-            sampled_out_ref[group, to] = jnp.where(small[to], out[at : at + SLAB], 0.0)
 
 
 def dilated_kernel(length_ref, message_ref, reply_ref):
@@ -302,7 +299,7 @@
 
 
 def join_kernel(
-    reply_ref, packed_ref, g_ref, out_ref, back_ref, weight_ref, dweight_ref, sampled_out_ref,
+    reply_ref, packed_ref, g_ref, weight_ref, dweight_ref, back_ref, out_ref,
     blended_ref, packed_grad_ref, blocks_ref,
 ):
     small = head_mask(SLAB)
@@ -335,9 +332,10 @@
         parts[0].append(back_ref[0, :, lanes] + unstack_slabs(jnp.where(small, mm(ds, k), 0.0)))
         parts[1].append(back_ref[1, :, lanes] + mm_tn(ds, q))
         parts[2].append(back_ref[2, :, lanes] + mm_tn(p.astype(BF), gm))
-        parts[3].append(unstack_slabs(sampled_out_ref[group] * share))
+        parts[3].append(unstack_slabs(jnp.where(small, share, 0.0)))
     whole = [jnp.concatenate(part, axis=1) for part in parts]
-    blended_ref[...] = jnp.where(sampled, whole[3] + placed(3), out_ref[...]).astype(BF)
+    out = out_ref[...]
+    blended_ref[...] = jnp.where(sampled, whole[3] * out + placed(3), out).astype(BF)
     grads = []
     for a in range(3):
         grad = (whole[a] + placed(a)).astype(BF)
@@ -347,17 +345,17 @@
     core = lax.axis_index("core")
     zero = jnp.zeros((ROWS, 24), F32)
     for b in range(16):
-        z_hi, xl, z_lo = b // 8, (b // 4) % 2, b % 4
+        xl, z = b // 8, b % 8
         for c in range(2):
-            dp = (z_hi * 4 + z_lo) * 4 + xl * 2 + c
+            dp = z * 4 + xl * 2 + c
             rel = (core + c) % 2
             block = jnp.concatenate([grads[:, 72 * dp : 72 * dp + 72], zero], axis=1)
             blocks_ref[rel, :, BLOCK * b : BLOCK * (b + 1)] = block.astype(BF)
 
 
 def finish_kernel(
-    length_ref, blended_ref, packed_grad_ref, xhat_ref, rstd_ref, w_qkv_ref, w_out_ref,
-    layer_ref, token_grad_ref,
+    length_ref, blended_ref, w_out_ref, packed_grad_ref, w_qkv_ref, xhat_ref, rstd_ref,
+    layer_ref, token_grad_ref, done_ref,
 ):
     length = length_ref[0]
     base = seg_index() * ROWS
@@ -371,64 +369,119 @@
     slope = jnp.mean(dn * xhat, axis=-1, keepdims=True)
     dx = ((dn - mean - xhat * slope) * rstd_ref[:, 0:1]).astype(BF)
     token_grad_ref[0] = mm_tn(order, dx).astype(BF)
-
-
-def weight_kernel(
-    n0_ref, n1_ref, b0_ref, b1_ref, p0_ref, p1_ref, g0_ref, g1_ref, along_y_ref, along_x_ref
-):
+    done_ref[...] = jnp.zeros(done_ref.shape, F32)
+
+
+def weight_kernel(n0_ref, n1_ref, b0_ref, b1_ref, p0_ref, p1_ref, g0_ref, g1_ref, out_ref):
     xh, xl, y = lax.axis_index("xh"), lax.axis_index("xl"), lax.axis_index("y")
+    core = lax.axis_index("core")
     left = jnp.concatenate([n0_ref[...], n1_ref[...], b0_ref[...], b1_ref[...]], axis=0)
     for part in range(4):
-        z_hi, to_xl = part // 2, part % 2
+        to_xl, half = part // 2, part % 2
         lanes = slice(part * WIDE, (part + 1) * WIDE)
         right = jnp.concatenate(
             [p0_ref[:, lanes], p1_ref[:, lanes], g0_ref[:, lanes], g1_ref[:, lanes]], axis=0
         )
         total = mm_tn(left, right).astype(BF)
-        xl_rel = (to_xl + xl) % 2
         for s in range(N_SEG):
-            xh_rel = (s // 4 + xh) % 2
+            x_rel = 2 * ((to_xl + xl) % 2) + (s // 4 + xh) % 2
             y_rel = (s % 4 - y + 4) % 4
-            chunk = total[BLOCK * s : BLOCK * (s + 1)]
-            if z_hi == 0:
-                along_y_ref[y_rel, xh_rel, xl_rel] = chunk
-            else:
-                along_x_ref[xh_rel, xl_rel, y_rel] = chunk
-
-
-def call(kernel, outs, specs, *args):
+            first = jnp.where(core == 0, y_rel, x_rel)
+            second = jnp.where(core == 0, x_rel, y_rel)
+            out_ref[first, second, :, half * WIDE : (half + 1) * WIDE] = total[
+                BLOCK * s : BLOCK * (s + 1)
+            ]
+
+
+def first_sum_kernel(own_ref, a_ref, b_ref, c_ref, out_ref):
+    for k in range(4):
+        total = own_ref[0, k].astype(F32) + a_ref[k].astype(F32)
+        total = total + (b_ref[k].astype(F32) + c_ref[k].astype(F32))
+        out_ref[k] = total.astype(BF)
+
+
+def second_sum_kernel(own_ref, a_ref, b_ref, c_ref, out_ref):
+    total = own_ref[0].astype(F32) + a_ref[...].astype(F32)
+    total = total + (b_ref[...].astype(F32) + c_ref[...].astype(F32))
+    for z in range(8):
+        out_ref[z] = total[:, BLOCK * z : BLOCK * (z + 1)].astype(BF)
+
+
+def last_sum_kernel(parts_ref, in_ref, out_ref):
+    total = parts_ref[0].astype(F32)
+    for z in range(1, 8):
+        total = total + parts_ref[z].astype(F32)
+    total = total.T
+    in_ref[...] = total[:72]
+    out_ref[...] = total[72:]
+
+
+class Held:
+    def __init__(self, source, target, sem):
+        self.target = target
+        self.copy = pltpu.make_async_copy(source, target, sem)
+        self.copy.start()
+        self.here = False
+
+    def __getitem__(self, index):
+        if not self.here:
+            self.copy.wait()
+            self.here = True
+        return self.target[index]
+
+
+def call(kernel, outs, *inputs):
+    specs = {"s": SMEM, "v": VMEM, "f": ANY, "h": ANY, "n": ANY}
+    kinds = [kind for kind, _ in inputs]
+    arrays = [
+        pltpu.with_memory_space_constraint(x, pltpu.HBM) if kind == "h" else x
+        for kind, x in inputs
+    ]
+    fetched = [x for kind, x in inputs if kind in "fh"]
+
+    def body(*refs):
+        n, m = len(kinds), len(outs)
+        slots = list(refs[n + m : -1]) if fetched else []
+        given = []
+        for kind, ref in zip(kinds, refs[:n]):
+            if kind in "fh":
+                given.append(Held(ref, slots.pop(0), refs[-1].at[len(slots)]))
+            elif kind != "n":
+                given.append(ref)
+        kernel(*given, *refs[n : n + m])
+
+    scratch = [pltpu.VMEM(x.shape, x.dtype) for x in fetched]
+    if fetched:
+        scratch.append(pltpu.SemaphoreType.DMA((len(fetched),)))
     return pl.pallas_call(
-        kernel,
+        body,
         out_shape=[jax.ShapeDtypeStruct(shape, dtype) for shape, dtype in outs],
-        in_specs=specs,
+        in_specs=[specs[kind] for kind in kinds],
         out_specs=[VMEM] * len(outs),
+        scratch_shapes=scratch,
         compiler_params=pltpu.CompilerParams(vmem_limit_bytes=LIMIT),
-    )(*args)
+        name=kernel.__name__,
+    )(*arrays)
 
 
 def to_core(x):
     return lax.ppermute(x, "core", [(0, 1), (1, 0)])
 
 
-def along_y(x, k):
-    return lax.ppermute(x, "y", [(i, (i + k) % 4) for i in range(4)])
-
-
-def along_x(x, xh_rel, xl_rel):
-    pairs = [(i, i ^ (2 * xl_rel + xh_rel)) for i in range(4)]
-    return lax.ppermute(x, ("xl", "xh"), pairs)
-
-
-def along_z(x, k):
-    return lax.ppermute(x, "z", [(i, (i + k) % 8) for i in range(8)])
-
-
-def add_up(parts):
-    return sum(part.astype(F32) for part in parts)
+def swap(x, k, stage):
+    pairs = []
+    for i in range(32):
+        xl, core, xh, y = i // 16, (i // 8) % 2, (i // 4) % 2, i % 4
+        if core == stage:
+            y = (y + k) % 4
+        else:
+            xl, xh = xl ^ (k // 2), xh ^ (k % 2)
+        pairs.append((i, ((xl * 2 + core) * 2 + xh) * 4 + y))
+    return lax.ppermute(x, ("xl", "core", "xh", "y"), pairs)
 
 
 def per_device(tokens, coords, lengths, w_qkv, w_out, cotangent):
-    message, packed, g, xhat, rstd, normed, out_grad, grad_blocks = call(
+    message, packed, g, xhat, rstd, normed, grad_blocks = call(
         first_kernel,
         [
             ((N_SEG, 4, SLAB, 128), BF),
@@ -437,63 +490,96 @@
             ((ROWS, D), F32),
             ((ROWS, 128), F32),
             ((ROWS, D), BF),
-            ((ROWS, D), BF),
             ((2, ROWS, 16 * BLOCK), BF),
         ],
-        [SMEM] + [VMEM] * 5,
-        lengths, tokens, coords, cotangent, w_qkv, w_out,
+        ("s", lengths),
+        ("h", jnp.transpose(coords, (0, 2, 1))),
+        ("h", tokens),
+        ("h", w_qkv),
+        ("h", cotangent),
+        ("h", w_out),
     )
     message = lax.all_to_all(message, ("xh", "y"), 0, 0, tiled=True)
     other_normed = to_core(normed)
     other_grad = to_core(grad_blocks[1])
-    out, back, weight, dweight, sampled_out = call(
+    out, back, weight, dweight = call(
         dense_kernel,
         [
             ((ROWS, D), F32),
             ((3, ROWS, D), F32),
             ((2, GROUP * SLAB, ROWS), F32),
             ((2, GROUP * SLAB, ROWS), F32),
-            ((2, GROUP * SLAB, WIDE), F32),
         ],
-        [SMEM] + [VMEM] * 2,
-        lengths, packed, g,
+        ("s", lengths),
+        ("v", packed),
+        ("v", g),
     )
     (reply,) = call(
-        dilated_kernel, [((N_SEG, 4, SLAB, 128), BF)], [SMEM, VMEM], lengths, message
+        dilated_kernel,
+        [((N_SEG, 4, SLAB, 128), BF)],
+        ("s", lengths),
+        ("v", message),
+        ("n", dweight),
+        ("n", other_normed),
+        ("n", other_grad),
     )
     reply = lax.all_to_all(reply, ("xh", "y"), 0, 0, tiled=True)
     blended, packed_grad, blocks = call(
         join_kernel,
         [((ROWS, D), BF), ((ROWS, 3 * D), BF), ((2, ROWS, 16 * BLOCK), BF)],
-        [VMEM] * 8,
-        reply, packed, g, out, back, weight, dweight, sampled_out,
+        ("v", reply),
+        ("v", packed),
+        ("v", g),
+        ("h", weight),
+        ("v", dweight),
+        ("v", back),
+        ("h", out),
     )
     other_blended = to_core(blended)
     other_blocks = to_core(blocks[1])
-    first, second = call(
+    (partial,) = call(
         weight_kernel,
-        [((4, 2, 2, BLOCK, WIDE), BF), ((2, 2, 4, BLOCK, WIDE), BF)],
-        [VMEM] * 8,
-        normed, other_normed, blended, other_blended,
-        blocks[0], other_blocks, grad_blocks[0], other_grad,
-    )
-    layer_out, token_grad = call(
+        [((4, 4, BLOCK, D), BF)],
+        ("f", normed),
+        ("f", other_normed),
+        ("v", blended),
+        ("v", other_blended),
+        ("v", blocks[0]),
+        ("v", other_blocks),
+        ("f", grad_blocks[0]),
+        ("f", other_grad),
+    )
+    layer_out, token_grad, done = call(
         finish_kernel,
-        [((1, ROWS, D), BF), ((1, ROWS, D), BF)],
-        [SMEM] + [VMEM] * 6,
-        lengths, blended, packed_grad, xhat, rstd, w_qkv, w_out,
-    )
-    near = [(0, 1), (1, 0), (1, 1)]
-    first = add_up([first[0]] + [along_y(first[k], k) for k in (1, 3, 2)]).astype(BF)
-    second = add_up([second[0, 0]] + [along_x(second[a, b], a, b) for a, b in near]).astype(BF)
-    first = add_up([first[0, 0]] + [along_x(first[a, b], a, b) for a, b in near]).astype(BF)
-    second = add_up([second[0]] + [along_y(second[k], k) for k in (1, 3, 2)]).astype(BF)
-    both = jnp.concatenate([first, second], axis=1)
-    both = both.reshape(BLOCK, 8, BLOCK).transpose(1, 0, 2)
-    z = lax.axis_index("z")
-    both = jnp.roll(both, -z, axis=0)
-    total = add_up([both[0]] + [along_z(both[k], k) for k in range(1, 8)])
-    return layer_out, token_grad, total[:, :72], total[:, 72:]
+        [((1, ROWS, D), BF), ((1, ROWS, D), BF), ((8, 128), F32)],
+        ("s", lengths),
+        ("f", blended),
+        ("h", w_out),
+        ("f", packed_grad),
+        ("h", w_qkv),
+        ("h", xhat),
+        ("h", rstd),
+    )
+    arrived = [swap(partial[k], k, 0) for k in (1, 2, 3)]
+    (partial,) = call(
+        first_sum_kernel,
+        [((4, BLOCK, D), BF)],
+        ("v", partial),
+        *[("v", x) for x in arrived],
+        ("n", done),
+    )
+    arrived = [swap(partial[k], k, 1) for k in (1, 2, 3)]
+    (partial,) = call(
+        second_sum_kernel,
+        [((8, BLOCK, BLOCK), BF)],
+        ("v", partial),
+        *[("v", x) for x in arrived],
+    )
+    arrived = lax.all_to_all(partial, "z", 0, 0, tiled=True)
+    grad_in, grad_out = call(
+        last_sum_kernel, [((72, BLOCK), F32), ((24, BLOCK), F32)], ("v", arrived)
+    )
+    return layer_out, token_grad, grad_in.T, grad_out.T
 
 
 def solution(mesh):

time: 124 us -> 94.4 us (0.76); the launches traced: 122 us -> 93.4 us
  starting transfers between devices: 50.7 us -> 15.8 us
  local copies, waits for them, and re-layouts: 21.9 us -> 2.58 us
  blocking collectives: 13 us -> 29.9 us
  Pallas kernels: 17.9 us -> 24.8 us
  waiting for transfers between devices: 12.2 us -> 18.9 us
  other arithmetic: 4.38 us -> 0 us
    ppermute x19 -> x6, starting transfers between devices: 43.3 us -> 7.77 us  [swap(): return lax.ppermute(x, ('xl', 'core', 'xh', 'y'), pairs)]
    all_to_all x1 -> x2, blocking collectives: 13 us -> 29.9 us  [the longest x1 18 us: per_device(): arrived = lax.all_to_all(partial, 'z', 0, 0, tiled=True)]
    unnamed x47 -> x8, local copies, waits for them, and re-layouts: 17.9 us -> 1.48 us
    pallas_call x6 -> x9, Pallas kernels: 17.9 us -> 24.8 us  [call(): pl.pallas_call(body, out_shape=[jax.ShapeDtypeStruct(shape, dtype) for sh...]
    ppermute x19 -> x6, waiting for transfers between devices: 10.8 us -> 15.8 us  [swap(): return lax.ppermute(x, ('xl', 'core', 'xh', 'y'), pairs)]
    convert_element_type x4 -> x0, other arithmetic: 2.64 us -> none  [the longest x1 1.29 us: per_device(): add_up([first[0]] + [along_y(first[k], k) for k in (1, 3, 2)]).astype(BF)]
    reshape x1 -> x0, local copies, waits for them, and re-layouts: 1.72 us -> none  [per_device(): both = both.reshape(BLOCK, 8, BLOCK).transpose(1, 0, 2)]
    concatenate x2 -> x0, other arithmetic: 1.71 us -> none  [the longest x1 1.03 us: per_device(): both = jnp.roll(both, -z, axis=0)]
  transfers between devices with their start and end apart: 24 -> 11, of which waited for: 6 -> 8; matrix products, arithmetic and copies ran while one was open for 3% -> 0% of each run, Pallas kernels for 7% -> 9%
where the time goes in v2:
time: 94.4 us; the launch traced here: 93.4 us
  blocking collectives  29.9 us (32%)
  Pallas kernels  24.8 us (26%)
  waiting for transfers between devices  18.9 us (20%)
  starting transfers between devices  15.8 us (17%)
  local copies, waits for them, and re-layouts  2.58 us (3%)
  between operations  1.4 us (1%)
    pallas_call x9, Pallas kernels, call(): pl.pallas_call(body, out_shape=[jax.ShapeDtypeStruct(shape, dtype) for sh...  24.8 us
    all_to_all x1, blocking collectives, per_device(): arrived = lax.all_to_all(partial, 'z', 0, 0, tiled=True)  18 us
    ppermute x6, waiting for transfers between devices, swap(): return lax.ppermute(x, ('xl', 'core', 'xh', 'y'), pairs)  15.8 us
    all_to_all x1, blocking collectives, per_device(): reply = lax.all_to_all(reply, ('xh', 'y'), 0, 0, tiled=True)  11.9 us
    ppermute x6, starting transfers between devices, swap(): return lax.ppermute(x, ('xl', 'core', 'xh', 'y'), pairs)  7.77 us
    all_to_all x1, starting transfers between devices, per_device(): message = lax.all_to_all(message, ('xh', 'y'), 0, 0, tiled=True)  7.45 us
  transfers between devices with their start and end apart: 11, of which 8 were waited for; matrix products, arithmetic and copies ran while one was open for 0% of the time, Pallas kernels for 9%

profile of v2, /device:TPU:6, one launch (start us, length us, event | category | flops | bytes accessed | tf_op | source)
XLA Modules:
  0.0 93.4 jit_solution(10638023507309599553)
XLA Ops:
  1.3 6.6 %first_kernel.1 = (bf16[8,4,32,128]{3,2,1,0:T(8,128)(2,1)}, bf16[128,2304]{1,0:T(8,128)(2,1)S(1)}, bf16[128,768]{1,0:T(8,128)(2,1)S(1)}, f32[128,768]{1,0:T(8,12...) custom-call(s32[1]{0:T(128)S(6)} %copy.10.refs_0_, ...), custom_call_target="tpu_custom_call" | custom-call | tf_op jit(solution)/shard_map/first_kernel/pallas_call | solution.py:456
  7.9 0.0 copy-start
  7.9 0.0 copy-start.3
  7.9 0.9 slice_bitcast_fusion.3
  8.8 0.0 copy-done
  8.8 0.0 copy-done.3
  8.8 0.0 collective-permute-start.1
  8.8 7.4 %all-to-all-start = ((bf16[8,4,32,128]{3,2,1,0:T(8,128)(2,1)}), bf16[8,4,32,128]{3,2,1,0:T(8,128)(2,1)S(1)}, u32[]{:S(2)}, u32[]{:S(2)}) async-start(bf16[8,4,32,128]{3,2,1,0:T(8,128)(2,1)} %get-tuple-element.23), calls=%async_computation | async-start | bytes 524288 | tf_op jit(solution)/shard_map/all_to_all | solution.py:502
  16.3 0.0 collective-permute-start
  16.3 3.4 %dense_kernel.1 = (f32[128,768]{1,0:T(8,128)S(1)}, f32[3,128,768]{2,1,0:T(8,128)S(1)}, f32[2,256,128]{2,1,0:T(8,128)S(1)}, f32[2,256,128]{2,1,0:T(8,128)S(1)}) custom-call(s32[1]{0:T(128)S(6)} %copy.10.refs_0_, bf16[128,2304]{1,0:T(8,128)(2,1)S(1)} %get-tuple-element.24.refs_1_, bf16[128,768]{1,0:T(8,128)(2,1)S(1)} %get-tuple-element.25.refs_2_), custom_call_target="tpu_custom_call" | custom-call | tf_op jit(solution)/shard_map/dense_kernel/pallas_call | solution.py:456
  19.7 0.0 copy-start.1
  19.7 0.8 copy-done.1
  20.4 0.0 copy-start.2
  20.4 0.7 copy-done.2
  21.1 0.0 collective-permute-done.refs_3_.refs_1_
  21.1 1.6 %all-to-all-done.refs_1_ = bf16[8,4,32,128]{3,2,1,0:T(8,128)(2,1)S(1)} async-done(((bf16[8,4,32,128]{3,2,1,0:T(8,128)(2,1)}), bf16[8,4,32,128]{3,2,1,0:T(8,128)(2,1)S(1)}, u32[]{:S(2)}, u32[]{:S(2)}) %all-to-all-start) | async-done | bytes 262176 | tf_op jit(solution)/shard_map/all_to_all | solution.py:502
  22.7 0.0 collective-permute-done.1.refs_4_.refs_7_
  22.8 1.6 %dilated_kernel.1 = bf16[8,4,32,128]{3,2,1,0:T(8,128)(2,1)S(1)} custom-call(s32[1]{0:T(128)S(6)} %copy.10.refs_0_, bf16[8,4,32,128]{3,2,1,0:T(8,128)(2,1)S(1)} %all-to-all-done.refs_1_, f32[2,256,128]{2,1,0:T(8,128)S(1)} %get-tuple-element.26.refs_2_.refs_4_, bf16[128,768]{1,0:T(8,128)(2,1)S(1)} %collective-permute-done.refs_3_.refs_1_, ...), custom_call_target="tpu_custom_call" | custom-call | tf_op jit(solution)/shard_map/dilated_kernel/pallas_call | solution.py:456
  24.3 11.9 %all_to_all.15.refs_0_ = bf16[8,4,32,128]{3,2,1,0:T(8,128)(2,1)S(1)} all-to-all(bf16[8,4,32,128]{3,2,1,0:T(8,128)(2,1)S(1)} %dilated_kernel.1), channel_id=1, replica_groups=mesh['z'=8,'xl'=2,'core'=2,'xh'=2,'y'=4] {'xh','y'}, dimensions={0} | all-to-all | bytes 524288 | tf_op jit(solution)/shard_map/all_to_all | solution.py:526
  36.2 4.0 %join_kernel.1 = (bf16[128,768]{1,0:T(8,128)(2,1)S(1)}, bf16[128,2304]{1,0:T(8,128)(2,1)S(1)}, bf16[2,128,1536]{2,1,0:T(8,128)(2,1)S(1)}) custom-call(bf16[8,4,32,128]{3,2,1,0:T(8,128)(2,1)S(1)} %all_to_all.15.refs_0_, bf16[128,2304]{1,0:T(8,128)(2,1)S(1)} %get-tuple-element.24.refs_1_, bf16[128,768]{1,0:T(8,128)(2,1)S(1)} %get-tuple-element.25.refs_2_, ...), custom_call_target="tpu_custom_call" | custom-call | tf_op jit(solution)/shard_map/join_kernel/pallas_call | solution.py:456
  40.3 0.1 slice_bitcast_fusion.4
  40.3 0.1 collective-permute-start.3
  40.4 0.5 collective-permute-start.2
  40.9 1.5 %collective-permute-done.2.refs_3_ = bf16[128,768]{1,0:T(8,128)(2,1)S(1)} collective-permute-done((bf16[128,768]{1,0:T(8,128)(2,1)S(1)}, bf16[128,768]{1,0:T(8,128)(2,1)S(1)}, u32[]{:S(2)}, u32[]{:S(2)}) %collective-permute-start.2) | collective-permute-done | bytes 196640 | tf_op jit(solution)/shard_map/ppermute | solution.py:468
  42.4 0.0 collective-permute-done.3.refs_5_
  42.4 2.9 %weight_kernel.1.refs_0_ = bf16[4,4,96,768]{3,2,1,0:T(8,128)(2,1)S(1)} custom-call(bf16[128,768]{1,0:T(8,128)(2,1)} %get-tuple-element.27.refs_0_, bf16[128,768]{1,0:T(8,128)(2,1)S(1)} %collective-permute-done.refs_3_.refs_1_, bf16[128,768]{1,0:T(8,128)(2,1)S(1)} %get-tuple-element.32.refs_1_.refs_2_, bf16[128,768]{1,0:T(8,128)(2,1)S(1)} %collective-permute-done.2.refs_3_, ...), custom_call_target="tpu_custom_call" | custom-call | tf_op jit(solution)/shard_map/weight_kernel/pallas_call | solution.py:456
  45.3 0.1 slice_bitcast_fusion
  45.4 1.5 %collective-permute-start.6 = (bf16[4,96,768]{2,1,0:T(8,128)(2,1)S(1)}, bf16[4,96,768]{2,1,0:T(8,128)(2,1)S(1)}, u32[]{:S(2)}, u32[]{:S(2)}) collective-permute-start(bf16[4,96,768]{2,1,0:T(8,128)(2,1)S(1)} %get-tuple-element.42), channel_id=1, source_target_pairs={{0,3},{1,0},{2,1},{3,2},{4,7},{5,4},{6,5},{7,6},{8,28},{9,29},{10,... | collective-permute-start | bytes 1769480 | tf_op jit(solution)/shard_map/ppermute | solution.py:480
  47.0 1.5 %collective-permute-start.5 = (bf16[4,96,768]{2,1,0:T(8,128)(2,1)S(1)}, bf16[4,96,768]{2,1,0:T(8,128)(2,1)S(1)}, u32[]{:S(2)}, u32[]{:S(2)}) collective-permute-start(bf16[4,96,768]{2,1,0:T(8,128)(2,1)S(1)} %get-tuple-element.43), channel_id=1, source_target_pairs={{0,2},{1,3},{2,0},{3,1},{4,6},{5,7},{6,4},{7,5},{8,24},{9,25},{10,... | collective-permute-start | bytes 1769480 | tf_op jit(solution)/shard_map/ppermute | solution.py:480
  48.4 0.0 collective-permute-start.4
  48.4 5.1 %finish_kernel.1 = (bf16[1,128,768]{2,1,0:T(8,128)(2,1)}, bf16[1,128,768]{2,1,0:T(8,128)(2,1)}, f32[8,128]{1,0:T(8,128)S(1)}) custom-call(s32[1]{0:T(128)S(6)} %copy.10.refs_0_, bf16[128,768]{1,0:T(8,128)(2,1)S(1)} %get-tuple-element.32.refs_1_.refs_2_, bf16[768,768]{1,0:T(8,128)(2,1)} %refs_2_.3, bf16[128,2304]{1,0:T(8,128)(2,1)S(1)} %get-tuple-element.33.refs_3_, ...), custom_call_target="tpu_custom_call" | custom-call | tf_op jit(solution)/shard_map/finish_kernel/pallas_call | solution.py:456
  53.6 1.8 %collective-permute-done.6.refs_3_ = bf16[4,96,768]{2,1,0:T(8,128)(2,1)S(1)} collective-permute-done((bf16[4,96,768]{2,1,0:T(8,128)(2,1)S(1)}, bf16[4,96,768]{2,1,0:T(8,128)(2,1)S(1)}, u32[]{:S(2)}, u32[]{:S(2)}) %collective-permute-start.6) | collective-permute-done | bytes 589856 | tf_op jit(solution)/shard_map/ppermute | solution.py:480
  55.4 3.1 %collective-permute-done.5.refs_2_ = bf16[4,96,768]{2,1,0:T(8,128)(2,1)S(1)} collective-permute-done((bf16[4,96,768]{2,1,0:T(8,128)(2,1)S(1)}, bf16[4,96,768]{2,1,0:T(8,128)(2,1)S(1)}, u32[]{:S(2)}, u32[]{:S(2)}) %collective-permute-start.5) | collective-permute-done | bytes 589856 | tf_op jit(solution)/shard_map/ppermute | solution.py:480
  58.5 6.2 %collective-permute-done.4.refs_1_ = bf16[4,96,768]{2,1,0:T(8,128)(2,1)S(1)} collective-permute-done((bf16[4,96,768]{2,1,0:T(8,128)(2,1)S(1)}, bf16[4,96,768]{2,1,0:T(8,128)(2,1)S(1)}, u32[]{:S(2)}, u32[]{:S(2)}) %collective-permute-start.4) | collective-permute-done | bytes 589856 | tf_op jit(solution)/shard_map/ppermute | solution.py:480
  64.7 0.3 first_sum_kernel.1.refs_0_
  65.0 2.3 %collective-permute-start.9 = (bf16[96,768]{1,0:T(8,128)(2,1)S(1)}, bf16[96,768]{1,0:T(8,128)(2,1)S(1)}, u32[]{:S(2)}, u32[]{:S(2)}) collective-permute-start(bf16[96,768]{1,0:T(8,128)(2,1)S(1)} %get-tuple-element.49), channel_id=1, source_target_pairs={{0,20},{1,21},{2,22},{3,23},{4,16},{5,17},{6,18},{7,19},{8,11},{9,... | collective-permute-start | bytes 442376 | tf_op jit(solution)/shard_map/ppermute | solution.py:480
  67.3 0.0 collective-permute-start.8
  67.3 2.5 %collective-permute-start.7 = (bf16[96,768]{1,0:T(8,128)(2,1)S(1)}, bf16[96,768]{1,0:T(8,128)(2,1)S(1)}, u32[]{:S(2)}, u32[]{:S(2)}) collective-permute-start(bf16[96,768]{1,0:T(8,128)(2,1)S(1)} %get-tuple-element.51), channel_id=1, source_target_pairs={{0,4},{1,5},{2,6},{3,7},{4,0},{5,1},{6,2},{7,3},{8,9},{9,10},{10,1... | collective-permute-start | bytes 442376 | tf_op jit(solution)/shard_map/ppermute | solution.py:480
  69.8 1.7 %collective-permute-done.9.refs_3_ = bf16[96,768]{1,0:T(8,128)(2,1)S(1)} collective-permute-done((bf16[96,768]{1,0:T(8,128)(2,1)S(1)}, bf16[96,768]{1,0:T(8,128)(2,1)S(1)}, u32[]{:S(2)}, u32[]{:S(2)}) %collective-permute-start.9) | collective-permute-done | bytes 147488 | tf_op jit(solution)/shard_map/ppermute | solution.py:480
  71.4 1.0 %collective-permute-done.8.refs_2_ = bf16[96,768]{1,0:T(8,128)(2,1)S(1)} collective-permute-done((bf16[96,768]{1,0:T(8,128)(2,1)S(1)}, bf16[96,768]{1,0:T(8,128)(2,1)S(1)}, u32[]{:S(2)}, u32[]{:S(2)}) %collective-permute-start.8) | collective-permute-done | bytes 147488 | tf_op jit(solution)/shard_map/ppermute | solution.py:480
  72.4 2.0 %collective-permute-done.7.refs_1_ = bf16[96,768]{1,0:T(8,128)(2,1)S(1)} collective-permute-done((bf16[96,768]{1,0:T(8,128)(2,1)S(1)}, bf16[96,768]{1,0:T(8,128)(2,1)S(1)}, u32[]{:S(2)}, u32[]{:S(2)}) %collective-permute-start.7) | collective-permute-done | bytes 147488 | tf_op jit(solution)/shard_map/ppermute | solution.py:480
  74.5 0.2 second_sum_kernel.1
  74.6 18.0 %all_to_all.16.refs_0_ = bf16[8,96,96]{2,1,0:T(8,128)(2,1)S(1)} all-to-all(bf16[8,96,96]{2,1,0:T(8,128)(2,1)S(1)} %second_sum_kernel.1), channel_id=1, replica_groups=mesh['z'=8,'xl'=2,'core'=2,'xh'=2,'y'=4] {'z'}, dimensions={0} | all-to-all | bytes 294912 | tf_op jit(solution)/shard_map/all_to_all | solution.py:578
  92.7 0.7 last_sum_kernel.1
  (1 shorter events, 0.0 us)
Async XLA Ops:
  7.9 0.9 copy-start
  7.9 0.9 copy-start.3
  8.8 13.9 %collective-permute-start.1 = (bf16[128,1536]{1,0:T(8,128)(2,1)}, bf16[128,1536]{1,0:T(8,128)(2,1)S(1)}, u32[]{:S(2)}, u32[]{:S(2)}) collective-permute-start(bf16[128,1536]{1,0:T(8,128)(2,1)} %get-tuple-element.46), channel_id=1, source_target_pairs={{0,8},{8,0},{1,9},{9,1},{2,10},{10,2},{3,11},{11,3},{4,12},{12,4},... | collective-permute-start | bytes 1179656 | tf_op jit(solution)/shard_map/ppermute | solution.py:468
  8.8 13.9 %all-to-all-start = ((bf16[8,4,32,128]{3,2,1,0:T(8,128)(2,1)}), bf16[8,4,32,128]{3,2,1,0:T(8,128)(2,1)S(1)}, u32[]{:S(2)}, u32[]{:S(2)}) async-start(bf16[8,4,32,128]{3,2,1,0:T(8,128)(2,1)} %get-tuple-element.23), calls=%async_computation | async-start | bytes 524288 | tf_op jit(solution)/shard_map/all_to_all | solution.py:502
  16.3 4.9 %collective-permute-start = (bf16[128,768]{1,0:T(8,128)(2,1)}, bf16[128,768]{1,0:T(8,128)(2,1)S(1)}, u32[]{:S(2)}, u32[]{:S(2)}) collective-permute-start(bf16[128,768]{1,0:T(8,128)(2,1)} %get-tuple-element.27.refs_0_), channel_id=1, source_target_pairs={{0,8},{8,0},{1,9},{9,1},{2,10},{10,2},{3,11},{11,3},{4,12},{12,4},... | collective-permute-start | bytes 589832 | tf_op jit(solution)/shard_map/ppermute | solution.py:468
  19.7 0.8 copy-start.1
  20.4 0.7 copy-start.2
  40.3 2.1 %collective-permute-start.3 = (bf16[128,1536]{1,0:T(8,128)(2,1)S(1)}, bf16[128,1536]{1,0:T(8,128)(2,1)S(1)}, u32[]{:S(2)}, u32[]{:S(2)}) collective-permute-start(bf16[128,1536]{1,0:T(8,128)(2,1)S(1)} %get-tuple-element.47), channel_id=1, source_target_pairs={{0,8},{8,0},{1,9},{9,1},{2,10},{10,2},{3,11},{11,3},{4,12},{12,4},... | collective-permute-start | bytes 1179656 | tf_op jit(solution)/shard_map/ppermute | solution.py:468
  40.4 2.0 %collective-permute-start.2 = (bf16[128,768]{1,0:T(8,128)(2,1)S(1)}, bf16[128,768]{1,0:T(8,128)(2,1)S(1)}, u32[]{:S(2)}, u32[]{:S(2)}) collective-permute-start(bf16[128,768]{1,0:T(8,128)(2,1)S(1)} %get-tuple-element.32.refs_1_.refs_2_), channel_id=1, source_target_pairs={{0,8},{8,0},{1,9},{9,1},{2,10},{10,2},{3,11},{11,3},{4,12},{12,4},... | collective-permute-start | bytes 589832 | tf_op jit(solution)/shard_map/ppermute | solution.py:468
  45.4 10.0 %collective-permute-start.6 = (bf16[4,96,768]{2,1,0:T(8,128)(2,1)S(1)}, bf16[4,96,768]{2,1,0:T(8,128)(2,1)S(1)}, u32[]{:S(2)}, u32[]{:S(2)}) collective-permute-start(bf16[4,96,768]{2,1,0:T(8,128)(2,1)S(1)} %get-tuple-element.42), channel_id=1, source_target_pairs={{0,3},{1,0},{2,1},{3,2},{4,7},{5,4},{6,5},{7,6},{8,28},{9,29},{10,... | collective-permute-start | bytes 1769480 | tf_op jit(solution)/shard_map/ppermute | solution.py:480
  47.0 11.5 %collective-permute-start.5 = (bf16[4,96,768]{2,1,0:T(8,128)(2,1)S(1)}, bf16[4,96,768]{2,1,0:T(8,128)(2,1)S(1)}, u32[]{:S(2)}, u32[]{:S(2)}) collective-permute-start(bf16[4,96,768]{2,1,0:T(8,128)(2,1)S(1)} %get-tuple-element.43), channel_id=1, source_target_pairs={{0,2},{1,3},{2,0},{3,1},{4,6},{5,7},{6,4},{7,5},{8,24},{9,25},{10,... | collective-permute-start | bytes 1769480 | tf_op jit(solution)/shard_map/ppermute | solution.py:480
  48.4 16.2 %collective-permute-start.4 = (bf16[4,96,768]{2,1,0:T(8,128)(2,1)S(1)}, bf16[4,96,768]{2,1,0:T(8,128)(2,1)S(1)}, u32[]{:S(2)}, u32[]{:S(2)}) collective-permute-start(bf16[4,96,768]{2,1,0:T(8,128)(2,1)S(1)} %get-tuple-element.44), channel_id=1, source_target_pairs={{0,1},{1,2},{2,3},{3,0},{4,5},{5,6},{6,7},{7,4},{8,12},{9,13},{10,... | collective-permute-start | bytes 1769480 | tf_op jit(solution)/shard_map/ppermute | solution.py:480
  65.0 6.4 %collective-permute-start.9 = (bf16[96,768]{1,0:T(8,128)(2,1)S(1)}, bf16[96,768]{1,0:T(8,128)(2,1)S(1)}, u32[]{:S(2)}, u32[]{:S(2)}) collective-permute-start(bf16[96,768]{1,0:T(8,128)(2,1)S(1)} %get-tuple-element.49), channel_id=1, source_target_pairs={{0,20},{1,21},{2,22},{3,23},{4,16},{5,17},{6,18},{7,19},{8,11},{9,... | collective-permute-start | bytes 442376 | tf_op jit(solution)/shard_map/ppermute | solution.py:480
  67.3 5.1 %collective-permute-start.8 = (bf16[96,768]{1,0:T(8,128)(2,1)S(1)}, bf16[96,768]{1,0:T(8,128)(2,1)S(1)}, u32[]{:S(2)}, u32[]{:S(2)}) collective-permute-start(bf16[96,768]{1,0:T(8,128)(2,1)S(1)} %get-tuple-element.50), channel_id=1, source_target_pairs={{0,16},{1,17},{2,18},{3,19},{4,20},{5,21},{6,22},{7,23},{8,10},{9,... | collective-permute-start | bytes 442376 | tf_op jit(solution)/shard_map/ppermute | solution.py:480
  67.3 7.2 %collective-permute-start.7 = (bf16[96,768]{1,0:T(8,128)(2,1)S(1)}, bf16[96,768]{1,0:T(8,128)(2,1)S(1)}, u32[]{:S(2)}, u32[]{:S(2)}) collective-permute-start(bf16[96,768]{1,0:T(8,128)(2,1)S(1)} %get-tuple-element.51), channel_id=1, source_target_pairs={{0,4},{1,5},{2,6},{3,7},{4,0},{5,1},{6,2},{7,3},{8,9},{9,10},{10,1... | collective-permute-start | bytes 442376 | tf_op jit(solution)/shard_map/ppermute | solution.py:480

commit v3 on v2

--- a/solution.py
+++ b/solution.py
@@ -16,6 +16,8 @@
 D = 768
 N_SEG = 8
 BLOCK = 96
+QKV_HALF = 640
+OUT_HALF = 256
 EPSILON = 1e-05
 NEG_FILL = -1e30
 SCALE = HEAD ** (-0.5)
@@ -118,29 +120,27 @@
 
 
 def first_kernel(
-    length_ref, coord_ref, tok_ref, w_qkv_ref, cot_ref, w_out_ref,
-    message_ref, packed_ref, g_ref, xhat_ref, rstd_ref, normed_ref, blocks_ref,
+    length_ref, coord_ref, cot_ref, tok_ref, w_out_ref, w_qkv_ref,
+    message_ref, packed_ref, g_ref, xhat_out, out_grad_out,
 ):
     length = length_ref[0]
     base = seg_index() * ROWS
     order = regroup()
-    coords = mm_nt(order, coord_ref[0].astype(F32).astype(BF))
-    code = sin_cos_code(coords[:, 0:1], coords[:, 1:2])
-    tokens = mm(order, tok_ref[0])
-    embedded = tokens + code
+    coords = coord_ref[0].astype(F32).astype(BF)
+    cotangent, tokens, w_out = cot_ref[0], tok_ref[0], w_out_ref[...]
+    live = (base + place_of(iota((ROWS, 1), 0))) < length
+    out_grad = jnp.where(live, mm(order, cotangent), 0.0).astype(BF)
+    out_grad_out.put(out_grad)
+    g = mm_nt(out_grad, w_out).astype(BF)
+    g_ref[...] = g
+    coords = mm_nt(order, coords)
+    embedded = mm(order, tokens) + sin_cos_code(coords[:, 0:1], coords[:, 1:2])
     centred = embedded - jnp.mean(embedded, axis=-1, keepdims=True)
     rstd = lax.rsqrt(jnp.mean(centred * centred, axis=-1, keepdims=True) + EPSILON)
     xhat = centred * rstd
-    normed = xhat.astype(BF)
-    xhat_ref[...] = xhat
-    rstd_ref[...] = jnp.broadcast_to(rstd, rstd_ref.shape)
-    normed_ref[...] = normed
-    packed = mm(normed, w_qkv_ref[...]).astype(BF)
+    xhat_out.put(jnp.concatenate([xhat, jnp.broadcast_to(rstd, (ROWS, 128))], axis=1))
+    packed = mm(xhat.astype(BF), w_qkv_ref[...]).astype(BF)
     packed_ref[...] = packed
-    live = (base + place_of(iota((ROWS, 1), 0))) < length
-    out_grad = jnp.where(live, mm(order, cot_ref[0]), 0.0).astype(BF)
-    g = mm_nt(out_grad, w_out_ref[...]).astype(BF)
-    g_ref[...] = g
 
     mask = head_mask(SLAB)
     key_col = place_of(iota((1, ROWS), 1))
@@ -183,20 +183,26 @@
                 part = put_scalars(part, columns[a])
             message_ref[j, a] = part.astype(BF)
 
-    core = lax.axis_index("core")
-    zero = jnp.zeros((ROWS, 72), F32)
-    wide = out_grad.astype(F32)
-    for b in range(16):
-        xl, z = b // 8, b % 8
-        for c in range(2):
-            dp = z * 4 + xl * 2 + c
-            rel = (core + c) % 2
-            block = jnp.concatenate([zero, wide[:, 24 * dp : 24 * dp + 24]], axis=1)
-            blocks_ref[rel, :, BLOCK * b : BLOCK * (b + 1)] = block.astype(BF)
+
+def by_owner(array, width, padded):
+    pad = jnp.zeros((ROWS, padded - 8 * width), array.dtype)
+    sides = []
+    for c in range(2):
+        pieces = []
+        for z_hi in range(2):
+            for xl in range(2):
+                for z_lo in range(4):
+                    dp = (z_hi * 4 + z_lo) * 4 + xl * 2 + c
+                    pieces.append(array[:, width * dp : width * (dp + 1)])
+            pieces.append(pad)
+        sides.append(jnp.concatenate(pieces, axis=1).astype(BF))
+    first = lax.axis_index("core") == 0
+    return jnp.where(first, sides[0], sides[1]), jnp.where(first, sides[1], sides[0])
 
 
 def dense_kernel(
-    length_ref, packed_ref, g_ref, out_ref, back_ref, weight_ref, dweight_ref
+    length_ref, packed_ref, g_ref, xhat_ref, out_grad_ref,
+    back_ref, soft_ref, early_ref,
 ):
     length = length_ref[0]
     base = seg_index() * ROWS
@@ -227,7 +233,7 @@
         out = mm(p.astype(BF), v)
         delta = jnp.sum(gm * out, axis=-1, keepdims=True)
         dp = mm_nt(gb, v)
-        out_ref[:, lanes] = fold(out)
+        back_ref[3, :, lanes] = fold(out)
         free_p = jnp.where(free, p, 0.0)
         ds = (free_p * (dp - delta) * SCALE).astype(BF)
         back_ref[0, :, lanes] = fold(mm(ds, k))
@@ -236,8 +242,12 @@
         for h in range(GROUP):
             at = ROWS * h + SLAB * (h % RATE)
             to = slice(SLAB * h, SLAB * (h + 1))
-            weight_ref[group, to] = p[at : at + SLAB]
-            dweight_ref[group, to] = dp[at : at + SLAB]
+            soft_ref[group, 0, to] = p[at : at + SLAB]
+            soft_ref[group, 1, to] = dp[at : at + SLAB]
+    mine, theirs = by_owner(out_grad_ref[...].astype(F32), 24, OUT_HALF)
+    early_ref[:, : 2 * OUT_HALF] = theirs
+    early_ref[:, 2 * OUT_HALF : 4 * OUT_HALF] = mine
+    early_ref[:, 4 * OUT_HALF :] = xhat_ref[:, :D].astype(BF)
 
 
 def dilated_kernel(length_ref, message_ref, reply_ref):
@@ -299,8 +309,8 @@
 
 
 def join_kernel(
-    reply_ref, packed_ref, g_ref, weight_ref, dweight_ref, back_ref, out_ref,
-    blended_ref, packed_grad_ref, blocks_ref,
+    reply_ref, packed_ref, g_ref, soft_ref, back_ref,
+    blended_ref, packed_grad_out, mine_ref, theirs_ref,
 ):
     small = head_mask(SLAB)
     shape = (ROWS, D)
@@ -327,34 +337,31 @@
         q = jnp.where(small, stack_slabs(packed_ref[:, :D], group).astype(F32), 0.0).astype(BF)
         gm = jnp.where(small, stack_slabs(g_ref[...], group).astype(F32), 0.0).astype(BF)
         k = packed_ref[:, D + group * WIDE : D + (group + 1) * WIDE]
-        p = weight_ref[group] * share
-        ds = (p * (dweight_ref[group] - delta) * SCALE).astype(BF)
+        p = soft_ref[group, 0] * share
+        ds = (p * (soft_ref[group, 1] - delta) * SCALE).astype(BF)
         parts[0].append(back_ref[0, :, lanes] + unstack_slabs(jnp.where(small, mm(ds, k), 0.0)))
         parts[1].append(back_ref[1, :, lanes] + mm_tn(ds, q))
         parts[2].append(back_ref[2, :, lanes] + mm_tn(p.astype(BF), gm))
         parts[3].append(unstack_slabs(jnp.where(small, share, 0.0)))
     whole = [jnp.concatenate(part, axis=1) for part in parts]
-    out = out_ref[...]
-    blended_ref[...] = jnp.where(sampled, whole[3] * out + placed(3), out).astype(BF)
+    out = back_ref[3]
+    blended = jnp.where(sampled, whole[3] * out + placed(3), out).astype(BF)
+    blended_ref[...] = blended
+    theirs_ref[:, 2 * QKV_HALF :] = blended
     grads = []
     for a in range(3):
         grad = (whole[a] + placed(a)).astype(BF)
-        packed_grad_ref[:, a * D : (a + 1) * D] = grad
+        packed_grad_out.put(grad, slice(None), slice(a * D, (a + 1) * D))
         grads.append(grad.astype(F32))
+    packed_grad_out.send(slice(None))
     grads = jnp.concatenate(grads, axis=1)
-    core = lax.axis_index("core")
-    zero = jnp.zeros((ROWS, 24), F32)
-    for b in range(16):
-        xl, z = b // 8, b % 8
-        for c in range(2):
-            dp = z * 4 + xl * 2 + c
-            rel = (core + c) % 2
-            block = jnp.concatenate([grads[:, 72 * dp : 72 * dp + 72], zero], axis=1)
-            blocks_ref[rel, :, BLOCK * b : BLOCK * (b + 1)] = block.astype(BF)
+    mine, theirs = by_owner(grads, 72, QKV_HALF)
+    mine_ref[...] = mine
+    theirs_ref[:, : 2 * QKV_HALF] = theirs
 
 
 def finish_kernel(
-    length_ref, blended_ref, w_out_ref, packed_grad_ref, w_qkv_ref, xhat_ref, rstd_ref,
+    length_ref, blended_ref, w_out_ref, packed_grad_ref, w_qkv_ref, xhat_ref,
     layer_ref, token_grad_ref, done_ref,
 ):
     length = length_ref[0]
@@ -364,47 +371,56 @@
     layer = jnp.where(live, mm(blended_ref[...], w_out_ref[...]), 0.0).astype(BF)
     layer_ref[0] = mm_tn(order, layer).astype(BF)
     dn = mm_nt(packed_grad_ref[...], w_qkv_ref[...])
-    xhat = xhat_ref[...]
+    xhat = xhat_ref[:, :D]
     mean = jnp.mean(dn, axis=-1, keepdims=True)
     slope = jnp.mean(dn * xhat, axis=-1, keepdims=True)
-    dx = ((dn - mean - xhat * slope) * rstd_ref[:, 0:1]).astype(BF)
+    dx = ((dn - mean - xhat * slope) * xhat_ref[:, D : D + 1]).astype(BF)
     token_grad_ref[0] = mm_tn(order, dx).astype(BF)
     done_ref[...] = jnp.zeros(done_ref.shape, F32)
 
 
-def weight_kernel(n0_ref, n1_ref, b0_ref, b1_ref, p0_ref, p1_ref, g0_ref, g1_ref, out_ref):
-    xh, xl, y = lax.axis_index("xh"), lax.axis_index("xl"), lax.axis_index("y")
-    core = lax.axis_index("core")
-    left = jnp.concatenate([n0_ref[...], n1_ref[...], b0_ref[...], b1_ref[...]], axis=0)
-    for part in range(4):
-        to_xl, half = part // 2, part % 2
-        lanes = slice(part * WIDE, (part + 1) * WIDE)
-        right = jnp.concatenate(
-            [p0_ref[:, lanes], p1_ref[:, lanes], g0_ref[:, lanes], g1_ref[:, lanes]], axis=0
+def weight_kernel(own_early_ref, early_ref, blended_ref, late_ref, mine_ref, partial_out):
+    def both(own, other):
+        return jnp.concatenate([own, other], axis=0)
+
+    normed = both(own_early_ref[:, 4 * OUT_HALF :], early_ref[:, 4 * OUT_HALF :])
+    blended = both(blended_ref[...], late_ref[:, 2 * QKV_HALF :])
+    for half in range(2):
+        at = half * QKV_HALF
+        qkv = mm_tn(normed, both(mine_ref[:, at : at + 576], late_ref[:, at : at + 576]))
+        at = half * OUT_HALF
+        out = mm_tn(
+            blended,
+            both(
+                own_early_ref[:, 2 * OUT_HALF + at : 2 * OUT_HALF + at + 192],
+                early_ref[:, at : at + 192],
+            ),
         )
-        total = mm_tn(left, right).astype(BF)
-        for s in range(N_SEG):
-            x_rel = 2 * ((to_xl + xl) % 2) + (s // 4 + xh) % 2
-            y_rel = (s % 4 - y + 4) % 4
-            first = jnp.where(core == 0, y_rel, x_rel)
-            second = jnp.where(core == 0, x_rel, y_rel)
-            out_ref[first, second, :, half * WIDE : (half + 1) * WIDE] = total[
-                BLOCK * s : BLOCK * (s + 1)
-            ]
-
-
-def first_sum_kernel(own_ref, a_ref, b_ref, c_ref, out_ref):
-    for k in range(4):
-        total = own_ref[0, k].astype(F32) + a_ref[k].astype(F32)
-        total = total + (b_ref[k].astype(F32) + c_ref[k].astype(F32))
-        out_ref[k] = total.astype(BF)
-
-
-def second_sum_kernel(own_ref, a_ref, b_ref, c_ref, out_ref):
-    total = own_ref[0].astype(F32) + a_ref[...].astype(F32)
-    total = total + (b_ref[...].astype(F32) + c_ref[...].astype(F32))
-    for z in range(8):
-        out_ref[z] = total[:, BLOCK * z : BLOCK * (z + 1)].astype(BF)
+        for xl in range(2):
+            total = jnp.concatenate(
+                [
+                    qkv[:, 288 * xl : 288 * (xl + 1)],
+                    out[:, BLOCK * xl : BLOCK * (xl + 1)],
+                ],
+                axis=1,
+            ).astype(BF)
+            for s in range(N_SEG):
+                lanes = slice(half * WIDE, (half + 1) * WIDE)
+                rows = total[BLOCK * s : BLOCK * (s + 1)]
+                partial_out.put(rows, N_SEG * xl + s, slice(None), lanes)
+            partial_out.send(slice(N_SEG * xl, N_SEG * (xl + 1)), slice(None), lanes)
+
+
+def plane_sum_kernel(parts_ref, out_ref):
+    for half in range(2):
+        lanes = slice(half * WIDE, (half + 1) * WIDE)
+        total = parts_ref[0, :, lanes].astype(F32)
+        for n in range(1, 16):
+            total = total + parts_ref[n, :, lanes].astype(F32)
+        for z in range(4):
+            out_ref[4 * half + z] = jnp.concatenate(
+                [total[:, 72 * z : 72 * z + 72], total[:, 288 + 24 * z : 312 + 24 * z]], axis=1
+            ).astype(BF)
 
 
 def last_sum_kernel(parts_ref, in_ref, out_ref):
@@ -430,6 +446,25 @@
         return self.target[index]
 
 
+class Sent:
+    def __init__(self, slot, target, sems, parts):
+        self.slot, self.target, self.sems, self.parts = slot, target, sems, parts
+        self.copies = []
+
+    def put(self, value, *index):
+        index = index or (slice(None),)
+        self.slot[index] = value
+        if self.parts == 1:
+            self.send(*index)
+
+    def send(self, *index):
+        copy = pltpu.make_async_copy(
+            self.slot.at[index], self.target.at[index], self.sems[len(self.copies)]
+        )
+        copy.start()
+        self.copies.append(copy)
+
+
 def call(kernel, outs, *inputs):
     specs = {"s": SMEM, "v": VMEM, "f": ANY, "h": ANY, "n": ANY}
     kinds = [kind for kind, _ in inputs]
@@ -437,27 +472,40 @@
         pltpu.with_memory_space_constraint(x, pltpu.HBM) if kind == "h" else x
         for kind, x in inputs
     ]
-    fetched = [x for kind, x in inputs if kind in "fh"]
+    moved = [x for kind, x in inputs if kind in "fh"]
+    count = len(moved) + sum(out[2] for out in outs if len(out) > 2)
+    moved += [jax.ShapeDtypeStruct(*out[:2]) for out in outs if len(out) > 2]
 
     def body(*refs):
         n, m = len(kinds), len(outs)
-        slots = list(refs[n + m : -1]) if fetched else []
-        given = []
+        slots = list(refs[n + m : -1]) if moved else []
+        sems = [refs[-1].at[i] for i in range(count)]
+        given, sent = [], []
         for kind, ref in zip(kinds, refs[:n]):
             if kind in "fh":
-                given.append(Held(ref, slots.pop(0), refs[-1].at[len(slots)]))
+                given.append(Held(ref, slots.pop(0), sems.pop(0)))
             elif kind != "n":
                 given.append(ref)
-        kernel(*given, *refs[n : n + m])
-
-    scratch = [pltpu.VMEM(x.shape, x.dtype) for x in fetched]
-    if fetched:
-        scratch.append(pltpu.SemaphoreType.DMA((len(fetched),)))
+        for out, ref in zip(outs, refs[n : n + m]):
+            if len(out) > 2:
+                ref = Sent(slots.pop(0), ref, [sems.pop(0) for _ in range(out[2])], out[2])
+                sent.append(ref)
+            given.append(ref)
+        kernel(*given)
+        for ref in sent:
+            for copy in ref.copies:
+                copy.wait()
+
+    scratch = [pltpu.VMEM(x.shape, x.dtype) for x in moved]
+    if moved:
+        scratch.append(pltpu.SemaphoreType.DMA((count,)))
     return pl.pallas_call(
         body,
-        out_shape=[jax.ShapeDtypeStruct(shape, dtype) for shape, dtype in outs],
+        out_shape=[
+            pltpu.HBM(*out[:2]) if len(out) > 2 else jax.ShapeDtypeStruct(*out) for out in outs
+        ],
         in_specs=[specs[kind] for kind in kinds],
-        out_specs=[VMEM] * len(outs),
+        out_specs=[ANY if len(out) > 2 else VMEM for out in outs],
         scratch_shapes=scratch,
         compiler_params=pltpu.CompilerParams(vmem_limit_bytes=LIMIT),
         name=kernel.__name__,
@@ -468,112 +516,84 @@
     return lax.ppermute(x, "core", [(0, 1), (1, 0)])
 
 
-def swap(x, k, stage):
-    pairs = []
-    for i in range(32):
-        xl, core, xh, y = i // 16, (i // 8) % 2, (i // 4) % 2, i % 4
-        if core == stage:
-            y = (y + k) % 4
-        else:
-            xl, xh = xl ^ (k // 2), xh ^ (k % 2)
-        pairs.append((i, ((xl * 2 + core) * 2 + xh) * 4 + y))
-    return lax.ppermute(x, ("xl", "core", "xh", "y"), pairs)
-
-
 def per_device(tokens, coords, lengths, w_qkv, w_out, cotangent):
-    message, packed, g, xhat, rstd, normed, grad_blocks = call(
+    message, packed, g, xhat, out_grad = call(
         first_kernel,
         [
             ((N_SEG, 4, SLAB, 128), BF),
             ((ROWS, 3 * D), BF),
             ((ROWS, D), BF),
-            ((ROWS, D), F32),
-            ((ROWS, 128), F32),
-            ((ROWS, D), BF),
-            ((2, ROWS, 16 * BLOCK), BF),
+            ((ROWS, D + 128), F32, 1),
+            ((ROWS, D), BF, 1),
         ],
         ("s", lengths),
         ("h", jnp.transpose(coords, (0, 2, 1))),
+        ("h", cotangent),
         ("h", tokens),
+        ("h", w_out),
         ("h", w_qkv),
-        ("h", cotangent),
-        ("h", w_out),
     )
     message = lax.all_to_all(message, ("xh", "y"), 0, 0, tiled=True)
-    other_normed = to_core(normed)
-    other_grad = to_core(grad_blocks[1])
-    out, back, weight, dweight = call(
+    back, soft, own_early = call(
         dense_kernel,
         [
-            ((ROWS, D), F32),
-            ((3, ROWS, D), F32),
-            ((2, GROUP * SLAB, ROWS), F32),
-            ((2, GROUP * SLAB, ROWS), F32),
+            ((4, ROWS, D), F32),
+            ((2, 2, GROUP * SLAB, ROWS), F32),
+            ((ROWS, 4 * OUT_HALF + D), BF),
         ],
         ("s", lengths),
         ("v", packed),
         ("v", g),
+        ("h", xhat),
+        ("h", out_grad),
     )
     (reply,) = call(
         dilated_kernel,
         [((N_SEG, 4, SLAB, 128), BF)],
         ("s", lengths),
         ("v", message),
-        ("n", dweight),
-        ("n", other_normed),
-        ("n", other_grad),
+        ("n", soft),
     )
     reply = lax.all_to_all(reply, ("xh", "y"), 0, 0, tiled=True)
-    blended, packed_grad, blocks = call(
+    early = to_core(own_early)
+    blended, packed_grad, mine, late = call(
         join_kernel,
-        [((ROWS, D), BF), ((ROWS, 3 * D), BF), ((2, ROWS, 16 * BLOCK), BF)],
+        [
+            ((ROWS, D), BF),
+            ((ROWS, 3 * D), BF, 2),
+            ((ROWS, 2 * QKV_HALF), BF),
+            ((ROWS, 2 * QKV_HALF + D), BF),
+        ],
         ("v", reply),
         ("v", packed),
-        ("v", g),
-        ("h", weight),
-        ("v", dweight),
+        ("h", g),
+        ("v", soft),
         ("v", back),
-        ("h", out),
-    )
-    other_blended = to_core(blended)
-    other_blocks = to_core(blocks[1])
+        ("n", early),
+    )
+    late = to_core(late)
     (partial,) = call(
         weight_kernel,
-        [((4, 4, BLOCK, D), BF)],
-        ("f", normed),
-        ("f", other_normed),
+        [((16, BLOCK, D), BF, 4)],
+        ("v", own_early),
+        ("v", early),
         ("v", blended),
-        ("v", other_blended),
-        ("v", blocks[0]),
-        ("v", other_blocks),
-        ("f", grad_blocks[0]),
-        ("f", other_grad),
-    )
+        ("v", late),
+        ("v", mine),
+    )
+    partial = lax.all_to_all(partial, ("xl", "xh", "y"), 0, 0, tiled=True)
     layer_out, token_grad, done = call(
         finish_kernel,
         [((1, ROWS, D), BF), ((1, ROWS, D), BF), ((8, 128), F32)],
         ("s", lengths),
         ("f", blended),
         ("h", w_out),
-        ("f", packed_grad),
+        ("h", packed_grad),
         ("h", w_qkv),
         ("h", xhat),
-        ("h", rstd),
-    )
-    arrived = [swap(partial[k], k, 0) for k in (1, 2, 3)]
+    )
     (partial,) = call(
-        first_sum_kernel,
-        [((4, BLOCK, D), BF)],
-        ("v", partial),
-        *[("v", x) for x in arrived],
-        ("n", done),
-    )
-    arrived = [swap(partial[k], k, 1) for k in (1, 2, 3)]
-    (partial,) = call(
-        second_sum_kernel,
-        [((8, BLOCK, BLOCK), BF)],
-        ("v", partial),
-        *[("v", x) for x in arrived],
+        plane_sum_kernel, [((8, BLOCK, BLOCK), BF)], ("v", partial), ("n", done)
     )
     arrived = lax.all_to_all(partial, "z", 0, 0, tiled=True)
     grad_in, grad_out = call(

time: 94.4 us -> 101 us (1.070)
  waiting for transfers between devices: 18.9 us -> 29.5 us
  local copies, waits for them, and re-layouts: 2.58 us -> 0.01 us
  starting transfers between devices: 15.8 us -> 14 us
    all_to_all x0 -> x1, waiting for transfers between devices: none -> 26.4 us  [per_device(): partial = lax.all_to_all(partial, ('xl', 'xh', 'y'), 0, 0, tiled=True)]
    ppermute x6 -> x0, waiting for transfers between devices: 15.8 us -> none  [swap(): return lax.ppermute(x, ('xl', 'core', 'xh', 'y'), pairs)]
    ppermute x6 -> x0, starting transfers between devices: 7.77 us -> none  [swap(): return lax.ppermute(x, ('xl', 'core', 'xh', 'y'), pairs)]
    all_to_all x0 -> x1, starting transfers between devices: none -> 6.34 us  [per_device(): partial = lax.all_to_all(partial, ('xl', 'xh', 'y'), 0, 0, tiled=True)]
    unnamed x8 -> x2, local copies, waits for them, and re-layouts: 1.48 us -> 0.01 us
    squeeze x4 -> x0, local copies, waits for them, and re-layouts: 1.1 us -> none  [the longest x1 0.89 us: per_device(): grad_blocks[0]]
    pallas_call x9 -> x8, Pallas kernels: 24.8 us -> 24.2 us  [call(): pl.pallas_call(body, out_shape=[pltpu.HBM(*out[:2]) if len(out) > 2 else...]
  transfers between devices with their start and end apart: 11 -> 4, of which waited for: 8 -> 3; matrix products, arithmetic and copies ran while one was open for 0% -> 0% of each run, Pallas kernels for 9% -> 11%
where the time goes in v3:
time: 101 us; the launch traced here: 99.5 us
  blocking collectives  30.5 us (30%)
  waiting for transfers between devices  29.5 us (29%)
  Pallas kernels  24.2 us (24%)
  starting transfers between devices  14 us (14%)
  between operations  1.37 us (1%)
    all_to_all x1, waiting for transfers between devices, per_device(): partial = lax.all_to_all(partial, ('xl', 'xh', 'y'), 0, 0, tiled=True)  26.4 us
    pallas_call x8, Pallas kernels, call(): pl.pallas_call(body, out_shape=[pltpu.HBM(*out[:2]) if len(out) > 2 else...  24.2 us
    all_to_all x1, blocking collectives, per_device(): arrived = lax.all_to_all(partial, 'z', 0, 0, tiled=True)  18.2 us
    all_to_all x1, blocking collectives, per_device(): reply = lax.all_to_all(reply, ('xh', 'y'), 0, 0, tiled=True)  12.3 us
    all_to_all x1, starting transfers between devices, per_device(): message = lax.all_to_all(message, ('xh', 'y'), 0, 0, tiled=True)  7.45 us
    all_to_all x1, starting transfers between devices, per_device(): partial = lax.all_to_all(partial, ('xl', 'xh', 'y'), 0, 0, tiled=True)  6.34 us
  transfers between devices with their start and end apart: 4, of which 3 were waited for; matrix products, arithmetic and copies ran while one was open for 0% of the time, Pallas kernels for 11%

profile of v3, /device:TPU:6, one launch (start us, length us, event | category | flops | bytes accessed | tf_op | source)
XLA Modules:
  0.0 99.5 jit_solution(14052503227393912256)
XLA Ops:
  1.3 5.2 %first_kernel.1 = (bf16[8,4,32,128]{3,2,1,0:T(8,128)(2,1)}, bf16[128,2304]{1,0:T(8,128)(2,1)S(1)}, bf16[128,768]{1,0:T(8,128)(2,1)S(1)}, f32[128,896]{1,0:T(8,128)}, bf16[128,768]{1,0:T(8,128)(2,1)}) custom-call(s32[1]{0:T(128)S(6)} %copy.10.refs_0_, s32[1,2,128]{2,1,0:T(2,128)} %bitcast.3, bf16[1,128,768]{2,1,0:T(8,128)(2,1)} %refs_2_.2, ...), custom_call_target="tpu_custom_call" | custom-call | tf_op jit(solution)/shard_map/first_kernel/pallas_call | solution.py:502
  6.4 0.0 copy-start
  6.5 7.4 %all-to-all-start = ((bf16[8,4,32,128]{3,2,1,0:T(8,128)(2,1)}), bf16[8,4,32,128]{3,2,1,0:T(8,128)(2,1)S(1)}, u32[]{:S(2)}, u32[]{:S(2)}) async-start(bf16[8,4,32,128]{3,2,1,0:T(8,128)(2,1)} %get-tuple-element.21), calls=%async_computation | async-start | bytes 524288 | tf_op jit(solution)/shard_map/all_to_all | solution.py:536
  13.9 4.5 %dense_kernel.1 = (f32[4,128,768]{2,1,0:T(8,128)S(1)}, f32[2,2,256,128]{3,2,1,0:T(8,128)S(1)}, bf16[128,1792]{1,0:T(8,128)(2,1)}) custom-call(s32[1]{0:T(128)S(6)} %copy.10.refs_0_, bf16[128,2304]{1,0:T(8,128)(2,1)S(1)} %get-tuple-element.22.refs_1_, bf16[128,768]{1,0:T(8,128)(2,1)S(1)} %get-tuple-element.23.refs_2_, ...), custom_call_target="tpu_custom_call" | custom-call | tf_op jit(solution)/shard_map/dense_kernel/pallas_call | solution.py:502
  18.4 0.0 copy-done
  18.4 0.1 collective-permute-start
  18.5 1.2 %all-to-all-done.refs_1_ = bf16[8,4,32,128]{3,2,1,0:T(8,128)(2,1)S(1)} async-done(((bf16[8,4,32,128]{3,2,1,0:T(8,128)(2,1)}), bf16[8,4,32,128]{3,2,1,0:T(8,128)(2,1)S(1)}, u32[]{:S(2)}, u32[]{:S(2)}) %all-to-all-start) | async-done | bytes 262176 | tf_op jit(solution)/shard_map/all_to_all | solution.py:536
  19.7 1.6 %dilated_kernel.1 = bf16[8,4,32,128]{3,2,1,0:T(8,128)(2,1)S(1)} custom-call(s32[1]{0:T(128)S(6)} %copy.10.refs_0_, bf16[8,4,32,128]{3,2,1,0:T(8,128)(2,1)S(1)} %all-to-all-done.refs_1_, f32[2,2,256,128]{3,2,1,0:T(8,128)S(1)} %get-tuple-element.26.refs_2_.refs_3_), custom_call_target="tpu_custom_call" | custom-call | tf_op jit(solution)/shard_map/dilated_kernel/pallas_call | solution.py:502
  21.3 12.3 %all_to_all.20.refs_0_ = bf16[8,4,32,128]{3,2,1,0:T(8,128)(2,1)S(1)} all-to-all(bf16[8,4,32,128]{3,2,1,0:T(8,128)(2,1)S(1)} %dilated_kernel.1), channel_id=1, replica_groups=mesh['z'=8,'xl'=2,'core'=2,'xh'=2,'y'=4] {'xh','y'}, dimensions={0} | all-to-all | bytes 524288 | tf_op jit(solution)/shard_map/all_to_all | solution.py:557
  33.6 0.0 collective-permute-done.refs_5_.refs_1_
  33.6 3.0 %join_kernel.1 = (bf16[128,768]{1,0:T(8,128)(2,1)S(1)}, bf16[128,2304]{1,0:T(8,128)(2,1)}, bf16[128,1280]{1,0:T(8,128)(2,1)S(1)}, bf16[128,2048]{1,0:T(8,128)(2,1)S(1)}) custom-call(bf16[8,4,32,128]{3,2,1,0:T(8,128)(2,1)S(1)} %all_to_all.20.refs_0_, bf16[128,2304]{1,0:T(8,128)(2,1)S(1)} %get-tuple-element.22.refs_1_, bf16[128,768]{1,0:T(8,128)(2,1)} %copy-done, ...), custom_call_target="tpu_custom_call" | custom-call | tf_op jit(solution)/shard_map/join_kernel/pallas_call | solution.py:502
  36.6 0.1 collective-permute-start.1
  36.7 1.9 %collective-permute-done.1.refs_3_ = bf16[128,2048]{1,0:T(8,128)(2,1)S(1)} collective-permute-done((bf16[128,2048]{1,0:T(8,128)(2,1)S(1)}, bf16[128,2048]{1,0:T(8,128)(2,1)S(1)}, u32[]{:S(2)}, u32[]{:S(2)}) %collective-permute-start.1) | collective-permute-done | bytes 524320 | tf_op jit(solution)/shard_map/ppermute | solution.py:516
  38.6 3.5 %weight_kernel.1 = bf16[16,96,768]{2,1,0:T(8,128)(2,1)} custom-call(bf16[128,1792]{1,0:T(8,128)(2,1)} %get-tuple-element.28.refs_0_, bf16[128,1792]{1,0:T(8,128)(2,1)S(1)} %collective-permute-done.refs_5_.refs_1_, bf16[128,768]{1,0:T(8,128)(2,1)S(1)} %get-tuple-element.29.refs_1_.refs_2_, bf16[128,2048]{1,0:T(8,128)(2,1)S(1)} %collective-permute-done.1.refs_3_, ...), custom_call_target="tpu_custom_call" | custom-call | tf_op jit(solution)/shard_map/weight_kernel/pallas_call | solution.py:502
  42.2 6.3 %all-to-all-start.2 = ((bf16[16,96,768]{2,1,0:T(8,128)(2,1)}), bf16[16,96,768]{2,1,0:T(8,128)(2,1)S(1)}, u32[]{:S(2)}, u32[]{:S(2)}) async-start(bf16[16,96,768]{2,1,0:T(8,128)(2,1)} %weight_kernel.1), calls=%async_computation.2 | async-start | bytes 4718592 | tf_op jit(solution)/shard_map/all_to_all | solution.py:584
  48.5 5.2 %finish_kernel.1 = (bf16[1,128,768]{2,1,0:T(8,128)(2,1)}, bf16[1,128,768]{2,1,0:T(8,128)(2,1)}, f32[8,128]{1,0:T(8,128)S(1)}) custom-call(s32[1]{0:T(128)S(6)} %copy.10.refs_0_, bf16[128,768]{1,0:T(8,128)(2,1)S(1)} %get-tuple-element.29.refs_1_.refs_2_, bf16[768,768]{1,0:T(8,128)(2,1)} %refs_2_.3, bf16[128,2304]{1,0:T(8,128)(2,1)} %get-tuple-element.30.refs_3_, ...), custom_call_target="tpu_custom_call" | custom-call | tf_op jit(solution)/shard_map/finish_kernel/pallas_call | solution.py:502
  53.8 26.4 %all-to-all-done.2.refs_0_ = bf16[16,96,768]{2,1,0:T(8,128)(2,1)S(1)} async-done(((bf16[16,96,768]{2,1,0:T(8,128)(2,1)}), bf16[16,96,768]{2,1,0:T(8,128)(2,1)S(1)}, u32[]{:S(2)}, u32[]{:S(2)}) %all-to-all-start.2) | async-done | bytes 2359328 | tf_op jit(solution)/shard_map/all_to_all | solution.py:584
  80.2 0.4 plane_sum_kernel.1
  80.6 18.2 %all_to_all.21.refs_0_ = bf16[8,96,96]{2,1,0:T(8,128)(2,1)S(1)} all-to-all(bf16[8,96,96]{2,1,0:T(8,128)(2,1)S(1)} %plane_sum_kernel.1), channel_id=1, replica_groups=mesh['z'=8,'xl'=2,'core'=2,'xh'=2,'y'=4] {'z'}, dimensions={0} | all-to-all | bytes 294912 | tf_op jit(solution)/shard_map/all_to_all | solution.py:598
  98.8 0.7 last_sum_kernel.1
Async XLA Ops:
  6.4 12.0 %copy-start = (bf16[128,768]{1,0:T(8,128)(2,1)}, bf16[128,768]{1,0:T(8,128)(2,1)S(1)}, u32[]{:S(2)}) copy-start(bf16[128,768]{1,0:T(8,128)(2,1)S(1)} %get-tuple-element.23.refs_2_) | copy-start | bytes 589828
  6.5 13.3 %all-to-all-start = ((bf16[8,4,32,128]{3,2,1,0:T(8,128)(2,1)}), bf16[8,4,32,128]{3,2,1,0:T(8,128)(2,1)S(1)}, u32[]{:S(2)}, u32[]{:S(2)}) async-start(bf16[8,4,32,128]{3,2,1,0:T(8,128)(2,1)} %get-tuple-element.21), calls=%async_computation | async-start | bytes 524288 | tf_op jit(solution)/shard_map/all_to_all | solution.py:536
  18.4 15.2 %collective-permute-start = (bf16[128,1792]{1,0:T(8,128)(2,1)}, bf16[128,1792]{1,0:T(8,128)(2,1)S(1)}, u32[]{:S(2)}, u32[]{:S(2)}) collective-permute-start(bf16[128,1792]{1,0:T(8,128)(2,1)} %get-tuple-element.28.refs_0_), channel_id=1, source_target_pairs={{0,8},{8,0},{1,9},{9,1},{2,10},{10,2},{3,11},{11,3},{4,12},{12,4},... | collective-permute-start | bytes 1376264 | tf_op jit(solution)/shard_map/ppermute | solution.py:516
  36.6 2.0 %collective-permute-start.1 = (bf16[128,2048]{1,0:T(8,128)(2,1)S(1)}, bf16[128,2048]{1,0:T(8,128)(2,1)S(1)}, u32[]{:S(2)}, u32[]{:S(2)}) collective-permute-start(bf16[128,2048]{1,0:T(8,128)(2,1)S(1)} %get-tuple-element.33), channel_id=1, source_target_pairs={{0,8},{8,0},{1,9},{9,1},{2,10},{10,2},{3,11},{11,3},{4,12},{12,4},... | collective-permute-start | bytes 1572872 | tf_op jit(solution)/shard_map/ppermute | solution.py:516
  42.2 38.0 %all-to-all-start.2 = ((bf16[16,96,768]{2,1,0:T(8,128)(2,1)}), bf16[16,96,768]{2,1,0:T(8,128)(2,1)S(1)}, u32[]{:S(2)}, u32[]{:S(2)}) async-start(bf16[16,96,768]{2,1,0:T(8,128)(2,1)} %weight_kernel.1), calls=%async_computation.2 | async-start | bytes 4718592 | tf_op jit(solution)/shard_map/all_to_all | solution.py:584

commit v4 on v3

--- a/solution.py
+++ b/solution.py
@@ -1,3 +1,5 @@
+import functools
+
 import jax
 import jax.numpy as jnp
 from jax import lax
@@ -310,7 +312,7 @@
 
 def join_kernel(
     reply_ref, packed_ref, g_ref, soft_ref, back_ref,
-    blended_ref, packed_grad_out, mine_ref, theirs_ref,
+    blended_ref, packed_grad_ref, mine_ref, theirs_ref,
 ):
     small = head_mask(SLAB)
     shape = (ROWS, D)
@@ -351,9 +353,8 @@
     grads = []
     for a in range(3):
         grad = (whole[a] + placed(a)).astype(BF)
-        packed_grad_out.put(grad, slice(None), slice(a * D, (a + 1) * D))
+        packed_grad_ref[:, a * D : (a + 1) * D] = grad
         grads.append(grad.astype(F32))
-    packed_grad_out.send(slice(None))
     grads = jnp.concatenate(grads, axis=1)
     mine, theirs = by_owner(grads, 72, QKV_HALF)
     mine_ref[...] = mine
@@ -379,55 +380,74 @@
     done_ref[...] = jnp.zeros(done_ref.shape, F32)
 
 
-def weight_kernel(own_early_ref, early_ref, blended_ref, late_ref, mine_ref, partial_out):
+def weight_kernel(
+    half, own_early_ref, early_ref, blended_ref, late_ref, mine_ref, out_ref
+):
+    xh, xl, y = lax.axis_index("xh"), lax.axis_index("xl"), lax.axis_index("y")
+    core = lax.axis_index("core")
+
     def both(own, other):
         return jnp.concatenate([own, other], axis=0)
 
-    normed = both(own_early_ref[:, 4 * OUT_HALF :], early_ref[:, 4 * OUT_HALF :])
-    blended = both(blended_ref[...], late_ref[:, 2 * QKV_HALF :])
+    at = half * QKV_HALF
+    qkv = mm_tn(
+        both(own_early_ref[:, 4 * OUT_HALF :], early_ref[:, 4 * OUT_HALF :]),
+        both(mine_ref[:, at : at + 576], late_ref[:, at : at + 576]),
+    ).astype(BF)
+    at = half * OUT_HALF
+    out = mm_tn(
+        both(blended_ref[...], late_ref[:, 2 * QKV_HALF :]),
+        both(
+            own_early_ref[:, 2 * OUT_HALF + at : 2 * OUT_HALF + at + 192],
+            early_ref[:, at : at + 192],
+        ),
+    ).astype(BF)
+    for to_xl in range(2):
+        total = jnp.concatenate(
+            [
+                qkv[:, 288 * to_xl : 288 * (to_xl + 1)].astype(F32),
+                out[:, BLOCK * to_xl : BLOCK * (to_xl + 1)].astype(F32),
+            ],
+            axis=1,
+        ).astype(BF)
+        for s in range(N_SEG):
+            x_rel = 2 * ((s // 4 + xh) % 2) + (to_xl + xl) % 2
+            y_rel = (s % 4 - y + 4) % 4
+            first = jnp.where(core == 0, y_rel, x_rel)
+            second = jnp.where(core == 0, x_rel, y_rel)
+            out_ref[first, second] = total[BLOCK * s : BLOCK * (s + 1)]
+
+
+def first_sum_kernel(*refs):
+    out_ref = refs[-1]
     for half in range(2):
-        at = half * QKV_HALF
-        qkv = mm_tn(normed, both(mine_ref[:, at : at + 576], late_ref[:, at : at + 576]))
-        at = half * OUT_HALF
-        out = mm_tn(
-            blended,
-            both(
-                own_early_ref[:, 2 * OUT_HALF + at : 2 * OUT_HALF + at + 192],
-                early_ref[:, at : at + 192],
-            ),
-        )
-        for xl in range(2):
-            total = jnp.concatenate(
-                [
-                    qkv[:, 288 * xl : 288 * (xl + 1)],
-                    out[:, BLOCK * xl : BLOCK * (xl + 1)],
-                ],
-                axis=1,
-            ).astype(BF)
-            for s in range(N_SEG):
-                lanes = slice(half * WIDE, (half + 1) * WIDE)
-                rows = total[BLOCK * s : BLOCK * (s + 1)]
-                partial_out.put(rows, N_SEG * xl + s, slice(None), lanes)
-            partial_out.send(slice(N_SEG * xl, N_SEG * (xl + 1)), slice(None), lanes)
-
-
-def plane_sum_kernel(parts_ref, out_ref):
+        own_ref, a_ref, b_ref, c_ref = refs[4 * half : 4 * half + 4]
+        for k in range(4):
+            total = own_ref[0, k].astype(F32) + a_ref[k].astype(F32)
+            total = total + (b_ref[k].astype(F32) + c_ref[k].astype(F32))
+            out_ref[k, :, half * WIDE : (half + 1) * WIDE] = total.astype(BF)
+
+
+def second_sum_kernel(own_ref, a_ref, b_ref, c_ref, out_ref):
+    whole = own_ref[0].astype(F32) + a_ref[...].astype(F32)
+    whole = whole + (b_ref[...].astype(F32) + c_ref[...].astype(F32))
     for half in range(2):
-        lanes = slice(half * WIDE, (half + 1) * WIDE)
-        total = parts_ref[0, :, lanes].astype(F32)
-        for n in range(1, 16):
-            total = total + parts_ref[n, :, lanes].astype(F32)
+        total = whole[:, half * WIDE : (half + 1) * WIDE]
         for z in range(4):
-            out_ref[4 * half + z] = jnp.concatenate(
+            piece = jnp.concatenate(
                 [total[:, 72 * z : 72 * z + 72], total[:, 288 + 24 * z : 312 + 24 * z]], axis=1
-            ).astype(BF)
+            )
+            side = jnp.concatenate([piece[72:, 32 * n : 32 * n + 32] for n in range(3)], axis=0)
+            out_ref[4 * half + z] = jnp.concatenate([piece[:72], side], axis=1).astype(BF)
 
 
 def last_sum_kernel(parts_ref, in_ref, out_ref):
     total = parts_ref[0].astype(F32)
     for z in range(1, 8):
         total = total + parts_ref[z].astype(F32)
-    total = total.T
+    side = total[:, BLOCK:]
+    foot = jnp.concatenate([side[24 * n : 24 * n + 24] for n in range(3)], axis=1)
+    total = jnp.concatenate([total[:, :BLOCK], foot], axis=0).T
     in_ref[...] = total[:72]
     out_ref[...] = total[72:]
 
@@ -447,22 +467,13 @@
 
 
 class Sent:
-    def __init__(self, slot, target, sems, parts):
-        self.slot, self.target, self.sems, self.parts = slot, target, sems, parts
-        self.copies = []
-
-    def put(self, value, *index):
-        index = index or (slice(None),)
-        self.slot[index] = value
-        if self.parts == 1:
-            self.send(*index)
-
-    def send(self, *index):
-        copy = pltpu.make_async_copy(
-            self.slot.at[index], self.target.at[index], self.sems[len(self.copies)]
-        )
-        copy.start()
-        self.copies.append(copy)
+    def __init__(self, slot, target, sem):
+        self.slot = slot
+        self.copy = pltpu.make_async_copy(slot, target, sem)
+
+    def put(self, value):
+        self.slot[...] = value
+        self.copy.start()
 
 
 def call(kernel, outs, *inputs):
@@ -473,32 +484,29 @@
         for kind, x in inputs
     ]
     moved = [x for kind, x in inputs if kind in "fh"]
-    count = len(moved) + sum(out[2] for out in outs if len(out) > 2)
     moved += [jax.ShapeDtypeStruct(*out[:2]) for out in outs if len(out) > 2]
 
     def body(*refs):
         n, m = len(kinds), len(outs)
         slots = list(refs[n + m : -1]) if moved else []
-        sems = [refs[-1].at[i] for i in range(count)]
         given, sent = [], []
         for kind, ref in zip(kinds, refs[:n]):
             if kind in "fh":
-                given.append(Held(ref, slots.pop(0), sems.pop(0)))
+                given.append(Held(ref, slots.pop(0), refs[-1].at[len(slots)]))
             elif kind != "n":
                 given.append(ref)
         for out, ref in zip(outs, refs[n : n + m]):
             if len(out) > 2:
-                ref = Sent(slots.pop(0), ref, [sems.pop(0) for _ in range(out[2])], out[2])
+                ref = Sent(slots.pop(0), ref, refs[-1].at[len(slots)])
                 sent.append(ref)
             given.append(ref)
         kernel(*given)
         for ref in sent:
-            for copy in ref.copies:
-                copy.wait()
+            ref.copy.wait()
 
     scratch = [pltpu.VMEM(x.shape, x.dtype) for x in moved]
     if moved:
-        scratch.append(pltpu.SemaphoreType.DMA((count,)))
+        scratch.append(pltpu.SemaphoreType.DMA((len(moved),)))
     return pl.pallas_call(
         body,
         out_shape=[
@@ -512,8 +520,28 @@
     )(*arrays)
 
 
+def named(name, kernel):
+    def run(*refs):
+        kernel(*refs)
+
+    run.__name__ = name
+    return run
+
+
 def to_core(x):
     return lax.ppermute(x, "core", [(0, 1), (1, 0)])
+
+
+def swap(x, k, stage):
+    pairs = []
+    for i in range(32):
+        xl, core, xh, y = i // 16, (i // 8) % 2, (i // 4) % 2, i % 4
+        if core == stage:
+            y = (y + k) % 4
+        else:
+            xl, xh = xl ^ (k % 2), xh ^ (k // 2)
+        pairs.append((i, ((xl * 2 + core) * 2 + xh) * 4 + y))
+    return lax.ppermute(x, ("xl", "core", "xh", "y"), pairs)
 
 
 def per_device(tokens, coords, lengths, w_qkv, w_out, cotangent):
@@ -523,8 +551,8 @@
             ((N_SEG, 4, SLAB, 128), BF),
             ((ROWS, 3 * D), BF),
             ((ROWS, D), BF),
-            ((ROWS, D + 128), F32, 1),
-            ((ROWS, D), BF, 1),
+            ((ROWS, D + 128), F32, "h"),
+            ((ROWS, D), BF, "h"),
         ],
         ("s", lengths),
         ("h", jnp.transpose(coords, (0, 2, 1))),
@@ -560,40 +588,48 @@
         join_kernel,
         [
             ((ROWS, D), BF),
-            ((ROWS, 3 * D), BF, 2),
+            ((ROWS, 3 * D), BF),
             ((ROWS, 2 * QKV_HALF), BF),
             ((ROWS, 2 * QKV_HALF + D), BF),
         ],
         ("v", reply),
         ("v", packed),
-        ("h", g),
+        ("v", g),
         ("v", soft),
         ("v", back),
         ("n", early),
     )
     late = to_core(late)
-    (partial,) = call(
-        weight_kernel,
-        [((16, BLOCK, D), BF, 4)],
-        ("v", own_early),
-        ("v", early),
-        ("v", blended),
-        ("v", late),
-        ("v", mine),
-    )
-    partial = lax.all_to_all(partial, ("xl", "xh", "y"), 0, 0, tiled=True)
+    halves = []
+    for half in range(2):
+        (partial,) = call(
+            named("weight_kernel", functools.partial(weight_kernel, half)),
+            [((4, 4, BLOCK, WIDE), BF)],
+            ("v", own_early),
+            ("v", early),
+            ("v", blended),
+            ("v", late),
+            ("v", mine),
+        )
+        halves.append(partial)
     layer_out, token_grad, done = call(
         finish_kernel,
         [((1, ROWS, D), BF), ((1, ROWS, D), BF), ((8, 128), F32)],
         ("s", lengths),
         ("f", blended),
         ("h", w_out),
-        ("h", packed_grad),
+        ("f", packed_grad),
         ("h", w_qkv),
         ("h", xhat),
     )
+    terms = []
+    for partial in halves:
+        terms.append(("v", partial))
+        terms += [("v", swap(partial[k], k, 0)) for k in (1, 3, 2)]
+    (partial,) = call(first_sum_kernel, [((4, BLOCK, D), BF)], *terms, ("n", done))
+    terms = [("v", swap(partial[k], k, 1)) for k in (1, 3, 2)]
     (partial,) = call(
-        plane_sum_kernel, [((8, BLOCK, BLOCK), BF)], ("v", partial), ("n", done)
+        second_sum_kernel, [((8, 72, 128), BF)], ("v", partial), *terms
     )
     arrived = lax.all_to_all(partial, "z", 0, 0, tiled=True)
     grad_in, grad_out = call(

time: 101 us -> 85.3 us (0.84)
  waiting for transfers between devices: 29.5 us -> 12 us
  starting transfers between devices: 14 us -> 19.3 us
  Pallas kernels: 24.2 us -> 20.6 us
  local copies, waits for them, and re-layouts: 0.01 us -> 1.37 us
    all_to_all x1 -> x0, waiting for transfers between devices: 26.4 us -> none  [per_device(): partial = lax.all_to_all(partial, ('xl', 'xh', 'y'), 0, 0, tiled=True)]
    ppermute x0 -> x9, starting transfers between devices: none -> 11.8 us  [swap(): return lax.ppermute(x, ('xl', 'core', 'xh', 'y'), pairs)]
    ppermute x0 -> x9, waiting for transfers between devices: none -> 9.19 us  [swap(): return lax.ppermute(x, ('xl', 'core', 'xh', 'y'), pairs)]
    all_to_all x1 -> x0, starting transfers between devices: 6.34 us -> none  [per_device(): partial = lax.all_to_all(partial, ('xl', 'xh', 'y'), 0, 0, tiled=True)]
    pallas_call x8 -> x10, Pallas kernels: 24.2 us -> 20.6 us  [call(): pl.pallas_call(body, out_shape=[pltpu.HBM(*out[:2]) if len(out) > 2 else...]
    unnamed x2 -> x4, local copies, waits for them, and re-layouts: 0.01 us -> 1.16 us
  transfers between devices with their start and end apart: 4 -> 12, of which waited for: 3 -> 8; matrix products, arithmetic and copies ran while one was open for 0% -> 0% of each run, Pallas kernels for 11% -> 13%
where the time goes in v4:
time: 85.3 us; the launch traced here: 84.7 us
  blocking collectives  30.1 us (35%)
  Pallas kernels  20.6 us (24%)
  starting transfers between devices  19.3 us (23%)
  waiting for transfers between devices  12 us (14%)
  between operations  1.4 us (2%)
  local copies, waits for them, and re-layouts  1.37 us (2%)
    pallas_call x10, Pallas kernels, call(): pl.pallas_call(body, out_shape=[pltpu.HBM(*out[:2]) if len(out) > 2 else...  20.6 us
    all_to_all x1, blocking collectives, per_device(): arrived = lax.all_to_all(partial, 'z', 0, 0, tiled=True)  17.5 us
    all_to_all x1, blocking collectives, per_device(): reply = lax.all_to_all(reply, ('xh', 'y'), 0, 0, tiled=True)  12.6 us
    ppermute x9, starting transfers between devices, swap(): return lax.ppermute(x, ('xl', 'core', 'xh', 'y'), pairs)  11.8 us
    ppermute x9, waiting for transfers between devices, swap(): return lax.ppermute(x, ('xl', 'core', 'xh', 'y'), pairs)  9.19 us
    all_to_all x1, starting transfers between devices, per_device(): message = lax.all_to_all(message, ('xh', 'y'), 0, 0, tiled=True)  7.44 us
    ppermute x2, waiting for transfers between devices, to_core(): return lax.ppermute(x, 'core', [(0, 1), (1, 0)])  1.9 us
  transfers between devices with their start and end apart: 12, of which 8 were waited for; matrix products, arithmetic and copies ran while one was open for 0% of the time, Pallas kernels for 13%

profile of v4, /device:TPU:6, one launch (start us, length us, event | category | flops | bytes accessed | tf_op | source)
XLA Modules:
  0.0 84.7 jit_solution(16802780665407870602)
XLA Ops:
  1.3 5.2 %first_kernel.1 = (bf16[8,4,32,128]{3,2,1,0:T(8,128)(2,1)}, bf16[128,2304]{1,0:T(8,128)(2,1)S(1)}, bf16[128,768]{1,0:T(8,128)(2,1)S(1)}, f32[128,896]{1,0:T(8,128)}, bf16[128,768]{1,0:T(8,128)(2,1)}) custom-call(s32[1]{0:T(128)S(6)} %copy.10.refs_0_, s32[1,2,128]{2,1,0:T(2,128)} %bitcast.21, bf16[1,128,768]{2,1,0:T(8,128)(2,1)} %refs_2_.2, ...), custom_call_target="tpu_custom_call" | custom-call | tf_op jit(solution)/shard_map/first_kernel/pallas_call | solution.py:510
  6.4 7.4 %all-to-all-start = ((bf16[8,4,32,128]{3,2,1,0:T(8,128)(2,1)}), bf16[8,4,32,128]{3,2,1,0:T(8,128)(2,1)S(1)}, u32[]{:S(2)}, u32[]{:S(2)}) async-start(bf16[8,4,32,128]{3,2,1,0:T(8,128)(2,1)} %get-tuple-element.21), calls=%async_computation | async-start | bytes 524288 | tf_op jit(solution)/shard_map/all_to_all | solution.py:564
  13.9 3.8 %dense_kernel.1 = (f32[4,128,768]{2,1,0:T(8,128)S(1)}, f32[2,2,256,128]{3,2,1,0:T(8,128)S(1)}, bf16[128,1792]{1,0:T(8,128)(2,1)S(1)}) custom-call(s32[1]{0:T(128)S(6)} %copy.10.refs_0_, bf16[128,2304]{1,0:T(8,128)(2,1)S(1)} %get-tuple-element.22.refs_1_, bf16[128,768]{1,0:T(8,128)(2,1)S(1)} %get-tuple-element.23.refs_2_, ...), custom_call_target="tpu_custom_call" | custom-call | tf_op jit(solution)/shard_map/dense_kernel/pallas_call | solution.py:510
  17.7 0.0 copy-start
  17.7 1.2 %copy-done = f32[4,128,768]{2,1,0:T(8,128)} copy-done((f32[4,128,768]{2,1,0:T(8,128)}, f32[4,128,768]{2,1,0:T(8,128)S(1)}, u32[]{:S(2)}) %copy-start) | copy-done | bytes 1572888
  18.8 0.0 collective-permute-start
  18.8 0.9 %all-to-all-done.refs_1_ = bf16[8,4,32,128]{3,2,1,0:T(8,128)(2,1)S(1)} async-done(((bf16[8,4,32,128]{3,2,1,0:T(8,128)(2,1)}), bf16[8,4,32,128]{3,2,1,0:T(8,128)(2,1)S(1)}, u32[]{:S(2)}, u32[]{:S(2)}) %all-to-all-start) | async-done | bytes 262176 | tf_op jit(solution)/shard_map/all_to_all | solution.py:564
  19.7 0.0 copy-start.1
  19.7 1.6 %dilated_kernel.1 = bf16[8,4,32,128]{3,2,1,0:T(8,128)(2,1)S(1)} custom-call(s32[1]{0:T(128)S(6)} %copy.10.refs_0_, bf16[8,4,32,128]{3,2,1,0:T(8,128)(2,1)S(1)} %all-to-all-done.refs_1_, f32[2,2,256,128]{3,2,1,0:T(8,128)S(1)} %get-tuple-element.26.refs_2_.refs_3_), custom_call_target="tpu_custom_call" | custom-call | tf_op jit(solution)/shard_map/dilated_kernel/pallas_call | solution.py:510
  21.3 12.6 %all_to_all.15.refs_0_ = bf16[8,4,32,128]{3,2,1,0:T(8,128)(2,1)S(1)} all-to-all(bf16[8,4,32,128]{3,2,1,0:T(8,128)(2,1)S(1)} %dilated_kernel.1), channel_id=1, replica_groups=mesh['z'=8,'xl'=2,'core'=2,'xh'=2,'y'=4] {'xh','y'}, dimensions={0} | all-to-all | bytes 524288 | tf_op jit(solution)/shard_map/all_to_all | solution.py:585
  33.9 0.0 collective-permute-done.refs_5_.refs_1_
  33.9 0.0 copy-done.1
  33.9 1.5 %join_kernel.1 = (bf16[128,768]{1,0:T(8,128)(2,1)S(1)}, bf16[128,2304]{1,0:T(8,128)(2,1)S(1)}, bf16[128,1280]{1,0:T(8,128)(2,1)S(1)}, bf16[128,2048]{1,0:T(8,128)(2,1)S(1)}) custom-call(bf16[8,4,32,128]{3,2,1,0:T(8,128)(2,1)S(1)} %all_to_all.15.refs_0_, bf16[128,2304]{1,0:T(8,128)(2,1)S(1)} %get-tuple-element.22.refs_1_, ...), custom_call_target="tpu_custom_call" | custom-call | tf_op jit(solution)/shard_map/join_kernel/pallas_call | solution.py:510
  35.4 0.1 collective-permute-start.1
  35.5 1.9 %collective-permute-done.1.refs_3_ = bf16[128,2048]{1,0:T(8,128)(2,1)S(1)} collective-permute-done((bf16[128,2048]{1,0:T(8,128)(2,1)S(1)}, bf16[128,2048]{1,0:T(8,128)(2,1)S(1)}, u32[]{:S(2)}, u32[]{:S(2)}) %collective-permute-start.1) | collective-permute-done | bytes 524320 | tf_op jit(solution)/shard_map/ppermute | solution.py:532
  37.4 0.9 %weight_kernel.2.refs_0_ = bf16[4,4,96,384]{3,2,1,0:T(8,128)(2,1)S(1)} custom-call(bf16[128,1792]{1,0:T(8,128)(2,1)S(1)} %get-tuple-element.28.refs_0_, bf16[128,1792]{1,0:T(8,128)(2,1)S(1)} %collective-permute-done.refs_5_.refs_1_, bf16[128,768]{1,0:T(8,128)(2,1)S(1)} %get-tuple-element.29.refs_1_.refs_2_, ...), custom_call_target="tpu_custom_call" | custom-call | tf_op jit(solution)/shard_map/weight_kernel/pallas_call | solution.py:510
  38.3 0.1 slice_bitcast_fusion.3
  38.4 0.9 %collective-permute-start.4 = (bf16[4,96,384]{2,1,0:T(8,128)(2,1)S(1)}, bf16[4,96,384]{2,1,0:T(8,128)(2,1)S(1)}, u32[]{:S(2)}, u32[]{:S(2)}) collective-permute-start(bf16[4,96,384]{2,1,0:T(8,128)(2,1)S(1)} %get-tuple-element.41), channel_id=1, source_target_pairs={{0,2},{1,3},{2,0},{3,1},{4,6},{5,7},{6,4},{7,5},{8,12},{9,13},{10,... | collective-permute-start | bytes 884744 | tf_op jit(solution)/shard_map/ppermute | solution.py:544
  39.3 2.7 %collective-permute-start.3 = (bf16[4,96,384]{2,1,0:T(8,128)(2,1)S(1)}, bf16[4,96,384]{2,1,0:T(8,128)(2,1)S(1)}, u32[]{:S(2)}, u32[]{:S(2)}) collective-permute-start(bf16[4,96,384]{2,1,0:T(8,128)(2,1)S(1)} %get-tuple-element.42), channel_id=1, source_target_pairs={{0,3},{1,0},{2,1},{3,2},{4,7},{5,4},{6,5},{7,6},{8,28},{9,29},{10,... | collective-permute-start | bytes 884744 | tf_op jit(solution)/shard_map/ppermute | solution.py:544
  42.0 0.0 collective-permute-start.2
  42.0 0.9 %weight_kernel.3.refs_4_ = bf16[4,4,96,384]{3,2,1,0:T(8,128)(2,1)S(1)} custom-call(bf16[128,1792]{1,0:T(8,128)(2,1)S(1)} %get-tuple-element.28.refs_0_, bf16[128,1792]{1,0:T(8,128)(2,1)S(1)} %collective-permute-done.refs_5_.refs_1_, bf16[128,768]{1,0:T(8,128)(2,1)S(1)} %get-tuple-element.29.refs_1_.refs_2_, ...), custom_call_target="tpu_custom_call" | custom-call | tf_op jit(solution)/shard_map/weight_kernel/pallas_call | solution.py:510
  42.9 0.1 slice_bitcast_fusion
  43.0 2.1 %collective-permute-start.7 = (bf16[4,96,384]{2,1,0:T(8,128)(2,1)S(1)}, bf16[4,96,384]{2,1,0:T(8,128)(2,1)S(1)}, u32[]{:S(2)}, u32[]{:S(2)}) collective-permute-start(bf16[4,96,384]{2,1,0:T(8,128)(2,1)S(1)} %get-tuple-element.38), channel_id=1, source_target_pairs={{0,2},{1,3},{2,0},{3,1},{4,6},{5,7},{6,4},{7,5},{8,12},{9,13},{10,... | collective-permute-start | bytes 884744 | tf_op jit(solution)/shard_map/ppermute | solution.py:544
  45.1 1.5 %collective-permute-start.6 = (bf16[4,96,384]{2,1,0:T(8,128)(2,1)S(1)}, bf16[4,96,384]{2,1,0:T(8,128)(2,1)S(1)}, u32[]{:S(2)}, u32[]{:S(2)}) collective-permute-start(bf16[4,96,384]{2,1,0:T(8,128)(2,1)S(1)} %get-tuple-element.39), channel_id=1, source_target_pairs={{0,3},{1,0},{2,1},{3,2},{4,7},{5,4},{6,5},{7,6},{8,28},{9,29},{10,... | collective-permute-start | bytes 884744 | tf_op jit(solution)/shard_map/ppermute | solution.py:544
  46.6 0.2 collective-permute-done.4.refs_3_
  46.7 1.0 %collective-permute-start.5 = (bf16[4,96,384]{2,1,0:T(8,128)(2,1)S(1)}, bf16[4,96,384]{2,1,0:T(8,128)(2,1)S(1)}, u32[]{:S(2)}, u32[]{:S(2)}) collective-permute-start(bf16[4,96,384]{2,1,0:T(8,128)(2,1)S(1)} %get-tuple-element.40), channel_id=1, source_target_pairs={{0,1},{1,2},{2,3},{3,0},{4,5},{5,6},{6,7},{7,4},{8,24},{9,25},{10,... | collective-permute-start | bytes 884744 | tf_op jit(solution)/shard_map/ppermute | solution.py:544
  47.7 5.1 %finish_kernel.1 = (bf16[1,128,768]{2,1,0:T(8,128)(2,1)}, bf16[1,128,768]{2,1,0:T(8,128)(2,1)}, f32[8,128]{1,0:T(8,128)S(1)}) custom-call(s32[1]{0:T(128)S(6)} %copy.10.refs_0_, bf16[128,768]{1,0:T(8,128)(2,1)S(1)} %get-tuple-element.29.refs_1_.refs_2_, bf16[768,768]{1,0:T(8,128)(2,1)} %refs_2_.3, bf16[128,2304]{1,0:T(8,128)(2,1)S(1)} %get-tuple-element.30.refs_3_, ...), custom_call_target="tpu_custom_call" | custom-call | tf_op jit(solution)/shard_map/finish_kernel/pallas_call | solution.py:510
  52.8 0.0 collective-permute-done.3.refs_2_
  52.8 0.0 collective-permute-done.2.refs_1_
  52.8 0.4 collective-permute-done.7.refs_7_
  53.1 1.9 %collective-permute-done.6.refs_6_ = bf16[4,96,384]{2,1,0:T(8,128)(2,1)S(1)} collective-permute-done((bf16[4,96,384]{2,1,0:T(8,128)(2,1)S(1)}, bf16[4,96,384]{2,1,0:T(8,128)(2,1)S(1)}, u32[]{:S(2)}, u32[]{:S(2)}) %collective-permute-start.6) | collective-permute-done | bytes 294944 | tf_op jit(solution)/shard_map/ppermute | solution.py:544
  55.1 1.2 %collective-permute-done.5.refs_5_ = bf16[4,96,384]{2,1,0:T(8,128)(2,1)S(1)} collective-permute-done((bf16[4,96,384]{2,1,0:T(8,128)(2,1)S(1)}, bf16[4,96,384]{2,1,0:T(8,128)(2,1)S(1)}, u32[]{:S(2)}, u32[]{:S(2)}) %collective-permute-start.5) | collective-permute-done | bytes 294944 | tf_op jit(solution)/shard_map/ppermute | solution.py:544
  56.3 0.3 first_sum_kernel.1.refs_0_
  56.6 2.8 %collective-permute-start.10 = (bf16[96,768]{1,0:T(8,128)(2,1)S(1)}, bf16[96,768]{1,0:T(8,128)(2,1)S(1)}, u32[]{:S(2)}, u32[]{:S(2)}) collective-permute-start(bf16[96,768]{1,0:T(8,128)(2,1)S(1)} %get-tuple-element.44), channel_id=1, source_target_pairs={{0,4},{1,5},{2,6},{3,7},{4,0},{5,1},{6,2},{7,3},{8,10},{9,11},{10,... | collective-permute-start | bytes 442376 | tf_op jit(solution)/shard_map/ppermute | solution.py:544
  59.4 0.8 collective-permute-start.9
  60.2 0.0 collective-permute-start.8
  60.2 3.1 %collective-permute-done.10.refs_3_ = bf16[96,768]{1,0:T(8,128)(2,1)S(1)} collective-permute-done((bf16[96,768]{1,0:T(8,128)(2,1)S(1)}, bf16[96,768]{1,0:T(8,128)(2,1)S(1)}, u32[]{:S(2)}, u32[]{:S(2)}) %collective-permute-start.10) | collective-permute-done | bytes 147488 | tf_op jit(solution)/shard_map/ppermute | solution.py:544
  63.4 2.4 %collective-permute-done.9.refs_2_ = bf16[96,768]{1,0:T(8,128)(2,1)S(1)} collective-permute-done((bf16[96,768]{1,0:T(8,128)(2,1)S(1)}, bf16[96,768]{1,0:T(8,128)(2,1)S(1)}, u32[]{:S(2)}, u32[]{:S(2)}) %collective-permute-start.9) | collective-permute-done | bytes 147488 | tf_op jit(solution)/shard_map/ppermute | solution.py:544
  65.8 0.0 collective-permute-done.8.refs_1_
  65.8 0.7 second_sum_kernel.1
  66.4 17.5 %all_to_all.16.refs_0_ = bf16[8,72,128]{2,1,0:T(8,128)(2,1)S(1)} all-to-all(bf16[8,72,128]{2,1,0:T(8,128)(2,1)S(1)} %second_sum_kernel.1), channel_id=1, replica_groups=mesh['z'=8,'xl'=2,'core'=2,'xh'=2,'y'=4] {'z'}, dimensions={0} | all-to-all | bytes 294912 | tf_op jit(solution)/shard_map/all_to_all | solution.py:634
  83.9 0.8 last_sum_kernel.1
  (1 shorter events, 0.0 us)
Async XLA Ops:
  6.4 13.3 %all-to-all-start = ((bf16[8,4,32,128]{3,2,1,0:T(8,128)(2,1)}), bf16[8,4,32,128]{3,2,1,0:T(8,128)(2,1)S(1)}, u32[]{:S(2)}, u32[]{:S(2)}) async-start(bf16[8,4,32,128]{3,2,1,0:T(8,128)(2,1)} %get-tuple-element.21), calls=%async_computation | async-start | bytes 524288 | tf_op jit(solution)/shard_map/all_to_all | solution.py:564
  17.7 1.2 %copy-start = (f32[4,128,768]{2,1,0:T(8,128)}, f32[4,128,768]{2,1,0:T(8,128)S(1)}, u32[]{:S(2)}) copy-start(f32[4,128,768]{2,1,0:T(8,128)S(1)} %get-tuple-element.27.refs_4_) | copy-start | bytes 4718596
  18.8 15.1 %collective-permute-start = (bf16[128,1792]{1,0:T(8,128)(2,1)S(1)}, bf16[128,1792]{1,0:T(8,128)(2,1)S(1)}, u32[]{:S(2)}, u32[]{:S(2)}) collective-permute-start(bf16[128,1792]{1,0:T(8,128)(2,1)S(1)} %get-tuple-element.28.refs_0_), channel_id=1, source_target_pairs={{0,8},{8,0},{1,9},{9,1},{2,10},{10,2},{3,11},{11,3},{4,12},{12,4},... | collective-permute-start | bytes 1376264 | tf_op jit(solution)/shard_map/ppermute | solution.py:532
  19.7 14.2 %copy-start.1 = (f32[4,128,768]{2,1,0:T(8,128)S(1)}, f32[4,128,768]{2,1,0:T(8,128)}, u32[]{:S(2)}) copy-start(f32[4,128,768]{2,1,0:T(8,128)} %copy-done) | copy-start | bytes 4718596
  35.4 2.0 %collective-permute-start.1 = (bf16[128,2048]{1,0:T(8,128)(2,1)S(1)}, bf16[128,2048]{1,0:T(8,128)(2,1)S(1)}, u32[]{:S(2)}, u32[]{:S(2)}) collective-permute-start(bf16[128,2048]{1,0:T(8,128)(2,1)S(1)} %get-tuple-element.33), channel_id=1, source_target_pairs={{0,8},{8,0},{1,9},{9,1},{2,10},{10,2},{3,11},{11,3},{4,12},{12,4},... | collective-permute-start | bytes 1572872 | tf_op jit(solution)/shard_map/ppermute | solution.py:532
  38.4 8.3 %collective-permute-start.4 = (bf16[4,96,384]{2,1,0:T(8,128)(2,1)S(1)}, bf16[4,96,384]{2,1,0:T(8,128)(2,1)S(1)}, u32[]{:S(2)}, u32[]{:S(2)}) collective-permute-start(bf16[4,96,384]{2,1,0:T(8,128)(2,1)S(1)} %get-tuple-element.41), channel_id=1, source_target_pairs={{0,2},{1,3},{2,0},{3,1},{4,6},{5,7},{6,4},{7,5},{8,12},{9,13},{10,... | collective-permute-start | bytes 884744 | tf_op jit(solution)/shard_map/ppermute | solution.py:544
  39.3 13.4 %collective-permute-start.3 = (bf16[4,96,384]{2,1,0:T(8,128)(2,1)S(1)}, bf16[4,96,384]{2,1,0:T(8,128)(2,1)S(1)}, u32[]{:S(2)}, u32[]{:S(2)}) collective-permute-start(bf16[4,96,384]{2,1,0:T(8,128)(2,1)S(1)} %get-tuple-element.42), channel_id=1, source_target_pairs={{0,3},{1,0},{2,1},{3,2},{4,7},{5,4},{6,5},{7,6},{8,28},{9,29},{10,... | collective-permute-start | bytes 884744 | tf_op jit(solution)/shard_map/ppermute | solution.py:544
  42.0 10.7 %collective-permute-start.2 = (bf16[4,96,384]{2,1,0:T(8,128)(2,1)S(1)}, bf16[4,96,384]{2,1,0:T(8,128)(2,1)S(1)}, u32[]{:S(2)}, u32[]{:S(2)}) collective-permute-start(bf16[4,96,384]{2,1,0:T(8,128)(2,1)S(1)} %get-tuple-element.43), channel_id=1, source_target_pairs={{0,1},{1,2},{2,3},{3,0},{4,5},{5,6},{6,7},{7,4},{8,24},{9,25},{10,... | collective-permute-start | bytes 884744 | tf_op jit(solution)/shard_map/ppermute | solution.py:544
  43.0 10.2 %collective-permute-start.7 = (bf16[4,96,384]{2,1,0:T(8,128)(2,1)S(1)}, bf16[4,96,384]{2,1,0:T(8,128)(2,1)S(1)}, u32[]{:S(2)}, u32[]{:S(2)}) collective-permute-start(bf16[4,96,384]{2,1,0:T(8,128)(2,1)S(1)} %get-tuple-element.38), channel_id=1, source_target_pairs={{0,2},{1,3},{2,0},{3,1},{4,6},{5,7},{6,4},{7,5},{8,12},{9,13},{10,... | collective-permute-start | bytes 884744 | tf_op jit(solution)/shard_map/ppermute | solution.py:544
  45.1 10.0 %collective-permute-start.6 = (bf16[4,96,384]{2,1,0:T(8,128)(2,1)S(1)}, bf16[4,96,384]{2,1,0:T(8,128)(2,1)S(1)}, u32[]{:S(2)}, u32[]{:S(2)}) collective-permute-start(bf16[4,96,384]{2,1,0:T(8,128)(2,1)S(1)} %get-tuple-element.39), channel_id=1, source_target_pairs={{0,3},{1,0},{2,1},{3,2},{4,7},{5,4},{6,5},{7,6},{8,28},{9,29},{10,... | collective-permute-start | bytes 884744 | tf_op jit(solution)/shard_map/ppermute | solution.py:544
  46.7 9.6 %collective-permute-start.5 = (bf16[4,96,384]{2,1,0:T(8,128)(2,1)S(1)}, bf16[4,96,384]{2,1,0:T(8,128)(2,1)S(1)}, u32[]{:S(2)}, u32[]{:S(2)}) collective-permute-start(bf16[4,96,384]{2,1,0:T(8,128)(2,1)S(1)} %get-tuple-element.40), channel_id=1, source_target_pairs={{0,1},{1,2},{2,3},{3,0},{4,5},{5,6},{6,7},{7,4},{8,24},{9,25},{10,... | collective-permute-start | bytes 884744 | tf_op jit(solution)/shard_map/ppermute | solution.py:544
  56.6 6.7 %collective-permute-start.10 = (bf16[96,768]{1,0:T(8,128)(2,1)S(1)}, bf16[96,768]{1,0:T(8,128)(2,1)S(1)}, u32[]{:S(2)}, u32[]{:S(2)}) collective-permute-start(bf16[96,768]{1,0:T(8,128)(2,1)S(1)} %get-tuple-element.44), channel_id=1, source_target_pairs={{0,4},{1,5},{2,6},{3,7},{4,0},{5,1},{6,2},{7,3},{8,10},{9,11},{10,... | collective-permute-start | bytes 442376 | tf_op jit(solution)/shard_map/ppermute | solution.py:544
  59.4 6.4 %collective-permute-start.9 = (bf16[96,768]{1,0:T(8,128)(2,1)S(1)}, bf16[96,768]{1,0:T(8,128)(2,1)S(1)}, u32[]{:S(2)}, u32[]{:S(2)}) collective-permute-start(bf16[96,768]{1,0:T(8,128)(2,1)S(1)} %get-tuple-element.45), channel_id=1, source_target_pairs={{0,20},{1,21},{2,22},{3,23},{4,16},{5,17},{6,18},{7,19},{8,11},{9,... | collective-permute-start | bytes 442376 | tf_op jit(solution)/shard_map/ppermute | solution.py:544
  60.2 5.5 %collective-permute-start.8 = (bf16[96,768]{1,0:T(8,128)(2,1)S(1)}, bf16[96,768]{1,0:T(8,128)(2,1)S(1)}, u32[]{:S(2)}, u32[]{:S(2)}) collective-permute-start(bf16[96,768]{1,0:T(8,128)(2,1)S(1)} %get-tuple-element.46), channel_id=1, source_target_pairs={{0,16},{1,17},{2,18},{3,19},{4,20},{5,21},{6,22},{7,23},{8,9},{9,1... | collective-permute-start | bytes 442376 | tf_op jit(solution)/shard_map/ppermute | solution.py:544

commit v5 on v4

--- a/solution.py
+++ b/solution.py
@@ -413,8 +413,8 @@
         for s in range(N_SEG):
             x_rel = 2 * ((s // 4 + xh) % 2) + (to_xl + xl) % 2
             y_rel = (s % 4 - y + 4) % 4
-            first = jnp.where(core == 0, y_rel, x_rel)
-            second = jnp.where(core == 0, x_rel, y_rel)
+            first = jnp.where(core == 1, y_rel, x_rel)
+            second = jnp.where(core == 1, x_rel, y_rel)
             out_ref[first, second] = total[BLOCK * s : BLOCK * (s + 1)]
 
 
@@ -536,7 +536,7 @@
     pairs = []
     for i in range(32):
         xl, core, xh, y = i // 16, (i // 8) % 2, (i // 4) % 2, i % 4
-        if core == stage:
+        if core != stage:
             y = (y + k) % 4
         else:
             xl, xh = xl ^ (k % 2), xh ^ (k // 2)

time: 85.3 us -> 86.4 us (1.013)
  waiting for transfers between devices: 12 us -> 13.2 us
    ppermute x9, waiting for transfers between devices: 9.19 us -> 10.4 us  [swap(): return lax.ppermute(x, ('xl', 'core', 'xh', 'y'), pairs)]
  transfers between devices with their start and end apart: 12 -> 12, of which waited for: 8 -> 6; matrix products, arithmetic and copies ran while one was open for 0% -> 0% of each run, Pallas kernels for 13% -> 13%
where the time goes in v5:
time: 86.4 us; the launch traced here: 85.8 us
  blocking collectives  30.1 us (35%)
  Pallas kernels  20.6 us (24%)
  starting transfers between devices  19.1 us (22%)
  waiting for transfers between devices  13.2 us (15%)
  between operations  1.41 us (2%)
  local copies, waits for them, and re-layouts  1.37 us (2%)
    pallas_call x10, Pallas kernels, call(): pl.pallas_call(body, out_shape=[pltpu.HBM(*out[:2]) if len(out) > 2 else...  20.6 us
    all_to_all x1, blocking collectives, per_device(): arrived = lax.all_to_all(partial, 'z', 0, 0, tiled=True)  17.5 us
    all_to_all x1, blocking collectives, per_device(): reply = lax.all_to_all(reply, ('xh', 'y'), 0, 0, tiled=True)  12.6 us
    ppermute x9, starting transfers between devices, swap(): return lax.ppermute(x, ('xl', 'core', 'xh', 'y'), pairs)  11.6 us
    ppermute x9, waiting for transfers between devices, swap(): return lax.ppermute(x, ('xl', 'core', 'xh', 'y'), pairs)  10.4 us
    all_to_all x1, starting transfers between devices, per_device(): message = lax.all_to_all(message, ('xh', 'y'), 0, 0, tiled=True)  7.44 us
    ppermute x2, waiting for transfers between devices, to_core(): return lax.ppermute(x, 'core', [(0, 1), (1, 0)])  1.9 us
  transfers between devices with their start and end apart: 12, of which 6 were waited for; matrix products, arithmetic and copies ran while one was open for 0% of the time, Pallas kernels for 13%

profile of v5, /device:TPU:6, one launch (start us, length us, event | category | flops | bytes accessed | tf_op | source)
XLA Modules:
  0.0 85.8 jit_solution(87854378981194271)
XLA Ops:
  1.3 5.2 %first_kernel.1 = (bf16[8,4,32,128]{3,2,1,0:T(8,128)(2,1)}, bf16[128,2304]{1,0:T(8,128)(2,1)S(1)}, bf16[128,768]{1,0:T(8,128)(2,1)S(1)}, f32[128,896]{1,0:T(8,128)}, bf16[128,768]{1,0:T(8,128)(2,1)}) custom-call(s32[1]{0:T(128)S(6)} %copy.10.refs_0_, s32[1,2,128]{2,1,0:T(2,128)} %bitcast.21, bf16[1,128,768]{2,1,0:T(8,128)(2,1)} %refs_2_.2, ...), custom_call_target="tpu_custom_call" | custom-call | tf_op jit(solution)/shard_map/first_kernel/pallas_call | solution.py:510
  6.4 7.4 %all-to-all-start = ((bf16[8,4,32,128]{3,2,1,0:T(8,128)(2,1)}), bf16[8,4,32,128]{3,2,1,0:T(8,128)(2,1)S(1)}, u32[]{:S(2)}, u32[]{:S(2)}) async-start(bf16[8,4,32,128]{3,2,1,0:T(8,128)(2,1)} %get-tuple-element.21), calls=%async_computation | async-start | bytes 524288 | tf_op jit(solution)/shard_map/all_to_all | solution.py:564
  13.9 3.8 %dense_kernel.1 = (f32[4,128,768]{2,1,0:T(8,128)S(1)}, f32[2,2,256,128]{3,2,1,0:T(8,128)S(1)}, bf16[128,1792]{1,0:T(8,128)(2,1)S(1)}) custom-call(s32[1]{0:T(128)S(6)} %copy.10.refs_0_, bf16[128,2304]{1,0:T(8,128)(2,1)S(1)} %get-tuple-element.22.refs_1_, bf16[128,768]{1,0:T(8,128)(2,1)S(1)} %get-tuple-element.23.refs_2_, ...), custom_call_target="tpu_custom_call" | custom-call | tf_op jit(solution)/shard_map/dense_kernel/pallas_call | solution.py:510
  17.7 0.0 copy-start
  17.7 1.2 %copy-done = f32[4,128,768]{2,1,0:T(8,128)} copy-done((f32[4,128,768]{2,1,0:T(8,128)}, f32[4,128,768]{2,1,0:T(8,128)S(1)}, u32[]{:S(2)}) %copy-start) | copy-done | bytes 1572888
  18.8 0.0 collective-permute-start
  18.8 0.9 %all-to-all-done.refs_1_ = bf16[8,4,32,128]{3,2,1,0:T(8,128)(2,1)S(1)} async-done(((bf16[8,4,32,128]{3,2,1,0:T(8,128)(2,1)}), bf16[8,4,32,128]{3,2,1,0:T(8,128)(2,1)S(1)}, u32[]{:S(2)}, u32[]{:S(2)}) %all-to-all-start) | async-done | bytes 262176 | tf_op jit(solution)/shard_map/all_to_all | solution.py:564
  19.7 0.0 copy-start.1
  19.7 1.6 %dilated_kernel.1 = bf16[8,4,32,128]{3,2,1,0:T(8,128)(2,1)S(1)} custom-call(s32[1]{0:T(128)S(6)} %copy.10.refs_0_, bf16[8,4,32,128]{3,2,1,0:T(8,128)(2,1)S(1)} %all-to-all-done.refs_1_, f32[2,2,256,128]{3,2,1,0:T(8,128)S(1)} %get-tuple-element.26.refs_2_.refs_3_), custom_call_target="tpu_custom_call" | custom-call | tf_op jit(solution)/shard_map/dilated_kernel/pallas_call | solution.py:510
  21.3 12.6 %all_to_all.15.refs_0_ = bf16[8,4,32,128]{3,2,1,0:T(8,128)(2,1)S(1)} all-to-all(bf16[8,4,32,128]{3,2,1,0:T(8,128)(2,1)S(1)} %dilated_kernel.1), channel_id=1, replica_groups=mesh['z'=8,'xl'=2,'core'=2,'xh'=2,'y'=4] {'xh','y'}, dimensions={0} | all-to-all | bytes 524288 | tf_op jit(solution)/shard_map/all_to_all | solution.py:585
  33.9 0.0 collective-permute-done.refs_5_.refs_1_
  33.9 0.0 copy-done.1
  33.9 1.5 %join_kernel.1 = (bf16[128,768]{1,0:T(8,128)(2,1)S(1)}, bf16[128,2304]{1,0:T(8,128)(2,1)S(1)}, bf16[128,1280]{1,0:T(8,128)(2,1)S(1)}, bf16[128,2048]{1,0:T(8,128)(2,1)S(1)}) custom-call(bf16[8,4,32,128]{3,2,1,0:T(8,128)(2,1)S(1)} %all_to_all.15.refs_0_, bf16[128,2304]{1,0:T(8,128)(2,1)S(1)} %get-tuple-element.22.refs_1_, ...), custom_call_target="tpu_custom_call" | custom-call | tf_op jit(solution)/shard_map/join_kernel/pallas_call | solution.py:510
  35.4 0.1 collective-permute-start.1
  35.5 1.9 %collective-permute-done.1.refs_3_ = bf16[128,2048]{1,0:T(8,128)(2,1)S(1)} collective-permute-done((bf16[128,2048]{1,0:T(8,128)(2,1)S(1)}, bf16[128,2048]{1,0:T(8,128)(2,1)S(1)}, u32[]{:S(2)}, u32[]{:S(2)}) %collective-permute-start.1) | collective-permute-done | bytes 524320 | tf_op jit(solution)/shard_map/ppermute | solution.py:532
  37.4 0.9 weight_kernel.2.refs_0_
  38.3 0.1 slice_bitcast_fusion.3
  38.4 2.9 %collective-permute-start.4 = (bf16[4,96,384]{2,1,0:T(8,128)(2,1)S(1)}, bf16[4,96,384]{2,1,0:T(8,128)(2,1)S(1)}, u32[]{:S(2)}, u32[]{:S(2)}) collective-permute-start(bf16[4,96,384]{2,1,0:T(8,128)(2,1)S(1)} %get-tuple-element.41), channel_id=1, source_target_pairs={{0,4},{1,5},{2,6},{3,7},{4,0},{5,1},{6,2},{7,3},{8,10},{9,11},{10,... | collective-permute-start | bytes 884744 | tf_op jit(solution)/shard_map/ppermute | solution.py:544
  41.3 0.7 collective-permute-start.3
  42.0 0.1 collective-permute-start.2
  42.1 0.9 weight_kernel.3.refs_4_
  43.0 0.1 slice_bitcast_fusion
  43.1 4.0 %collective-permute-start.7 = (bf16[4,96,384]{2,1,0:T(8,128)(2,1)S(1)}, bf16[4,96,384]{2,1,0:T(8,128)(2,1)S(1)}, u32[]{:S(2)}, u32[]{:S(2)}) collective-permute-start(bf16[4,96,384]{2,1,0:T(8,128)(2,1)S(1)} %get-tuple-element.38), channel_id=1, source_target_pairs={{0,4},{1,5},{2,6},{3,7},{4,0},{5,1},{6,2},{7,3},{8,10},{9,11},{10,... | collective-permute-start | bytes 884744 | tf_op jit(solution)/shard_map/ppermute | solution.py:544
  47.0 0.7 collective-permute-start.6
  47.8 0.0 collective-permute-done.4.refs_3_
  47.8 0.0 collective-permute-start.5
  47.8 5.1 %finish_kernel.1 = (bf16[1,128,768]{2,1,0:T(8,128)(2,1)}, bf16[1,128,768]{2,1,0:T(8,128)(2,1)}, f32[8,128]{1,0:T(8,128)S(1)}) custom-call(s32[1]{0:T(128)S(6)} %copy.10.refs_0_, bf16[128,768]{1,0:T(8,128)(2,1)S(1)} %get-tuple-element.29.refs_1_.refs_2_, bf16[768,768]{1,0:T(8,128)(2,1)} %refs_2_.3, bf16[128,2304]{1,0:T(8,128)(2,1)S(1)} %get-tuple-element.30.refs_3_, ...), custom_call_target="tpu_custom_call" | custom-call | tf_op jit(solution)/shard_map/finish_kernel/pallas_call | solution.py:510
  52.9 0.0 collective-permute-done.3.refs_2_
  52.9 0.0 collective-permute-done.2.refs_1_
  52.9 1.0 %collective-permute-done.7.refs_7_ = bf16[4,96,384]{2,1,0:T(8,128)(2,1)S(1)} collective-permute-done((bf16[4,96,384]{2,1,0:T(8,128)(2,1)S(1)}, bf16[4,96,384]{2,1,0:T(8,128)(2,1)S(1)}, u32[]{:S(2)}, u32[]{:S(2)}) %collective-permute-start.7) | collective-permute-done | bytes 294944 | tf_op jit(solution)/shard_map/ppermute | solution.py:544
  53.9 3.1 %collective-permute-done.6.refs_6_ = bf16[4,96,384]{2,1,0:T(8,128)(2,1)S(1)} collective-permute-done((bf16[4,96,384]{2,1,0:T(8,128)(2,1)S(1)}, bf16[4,96,384]{2,1,0:T(8,128)(2,1)S(1)}, u32[]{:S(2)}, u32[]{:S(2)}) %collective-permute-start.6) | collective-permute-done | bytes 294944 | tf_op jit(solution)/shard_map/ppermute | solution.py:544
  57.0 0.0 collective-permute-done.5.refs_5_
  57.0 0.3 first_sum_kernel.1.refs_0_
  57.3 1.1 %collective-permute-start.10 = (bf16[96,768]{1,0:T(8,128)(2,1)S(1)}, bf16[96,768]{1,0:T(8,128)(2,1)S(1)}, u32[]{:S(2)}, u32[]{:S(2)}) collective-permute-start(bf16[96,768]{1,0:T(8,128)(2,1)S(1)} %get-tuple-element.44), channel_id=1, source_target_pairs={{0,2},{1,3},{2,0},{3,1},{4,6},{5,7},{6,4},{7,5},{8,12},{9,13},{10,... | collective-permute-start | bytes 442376 | tf_op jit(solution)/shard_map/ppermute | solution.py:544
  58.5 2.0 %collective-permute-start.9 = (bf16[96,768]{1,0:T(8,128)(2,1)S(1)}, bf16[96,768]{1,0:T(8,128)(2,1)S(1)}, u32[]{:S(2)}, u32[]{:S(2)}) collective-permute-start(bf16[96,768]{1,0:T(8,128)(2,1)S(1)} %get-tuple-element.45), channel_id=1, source_target_pairs={{0,3},{1,0},{2,1},{3,2},{4,7},{5,4},{6,5},{7,6},{8,28},{9,29},{10,... | collective-permute-start | bytes 442376 | tf_op jit(solution)/shard_map/ppermute | solution.py:544
  60.4 0.1 collective-permute-start.8
  60.5 3.6 %collective-permute-done.10.refs_3_ = bf16[96,768]{1,0:T(8,128)(2,1)S(1)} collective-permute-done((bf16[96,768]{1,0:T(8,128)(2,1)S(1)}, bf16[96,768]{1,0:T(8,128)(2,1)S(1)}, u32[]{:S(2)}, u32[]{:S(2)}) %collective-permute-start.10) | collective-permute-done | bytes 147488 | tf_op jit(solution)/shard_map/ppermute | solution.py:544
  64.1 0.0 collective-permute-done.9.refs_2_
  64.1 2.7 %collective-permute-done.8.refs_1_ = bf16[96,768]{1,0:T(8,128)(2,1)S(1)} collective-permute-done((bf16[96,768]{1,0:T(8,128)(2,1)S(1)}, bf16[96,768]{1,0:T(8,128)(2,1)S(1)}, u32[]{:S(2)}, u32[]{:S(2)}) %collective-permute-start.8) | collective-permute-done | bytes 147488 | tf_op jit(solution)/shard_map/ppermute | solution.py:544
  66.8 0.7 second_sum_kernel.1
  67.5 17.5 %all_to_all.16.refs_0_ = bf16[8,72,128]{2,1,0:T(8,128)(2,1)S(1)} all-to-all(bf16[8,72,128]{2,1,0:T(8,128)(2,1)S(1)} %second_sum_kernel.1), channel_id=1, replica_groups=mesh['z'=8,'xl'=2,'core'=2,'xh'=2,'y'=4] {'z'}, dimensions={0} | all-to-all | bytes 294912 | tf_op jit(solution)/shard_map/all_to_all | solution.py:634
  85.0 0.8 last_sum_kernel.1
  (1 shorter events, 0.0 us)
Async XLA Ops:
  6.4 13.3 %all-to-all-start = ((bf16[8,4,32,128]{3,2,1,0:T(8,128)(2,1)}), bf16[8,4,32,128]{3,2,1,0:T(8,128)(2,1)S(1)}, u32[]{:S(2)}, u32[]{:S(2)}) async-start(bf16[8,4,32,128]{3,2,1,0:T(8,128)(2,1)} %get-tuple-element.21), calls=%async_computation | async-start | bytes 524288 | tf_op jit(solution)/shard_map/all_to_all | solution.py:564
  17.7 1.2 %copy-start = (f32[4,128,768]{2,1,0:T(8,128)}, f32[4,128,768]{2,1,0:T(8,128)S(1)}, u32[]{:S(2)}) copy-start(f32[4,128,768]{2,1,0:T(8,128)S(1)} %get-tuple-element.27.refs_4_) | copy-start | bytes 4718596
  18.8 15.1 %collective-permute-start = (bf16[128,1792]{1,0:T(8,128)(2,1)S(1)}, bf16[128,1792]{1,0:T(8,128)(2,1)S(1)}, u32[]{:S(2)}, u32[]{:S(2)}) collective-permute-start(bf16[128,1792]{1,0:T(8,128)(2,1)S(1)} %get-tuple-element.28.refs_0_), channel_id=1, source_target_pairs={{0,8},{8,0},{1,9},{9,1},{2,10},{10,2},{3,11},{11,3},{4,12},{12,4},... | collective-permute-start | bytes 1376264 | tf_op jit(solution)/shard_map/ppermute | solution.py:532
  19.7 14.2 %copy-start.1 = (f32[4,128,768]{2,1,0:T(8,128)S(1)}, f32[4,128,768]{2,1,0:T(8,128)}, u32[]{:S(2)}) copy-start(f32[4,128,768]{2,1,0:T(8,128)} %copy-done) | copy-start | bytes 4718596
  35.4 2.0 %collective-permute-start.1 = (bf16[128,2048]{1,0:T(8,128)(2,1)S(1)}, bf16[128,2048]{1,0:T(8,128)(2,1)S(1)}, u32[]{:S(2)}, u32[]{:S(2)}) collective-permute-start(bf16[128,2048]{1,0:T(8,128)(2,1)S(1)} %get-tuple-element.33), channel_id=1, source_target_pairs={{0,8},{8,0},{1,9},{9,1},{2,10},{10,2},{3,11},{11,3},{4,12},{12,4},... | collective-permute-start | bytes 1572872 | tf_op jit(solution)/shard_map/ppermute | solution.py:532
  38.4 9.3 %collective-permute-start.4 = (bf16[4,96,384]{2,1,0:T(8,128)(2,1)S(1)}, bf16[4,96,384]{2,1,0:T(8,128)(2,1)S(1)}, u32[]{:S(2)}, u32[]{:S(2)}) collective-permute-start(bf16[4,96,384]{2,1,0:T(8,128)(2,1)S(1)} %get-tuple-element.41), channel_id=1, source_target_pairs={{0,4},{1,5},{2,6},{3,7},{4,0},{5,1},{6,2},{7,3},{8,10},{9,11},{10,... | collective-permute-start | bytes 884744 | tf_op jit(solution)/shard_map/ppermute | solution.py:544
  41.3 11.6 %collective-permute-start.3 = (bf16[4,96,384]{2,1,0:T(8,128)(2,1)S(1)}, bf16[4,96,384]{2,1,0:T(8,128)(2,1)S(1)}, u32[]{:S(2)}, u32[]{:S(2)}) collective-permute-start(bf16[4,96,384]{2,1,0:T(8,128)(2,1)S(1)} %get-tuple-element.42), channel_id=1, source_target_pairs={{0,20},{1,21},{2,22},{3,23},{4,16},{5,17},{6,18},{7,19},{8,11},{9,... | collective-permute-start | bytes 884744 | tf_op jit(solution)/shard_map/ppermute | solution.py:544
  42.0 10.9 %collective-permute-start.2 = (bf16[4,96,384]{2,1,0:T(8,128)(2,1)S(1)}, bf16[4,96,384]{2,1,0:T(8,128)(2,1)S(1)}, u32[]{:S(2)}, u32[]{:S(2)}) collective-permute-start(bf16[4,96,384]{2,1,0:T(8,128)(2,1)S(1)} %get-tuple-element.43), channel_id=1, source_target_pairs={{0,16},{1,17},{2,18},{3,19},{4,20},{5,21},{6,22},{7,23},{8,9},{9,1... | collective-permute-start | bytes 884744 | tf_op jit(solution)/shard_map/ppermute | solution.py:544
  43.1 10.9 %collective-permute-start.7 = (bf16[4,96,384]{2,1,0:T(8,128)(2,1)S(1)}, bf16[4,96,384]{2,1,0:T(8,128)(2,1)S(1)}, u32[]{:S(2)}, u32[]{:S(2)}) collective-permute-start(bf16[4,96,384]{2,1,0:T(8,128)(2,1)S(1)} %get-tuple-element.38), channel_id=1, source_target_pairs={{0,4},{1,5},{2,6},{3,7},{4,0},{5,1},{6,2},{7,3},{8,10},{9,11},{10,... | collective-permute-start | bytes 884744 | tf_op jit(solution)/shard_map/ppermute | solution.py:544
  47.0 10.0 %collective-permute-start.6 = (bf16[4,96,384]{2,1,0:T(8,128)(2,1)S(1)}, bf16[4,96,384]{2,1,0:T(8,128)(2,1)S(1)}, u32[]{:S(2)}, u32[]{:S(2)}) collective-permute-start(bf16[4,96,384]{2,1,0:T(8,128)(2,1)S(1)} %get-tuple-element.39), channel_id=1, source_target_pairs={{0,20},{1,21},{2,22},{3,23},{4,16},{5,17},{6,18},{7,19},{8,11},{9,... | collective-permute-start | bytes 884744 | tf_op jit(solution)/shard_map/ppermute | solution.py:544
  47.8 9.2 %collective-permute-start.5 = (bf16[4,96,384]{2,1,0:T(8,128)(2,1)S(1)}, bf16[4,96,384]{2,1,0:T(8,128)(2,1)S(1)}, u32[]{:S(2)}, u32[]{:S(2)}) collective-permute-start(bf16[4,96,384]{2,1,0:T(8,128)(2,1)S(1)} %get-tuple-element.40), channel_id=1, source_target_pairs={{0,16},{1,17},{2,18},{3,19},{4,20},{5,21},{6,22},{7,23},{8,9},{9,1... | collective-permute-start | bytes 884744 | tf_op jit(solution)/shard_map/ppermute | solution.py:544
  57.3 6.7 %collective-permute-start.10 = (bf16[96,768]{1,0:T(8,128)(2,1)S(1)}, bf16[96,768]{1,0:T(8,128)(2,1)S(1)}, u32[]{:S(2)}, u32[]{:S(2)}) collective-permute-start(bf16[96,768]{1,0:T(8,128)(2,1)S(1)} %get-tuple-element.44), channel_id=1, source_target_pairs={{0,2},{1,3},{2,0},{3,1},{4,6},{5,7},{6,4},{7,5},{8,12},{9,13},{10,... | collective-permute-start | bytes 442376 | tf_op jit(solution)/shard_map/ppermute | solution.py:544
  58.5 5.6 %collective-permute-start.9 = (bf16[96,768]{1,0:T(8,128)(2,1)S(1)}, bf16[96,768]{1,0:T(8,128)(2,1)S(1)}, u32[]{:S(2)}, u32[]{:S(2)}) collective-permute-start(bf16[96,768]{1,0:T(8,128)(2,1)S(1)} %get-tuple-element.45), channel_id=1, source_target_pairs={{0,3},{1,0},{2,1},{3,2},{4,7},{5,4},{6,5},{7,6},{8,28},{9,29},{10,... | collective-permute-start | bytes 442376 | tf_op jit(solution)/shard_map/ppermute | solution.py:544
  60.4 6.4 %collective-permute-start.8 = (bf16[96,768]{1,0:T(8,128)(2,1)S(1)}, bf16[96,768]{1,0:T(8,128)(2,1)S(1)}, u32[]{:S(2)}, u32[]{:S(2)}) collective-permute-start(bf16[96,768]{1,0:T(8,128)(2,1)S(1)} %get-tuple-element.46), channel_id=1, source_target_pairs={{0,1},{1,2},{2,3},{3,0},{4,5},{5,6},{6,7},{7,4},{8,24},{9,25},{10,... | collective-permute-start | bytes 442376 | tf_op jit(solution)/shard_map/ppermute | solution.py:544

commit v6 on v4

--- a/solution.py
+++ b/solution.py
@@ -627,7 +627,7 @@
         terms.append(("v", partial))
         terms += [("v", swap(partial[k], k, 0)) for k in (1, 3, 2)]
     (partial,) = call(first_sum_kernel, [((4, BLOCK, D), BF)], *terms, ("n", done))
-    terms = [("v", swap(partial[k], k, 1)) for k in (1, 3, 2)]
+    terms = [("v", swap(partial[k], k, 1)) for k in (3, 1, 2)]
     (partial,) = call(
         second_sum_kernel, [((8, 72, 128), BF)], ("v", partial), *terms
     )

time: 85.3 us -> 85.8 us (level)
  transfers between devices with their start and end apart: 12 -> 12, of which waited for: 8 -> 9; matrix products, arithmetic and copies ran while one was open for 0% -> 0% of each run, Pallas kernels for 13% -> 13%
where the time goes in v6:
time: 85.8 us; the launch traced here: 85.5 us
  blocking collectives  30.1 us (35%)
  Pallas kernels  20.6 us (24%)
  starting transfers between devices  19.9 us (23%)
  waiting for transfers between devices  12.2 us (14%)
  between operations  1.4 us (2%)
  local copies, waits for them, and re-layouts  1.37 us (2%)
    pallas_call x10, Pallas kernels, call(): pl.pallas_call(body, out_shape=[pltpu.HBM(*out[:2]) if len(out) > 2 else...  20.6 us
    all_to_all x1, blocking collectives, per_device(): arrived = lax.all_to_all(partial, 'z', 0, 0, tiled=True)  17.5 us
    all_to_all x1, blocking collectives, per_device(): reply = lax.all_to_all(reply, ('xh', 'y'), 0, 0, tiled=True)  12.6 us
    ppermute x9, starting transfers between devices, swap(): return lax.ppermute(x, ('xl', 'core', 'xh', 'y'), pairs)  12.3 us
    ppermute x9, waiting for transfers between devices, swap(): return lax.ppermute(x, ('xl', 'core', 'xh', 'y'), pairs)  9.44 us
    all_to_all x1, starting transfers between devices, per_device(): message = lax.all_to_all(message, ('xh', 'y'), 0, 0, tiled=True)  7.44 us
    ppermute x2, waiting for transfers between devices, to_core(): return lax.ppermute(x, 'core', [(0, 1), (1, 0)])  1.9 us
  transfers between devices with their start and end apart: 12, of which 9 were waited for; matrix products, arithmetic and copies ran while one was open for 0% of the time, Pallas kernels for 13%

profile of v6, /device:TPU:6, one launch (start us, length us, event | category | flops | bytes accessed | tf_op | source)
XLA Modules:
  0.0 85.5 jit_solution(4466205616587863040)
XLA Ops:
  1.3 5.2 %first_kernel.1 = (bf16[8,4,32,128]{3,2,1,0:T(8,128)(2,1)}, bf16[128,2304]{1,0:T(8,128)(2,1)S(1)}, bf16[128,768]{1,0:T(8,128)(2,1)S(1)}, f32[128,896]{1,0:T(8,128)}, bf16[128,768]{1,0:T(8,128)(2,1)}) custom-call(s32[1]{0:T(128)S(6)} %copy.10.refs_0_, s32[1,2,128]{2,1,0:T(2,128)} %bitcast.21, bf16[1,128,768]{2,1,0:T(8,128)(2,1)} %refs_2_.2, ...), custom_call_target="tpu_custom_call" | custom-call | tf_op jit(solution)/shard_map/first_kernel/pallas_call | solution.py:510
  6.4 7.4 %all-to-all-start = ((bf16[8,4,32,128]{3,2,1,0:T(8,128)(2,1)}), bf16[8,4,32,128]{3,2,1,0:T(8,128)(2,1)S(1)}, u32[]{:S(2)}, u32[]{:S(2)}) async-start(bf16[8,4,32,128]{3,2,1,0:T(8,128)(2,1)} %get-tuple-element.21), calls=%async_computation | async-start | bytes 524288 | tf_op jit(solution)/shard_map/all_to_all | solution.py:564
  13.9 3.8 %dense_kernel.1 = (f32[4,128,768]{2,1,0:T(8,128)S(1)}, f32[2,2,256,128]{3,2,1,0:T(8,128)S(1)}, bf16[128,1792]{1,0:T(8,128)(2,1)S(1)}) custom-call(s32[1]{0:T(128)S(6)} %copy.10.refs_0_, bf16[128,2304]{1,0:T(8,128)(2,1)S(1)} %get-tuple-element.22.refs_1_, bf16[128,768]{1,0:T(8,128)(2,1)S(1)} %get-tuple-element.23.refs_2_, ...), custom_call_target="tpu_custom_call" | custom-call | tf_op jit(solution)/shard_map/dense_kernel/pallas_call | solution.py:510
  17.7 0.0 copy-start
  17.7 1.2 %copy-done = f32[4,128,768]{2,1,0:T(8,128)} copy-done((f32[4,128,768]{2,1,0:T(8,128)}, f32[4,128,768]{2,1,0:T(8,128)S(1)}, u32[]{:S(2)}) %copy-start) | copy-done | bytes 1572888
  18.8 0.0 collective-permute-start
  18.8 0.9 %all-to-all-done.refs_1_ = bf16[8,4,32,128]{3,2,1,0:T(8,128)(2,1)S(1)} async-done(((bf16[8,4,32,128]{3,2,1,0:T(8,128)(2,1)}), bf16[8,4,32,128]{3,2,1,0:T(8,128)(2,1)S(1)}, u32[]{:S(2)}, u32[]{:S(2)}) %all-to-all-start) | async-done | bytes 262176 | tf_op jit(solution)/shard_map/all_to_all | solution.py:564
  19.7 0.0 copy-start.1
  19.7 1.6 %dilated_kernel.1 = bf16[8,4,32,128]{3,2,1,0:T(8,128)(2,1)S(1)} custom-call(s32[1]{0:T(128)S(6)} %copy.10.refs_0_, bf16[8,4,32,128]{3,2,1,0:T(8,128)(2,1)S(1)} %all-to-all-done.refs_1_, f32[2,2,256,128]{3,2,1,0:T(8,128)S(1)} %get-tuple-element.26.refs_2_.refs_3_), custom_call_target="tpu_custom_call" | custom-call | tf_op jit(solution)/shard_map/dilated_kernel/pallas_call | solution.py:510
  21.3 12.6 %all_to_all.15.refs_0_ = bf16[8,4,32,128]{3,2,1,0:T(8,128)(2,1)S(1)} all-to-all(bf16[8,4,32,128]{3,2,1,0:T(8,128)(2,1)S(1)} %dilated_kernel.1), channel_id=1, replica_groups=mesh['z'=8,'xl'=2,'core'=2,'xh'=2,'y'=4] {'xh','y'}, dimensions={0} | all-to-all | bytes 524288 | tf_op jit(solution)/shard_map/all_to_all | solution.py:585
  33.9 0.0 collective-permute-done.refs_5_.refs_1_
  33.9 0.0 copy-done.1
  33.9 1.5 %join_kernel.1 = (bf16[128,768]{1,0:T(8,128)(2,1)S(1)}, bf16[128,2304]{1,0:T(8,128)(2,1)S(1)}, bf16[128,1280]{1,0:T(8,128)(2,1)S(1)}, bf16[128,2048]{1,0:T(8,128)(2,1)S(1)}) custom-call(bf16[8,4,32,128]{3,2,1,0:T(8,128)(2,1)S(1)} %all_to_all.15.refs_0_, bf16[128,2304]{1,0:T(8,128)(2,1)S(1)} %get-tuple-element.22.refs_1_, ...), custom_call_target="tpu_custom_call" | custom-call | tf_op jit(solution)/shard_map/join_kernel/pallas_call | solution.py:510
  35.4 0.1 collective-permute-start.1
  35.5 1.9 %collective-permute-done.1.refs_3_ = bf16[128,2048]{1,0:T(8,128)(2,1)S(1)} collective-permute-done((bf16[128,2048]{1,0:T(8,128)(2,1)S(1)}, bf16[128,2048]{1,0:T(8,128)(2,1)S(1)}, u32[]{:S(2)}, u32[]{:S(2)}) %collective-permute-start.1) | collective-permute-done | bytes 524320 | tf_op jit(solution)/shard_map/ppermute | solution.py:532
  37.4 0.9 %weight_kernel.2.refs_0_ = bf16[4,4,96,384]{3,2,1,0:T(8,128)(2,1)S(1)} custom-call(bf16[128,1792]{1,0:T(8,128)(2,1)S(1)} %get-tuple-element.28.refs_0_, bf16[128,1792]{1,0:T(8,128)(2,1)S(1)} %collective-permute-done.refs_5_.refs_1_, bf16[128,768]{1,0:T(8,128)(2,1)S(1)} %get-tuple-element.29.refs_1_.refs_2_, ...), custom_call_target="tpu_custom_call" | custom-call | tf_op jit(solution)/shard_map/weight_kernel/pallas_call | solution.py:510
  38.3 0.1 slice_bitcast_fusion.3
  38.4 0.9 %collective-permute-start.4 = (bf16[4,96,384]{2,1,0:T(8,128)(2,1)S(1)}, bf16[4,96,384]{2,1,0:T(8,128)(2,1)S(1)}, u32[]{:S(2)}, u32[]{:S(2)}) collective-permute-start(bf16[4,96,384]{2,1,0:T(8,128)(2,1)S(1)} %get-tuple-element.41), channel_id=1, source_target_pairs={{0,2},{1,3},{2,0},{3,1},{4,6},{5,7},{6,4},{7,5},{8,12},{9,13},{10,... | collective-permute-start | bytes 884744 | tf_op jit(solution)/shard_map/ppermute | solution.py:544
  39.3 2.7 %collective-permute-start.3 = (bf16[4,96,384]{2,1,0:T(8,128)(2,1)S(1)}, bf16[4,96,384]{2,1,0:T(8,128)(2,1)S(1)}, u32[]{:S(2)}, u32[]{:S(2)}) collective-permute-start(bf16[4,96,384]{2,1,0:T(8,128)(2,1)S(1)} %get-tuple-element.42), channel_id=1, source_target_pairs={{0,3},{1,0},{2,1},{3,2},{4,7},{5,4},{6,5},{7,6},{8,28},{9,29},{10,... | collective-permute-start | bytes 884744 | tf_op jit(solution)/shard_map/ppermute | solution.py:544
  42.0 0.0 collective-permute-start.2
  42.0 0.9 %weight_kernel.3.refs_4_ = bf16[4,4,96,384]{3,2,1,0:T(8,128)(2,1)S(1)} custom-call(bf16[128,1792]{1,0:T(8,128)(2,1)S(1)} %get-tuple-element.28.refs_0_, bf16[128,1792]{1,0:T(8,128)(2,1)S(1)} %collective-permute-done.refs_5_.refs_1_, bf16[128,768]{1,0:T(8,128)(2,1)S(1)} %get-tuple-element.29.refs_1_.refs_2_, ...), custom_call_target="tpu_custom_call" | custom-call | tf_op jit(solution)/shard_map/weight_kernel/pallas_call | solution.py:510
  42.9 0.1 slice_bitcast_fusion
  43.0 2.1 %collective-permute-start.7 = (bf16[4,96,384]{2,1,0:T(8,128)(2,1)S(1)}, bf16[4,96,384]{2,1,0:T(8,128)(2,1)S(1)}, u32[]{:S(2)}, u32[]{:S(2)}) collective-permute-start(bf16[4,96,384]{2,1,0:T(8,128)(2,1)S(1)} %get-tuple-element.38), channel_id=1, source_target_pairs={{0,2},{1,3},{2,0},{3,1},{4,6},{5,7},{6,4},{7,5},{8,12},{9,13},{10,... | collective-permute-start | bytes 884744 | tf_op jit(solution)/shard_map/ppermute | solution.py:544
  45.1 1.5 %collective-permute-start.6 = (bf16[4,96,384]{2,1,0:T(8,128)(2,1)S(1)}, bf16[4,96,384]{2,1,0:T(8,128)(2,1)S(1)}, u32[]{:S(2)}, u32[]{:S(2)}) collective-permute-start(bf16[4,96,384]{2,1,0:T(8,128)(2,1)S(1)} %get-tuple-element.39), channel_id=1, source_target_pairs={{0,3},{1,0},{2,1},{3,2},{4,7},{5,4},{6,5},{7,6},{8,28},{9,29},{10,... | collective-permute-start | bytes 884744 | tf_op jit(solution)/shard_map/ppermute | solution.py:544
  46.6 0.2 collective-permute-done.4.refs_3_
  46.7 1.0 %collective-permute-start.5 = (bf16[4,96,384]{2,1,0:T(8,128)(2,1)S(1)}, bf16[4,96,384]{2,1,0:T(8,128)(2,1)S(1)}, u32[]{:S(2)}, u32[]{:S(2)}) collective-permute-start(bf16[4,96,384]{2,1,0:T(8,128)(2,1)S(1)} %get-tuple-element.40), channel_id=1, source_target_pairs={{0,1},{1,2},{2,3},{3,0},{4,5},{5,6},{6,7},{7,4},{8,24},{9,25},{10,... | collective-permute-start | bytes 884744 | tf_op jit(solution)/shard_map/ppermute | solution.py:544
  47.7 5.1 %finish_kernel.1 = (bf16[1,128,768]{2,1,0:T(8,128)(2,1)}, bf16[1,128,768]{2,1,0:T(8,128)(2,1)}, f32[8,128]{1,0:T(8,128)S(1)}) custom-call(s32[1]{0:T(128)S(6)} %copy.10.refs_0_, bf16[128,768]{1,0:T(8,128)(2,1)S(1)} %get-tuple-element.29.refs_1_.refs_2_, bf16[768,768]{1,0:T(8,128)(2,1)} %refs_2_.3, bf16[128,2304]{1,0:T(8,128)(2,1)S(1)} %get-tuple-element.30.refs_3_, ...), custom_call_target="tpu_custom_call" | custom-call | tf_op jit(solution)/shard_map/finish_kernel/pallas_call | solution.py:510
  52.8 0.0 collective-permute-done.3.refs_2_
  52.8 0.0 collective-permute-done.2.refs_1_
  52.8 0.4 collective-permute-done.7.refs_7_
  53.1 1.9 %collective-permute-done.6.refs_6_ = bf16[4,96,384]{2,1,0:T(8,128)(2,1)S(1)} collective-permute-done((bf16[4,96,384]{2,1,0:T(8,128)(2,1)S(1)}, bf16[4,96,384]{2,1,0:T(8,128)(2,1)S(1)}, u32[]{:S(2)}, u32[]{:S(2)}) %collective-permute-start.6) | collective-permute-done | bytes 294944 | tf_op jit(solution)/shard_map/ppermute | solution.py:544
  55.1 1.2 %collective-permute-done.5.refs_5_ = bf16[4,96,384]{2,1,0:T(8,128)(2,1)S(1)} collective-permute-done((bf16[4,96,384]{2,1,0:T(8,128)(2,1)S(1)}, bf16[4,96,384]{2,1,0:T(8,128)(2,1)S(1)}, u32[]{:S(2)}, u32[]{:S(2)}) %collective-permute-start.5) | collective-permute-done | bytes 294944 | tf_op jit(solution)/shard_map/ppermute | solution.py:544
  56.3 0.3 first_sum_kernel.1.refs_0_
  56.6 2.8 %collective-permute-start.10 = (bf16[96,768]{1,0:T(8,128)(2,1)S(1)}, bf16[96,768]{1,0:T(8,128)(2,1)S(1)}, u32[]{:S(2)}, u32[]{:S(2)}) collective-permute-start(bf16[96,768]{1,0:T(8,128)(2,1)S(1)} %get-tuple-element.44), channel_id=1, source_target_pairs={{0,4},{1,5},{2,6},{3,7},{4,0},{5,1},{6,2},{7,3},{8,10},{9,11},{10,... | collective-permute-start | bytes 442376 | tf_op jit(solution)/shard_map/ppermute | solution.py:544
  59.4 0.8 collective-permute-start.9
  60.2 0.6 collective-permute-start.8
  60.8 2.6 %collective-permute-done.10.refs_3_ = bf16[96,768]{1,0:T(8,128)(2,1)S(1)} collective-permute-done((bf16[96,768]{1,0:T(8,128)(2,1)S(1)}, bf16[96,768]{1,0:T(8,128)(2,1)S(1)}, u32[]{:S(2)}, u32[]{:S(2)}) %collective-permute-start.10) | collective-permute-done | bytes 147488 | tf_op jit(solution)/shard_map/ppermute | solution.py:544
  63.4 1.6 %collective-permute-done.9.refs_2_ = bf16[96,768]{1,0:T(8,128)(2,1)S(1)} collective-permute-done((bf16[96,768]{1,0:T(8,128)(2,1)S(1)}, bf16[96,768]{1,0:T(8,128)(2,1)S(1)}, u32[]{:S(2)}, u32[]{:S(2)}) %collective-permute-start.9) | collective-permute-done | bytes 147488 | tf_op jit(solution)/shard_map/ppermute | solution.py:544
  64.9 1.7 %collective-permute-done.8.refs_1_ = bf16[96,768]{1,0:T(8,128)(2,1)S(1)} collective-permute-done((bf16[96,768]{1,0:T(8,128)(2,1)S(1)}, bf16[96,768]{1,0:T(8,128)(2,1)S(1)}, u32[]{:S(2)}, u32[]{:S(2)}) %collective-permute-start.8) | collective-permute-done | bytes 147488 | tf_op jit(solution)/shard_map/ppermute | solution.py:544
  66.6 0.7 second_sum_kernel.1
  67.3 17.5 %all_to_all.16.refs_0_ = bf16[8,72,128]{2,1,0:T(8,128)(2,1)S(1)} all-to-all(bf16[8,72,128]{2,1,0:T(8,128)(2,1)S(1)} %second_sum_kernel.1), channel_id=1, replica_groups=mesh['z'=8,'xl'=2,'core'=2,'xh'=2,'y'=4] {'z'}, dimensions={0} | all-to-all | bytes 294912 | tf_op jit(solution)/shard_map/all_to_all | solution.py:634
  84.8 0.8 last_sum_kernel.1
  (1 shorter events, 0.0 us)
Async XLA Ops:
  6.4 13.3 %all-to-all-start = ((bf16[8,4,32,128]{3,2,1,0:T(8,128)(2,1)}), bf16[8,4,32,128]{3,2,1,0:T(8,128)(2,1)S(1)}, u32[]{:S(2)}, u32[]{:S(2)}) async-start(bf16[8,4,32,128]{3,2,1,0:T(8,128)(2,1)} %get-tuple-element.21), calls=%async_computation | async-start | bytes 524288 | tf_op jit(solution)/shard_map/all_to_all | solution.py:564
  17.7 1.2 %copy-start = (f32[4,128,768]{2,1,0:T(8,128)}, f32[4,128,768]{2,1,0:T(8,128)S(1)}, u32[]{:S(2)}) copy-start(f32[4,128,768]{2,1,0:T(8,128)S(1)} %get-tuple-element.27.refs_4_) | copy-start | bytes 4718596
  18.8 15.1 %collective-permute-start = (bf16[128,1792]{1,0:T(8,128)(2,1)S(1)}, bf16[128,1792]{1,0:T(8,128)(2,1)S(1)}, u32[]{:S(2)}, u32[]{:S(2)}) collective-permute-start(bf16[128,1792]{1,0:T(8,128)(2,1)S(1)} %get-tuple-element.28.refs_0_), channel_id=1, source_target_pairs={{0,8},{8,0},{1,9},{9,1},{2,10},{10,2},{3,11},{11,3},{4,12},{12,4},... | collective-permute-start | bytes 1376264 | tf_op jit(solution)/shard_map/ppermute | solution.py:532
  19.7 14.2 %copy-start.1 = (f32[4,128,768]{2,1,0:T(8,128)S(1)}, f32[4,128,768]{2,1,0:T(8,128)}, u32[]{:S(2)}) copy-start(f32[4,128,768]{2,1,0:T(8,128)} %copy-done) | copy-start | bytes 4718596
  35.4 2.0 %collective-permute-start.1 = (bf16[128,2048]{1,0:T(8,128)(2,1)S(1)}, bf16[128,2048]{1,0:T(8,128)(2,1)S(1)}, u32[]{:S(2)}, u32[]{:S(2)}) collective-permute-start(bf16[128,2048]{1,0:T(8,128)(2,1)S(1)} %get-tuple-element.33), channel_id=1, source_target_pairs={{0,8},{8,0},{1,9},{9,1},{2,10},{10,2},{3,11},{11,3},{4,12},{12,4},... | collective-permute-start | bytes 1572872 | tf_op jit(solution)/shard_map/ppermute | solution.py:532
  38.4 8.3 %collective-permute-start.4 = (bf16[4,96,384]{2,1,0:T(8,128)(2,1)S(1)}, bf16[4,96,384]{2,1,0:T(8,128)(2,1)S(1)}, u32[]{:S(2)}, u32[]{:S(2)}) collective-permute-start(bf16[4,96,384]{2,1,0:T(8,128)(2,1)S(1)} %get-tuple-element.41), channel_id=1, source_target_pairs={{0,2},{1,3},{2,0},{3,1},{4,6},{5,7},{6,4},{7,5},{8,12},{9,13},{10,... | collective-permute-start | bytes 884744 | tf_op jit(solution)/shard_map/ppermute | solution.py:544
  39.3 13.4 %collective-permute-start.3 = (bf16[4,96,384]{2,1,0:T(8,128)(2,1)S(1)}, bf16[4,96,384]{2,1,0:T(8,128)(2,1)S(1)}, u32[]{:S(2)}, u32[]{:S(2)}) collective-permute-start(bf16[4,96,384]{2,1,0:T(8,128)(2,1)S(1)} %get-tuple-element.42), channel_id=1, source_target_pairs={{0,3},{1,0},{2,1},{3,2},{4,7},{5,4},{6,5},{7,6},{8,28},{9,29},{10,... | collective-permute-start | bytes 884744 | tf_op jit(solution)/shard_map/ppermute | solution.py:544
  42.0 10.7 %collective-permute-start.2 = (bf16[4,96,384]{2,1,0:T(8,128)(2,1)S(1)}, bf16[4,96,384]{2,1,0:T(8,128)(2,1)S(1)}, u32[]{:S(2)}, u32[]{:S(2)}) collective-permute-start(bf16[4,96,384]{2,1,0:T(8,128)(2,1)S(1)} %get-tuple-element.43), channel_id=1, source_target_pairs={{0,1},{1,2},{2,3},{3,0},{4,5},{5,6},{6,7},{7,4},{8,24},{9,25},{10,... | collective-permute-start | bytes 884744 | tf_op jit(solution)/shard_map/ppermute | solution.py:544
  43.0 10.2 %collective-permute-start.7 = (bf16[4,96,384]{2,1,0:T(8,128)(2,1)S(1)}, bf16[4,96,384]{2,1,0:T(8,128)(2,1)S(1)}, u32[]{:S(2)}, u32[]{:S(2)}) collective-permute-start(bf16[4,96,384]{2,1,0:T(8,128)(2,1)S(1)} %get-tuple-element.38), channel_id=1, source_target_pairs={{0,2},{1,3},{2,0},{3,1},{4,6},{5,7},{6,4},{7,5},{8,12},{9,13},{10,... | collective-permute-start | bytes 884744 | tf_op jit(solution)/shard_map/ppermute | solution.py:544
  45.1 10.0 %collective-permute-start.6 = (bf16[4,96,384]{2,1,0:T(8,128)(2,1)S(1)}, bf16[4,96,384]{2,1,0:T(8,128)(2,1)S(1)}, u32[]{:S(2)}, u32[]{:S(2)}) collective-permute-start(bf16[4,96,384]{2,1,0:T(8,128)(2,1)S(1)} %get-tuple-element.39), channel_id=1, source_target_pairs={{0,3},{1,0},{2,1},{3,2},{4,7},{5,4},{6,5},{7,6},{8,28},{9,29},{10,... | collective-permute-start | bytes 884744 | tf_op jit(solution)/shard_map/ppermute | solution.py:544
  46.7 9.6 %collective-permute-start.5 = (bf16[4,96,384]{2,1,0:T(8,128)(2,1)S(1)}, bf16[4,96,384]{2,1,0:T(8,128)(2,1)S(1)}, u32[]{:S(2)}, u32[]{:S(2)}) collective-permute-start(bf16[4,96,384]{2,1,0:T(8,128)(2,1)S(1)} %get-tuple-element.40), channel_id=1, source_target_pairs={{0,1},{1,2},{2,3},{3,0},{4,5},{5,6},{6,7},{7,4},{8,24},{9,25},{10,... | collective-permute-start | bytes 884744 | tf_op jit(solution)/shard_map/ppermute | solution.py:544
  56.6 6.7 %collective-permute-start.10 = (bf16[96,768]{1,0:T(8,128)(2,1)S(1)}, bf16[96,768]{1,0:T(8,128)(2,1)S(1)}, u32[]{:S(2)}, u32[]{:S(2)}) collective-permute-start(bf16[96,768]{1,0:T(8,128)(2,1)S(1)} %get-tuple-element.44), channel_id=1, source_target_pairs={{0,4},{1,5},{2,6},{3,7},{4,0},{5,1},{6,2},{7,3},{8,10},{9,11},{10,... | collective-permute-start | bytes 442376 | tf_op jit(solution)/shard_map/ppermute | solution.py:544
  59.4 5.5 %collective-permute-start.9 = (bf16[96,768]{1,0:T(8,128)(2,1)S(1)}, bf16[96,768]{1,0:T(8,128)(2,1)S(1)}, u32[]{:S(2)}, u32[]{:S(2)}) collective-permute-start(bf16[96,768]{1,0:T(8,128)(2,1)S(1)} %get-tuple-element.45), channel_id=1, source_target_pairs={{0,16},{1,17},{2,18},{3,19},{4,20},{5,21},{6,22},{7,23},{8,9},{9,1... | collective-permute-start | bytes 442376 | tf_op jit(solution)/shard_map/ppermute | solution.py:544
  60.2 6.4 %collective-permute-start.8 = (bf16[96,768]{1,0:T(8,128)(2,1)S(1)}, bf16[96,768]{1,0:T(8,128)(2,1)S(1)}, u32[]{:S(2)}, u32[]{:S(2)}) collective-permute-start(bf16[96,768]{1,0:T(8,128)(2,1)S(1)} %get-tuple-element.46), channel_id=1, source_target_pairs={{0,20},{1,21},{2,22},{3,23},{4,16},{5,17},{6,18},{7,19},{8,11},{9,... | collective-permute-start | bytes 442376 | tf_op jit(solution)/shard_map/ppermute | solution.py:544
